TPU v7x, 512 devices: a whole 4x4x16 slice. The times are simulated.
512 devices in a mesh: tm: 32 (over x, y, core), head: 16 (over z).
Axes of the slice: x: 4, y: 4, z: 16, core: 2. Of those that a mesh axis runs over, the one named last changes fastest.
Arguments:
- queries: bfloat16 [16384, 4096], P('tm', 'head'), may hold values from -40 to 40
- keys: bfloat16 [16384, 4096], P('tm', 'head'), may hold values from -40 to 40
- values: bfloat16 [16384, 4096], P('tm', 'head'), may hold values from -6 to 6
- block_mask: int32 [6, 4, 4], replicated, may hold values from 0 to 1, as said below
- out_weight: bfloat16 [4096, 2560], P('head'), may hold values from -0.09375 to 0.09375
Outputs:
- projected: bfloat16 [16384, 2560], P(('tm', 'head'))
Inputs may be any that keep to these rules, and one draw needn't show every extreme that they name: `block_mask`: entry [c, a, b] is 1 where query block a of a frame may see key block b of a frame in distance class c; class 0 is all ones, every class has its diagonal blocks.
All inputs are finite; a program needn't handle non-finite values.
Results may differ from a plain program's by a relative error of at most 0.025.
Values may be sent and summed in bfloat16 or wider, within the bound.
No kernel may reach another device: no remote copies, remote signals or barrier semaphores. Data moves between devices by JAX's collectives and lax.ppermute only.
A program may use at most 64 MiB of HBM per device.

v0:
```python
import math

import jax
import jax.numpy as jnp
from jax import lax
from jax.sharding import PartitionSpec as P

HD = 128
BLK = 128


def expand_mask(table):
    return jnp.repeat(jnp.repeat(table, BLK, axis=0), BLK, axis=1) > 0


def absorb(running, queries, key_rows, value_rows, allowed):
    factor = 1.0 / math.sqrt(HD)
    maxima, totals, weighted = running
    new_max = []
    new_tot = []
    new_acc = []
    for head_no in range(maxima.shape[0]):
        lo_col = head_no * HD
        query_head = queries[:, lo_col : lo_col + HD]
        key_head = key_rows[:, lo_col : lo_col + HD]
        value_head = value_rows[:, lo_col : lo_col + HD]
        scores = (
            lax.dot_general(
                query_head, key_head, (((1,), (1,)), ((), ())), preferred_element_type=jnp.float32
            )
            * factor
        )
        scores = jnp.where(allowed, scores, jnp.float32(-1e30))
        old_max = maxima[head_no]
        peak = jnp.maximum(old_max, jnp.max(scores, axis=1))
        weights = jnp.where(allowed, jnp.exp(scores - peak[:, None]), jnp.float32(0.0))
        shrink = jnp.exp(old_max - peak)
        new_max.append(peak)
        new_tot.append(totals[head_no] * shrink + jnp.sum(weights, axis=1))
        product = jnp.dot(
            weights.astype(jnp.bfloat16), value_head, preferred_element_type=jnp.float32
        )
        new_acc.append(weighted[head_no] * shrink[:, None] + product)
    return (jnp.stack(new_max), jnp.stack(new_tot), jnp.stack(new_acc))


def shards(queries, keys, values, block_mask, out_weight):
    frame_tok = queries.shape[0]
    heads_here = queries.shape[1] // HD
    chain_len = lax.axis_size("tm")
    position = lax.axis_index("tm")
    levels = chain_len.bit_length() - 1
    tables = [expand_mask(block_mask[level]) for level in range(levels + 1)]
    running = (
        jnp.full((heads_here, frame_tok), -1e30, jnp.float32),
        jnp.zeros((heads_here, frame_tok), jnp.float32),
        jnp.zeros((heads_here, frame_tok, HD), jnp.float32),
    )
    running = absorb(running, queries, keys, values, tables[0])
    key_piece = lax.all_gather(keys, "tm", axis=0, tiled=True)
    value_piece = lax.all_gather(values, "tm", axis=0, tiled=True)
    frame_count = key_piece.shape[0] // frame_tok

    def visit_frame(frame_slot, inner):
        distance = jnp.abs(frame_slot - position)
        allowed = jnp.zeros((frame_tok, frame_tok), jnp.bool_)
        present = jnp.zeros((), jnp.bool_)
        for level in range(1, levels + 1):
            matched = distance == 2 ** (level - 1)
            allowed = allowed | tables[level] & matched
            present = present | matched
        key_rows = lax.dynamic_slice_in_dim(key_piece, frame_slot * frame_tok, frame_tok, 0)
        value_rows = lax.dynamic_slice_in_dim(value_piece, frame_slot * frame_tok, frame_tok, 0)
        return lax.cond(
            present,
            lambda held: absorb(held, queries, key_rows, value_rows, allowed),
            lambda held: held,
            inner,
        )

    running = lax.fori_loop(0, frame_count, visit_frame, running)
    maxima, totals, weighted = running
    attended = jnp.concatenate(
        [weighted[head_no] / totals[head_no][:, None] for head_no in range(heads_here)], axis=1
    ).astype(jnp.bfloat16)
    return lax.psum_scatter(
        jnp.dot(attended, out_weight, preferred_element_type=jnp.float32).astype(jnp.bfloat16),
        "head",
        scatter_dimension=0,
        tiled=True,
    )


def solution(mesh):
    return jax.shard_map(
        shards,
        mesh=mesh,
        in_specs=(P("tm", "head"), P("tm", "head"), P("tm", "head"), P(), P("head", None)),
        out_specs=P(("tm", "head"), None),
        check_vma=False,
    )
```

profile of v0, /device:TPU:2, one launch (start us, length us, event | category | flops | bytes accessed | tf_op | source)
XLA Modules:
  0.0 309.3 jit_solution(8901194601746905050)
XLA Ops:
  6.5 0.7 all-gather.3.cloned.1.call-update
  7.3 0.7 all-gather.5.cloned.1.call-update
  8.1 1.0 slice_compare_fusion
  9.3 1.3 fusion.58
  10.6 2.2 fusion.59
  13.5 1.6 fusion.39
  15.2 1.2 fusion.36
  16.5 1.2 fusion.37
  18.1 65.1 %all-gather.3.cloned.1.call-done = bf16[16384,256]{1,0:T(8,128)(2,1)} async-done(((bf16[512,256]{1,0:T(8,128)(2,1)}), bf16[16384,256]{1,0:T(8,128)(2,1)}) %all-gather.3.cloned.1.call-update) | async-done | bytes 8388624 | tf_op jit(solution)/shard_map/all_gather | solution.py:60
  83.2 71.1 %all-gather.5.cloned.1.call-done = bf16[16384,256]{1,0:T(8,128)(2,1)} async-done(((bf16[512,256]{1,0:T(8,128)(2,1)}), bf16[16384,256]{1,0:T(8,128)(2,1)}) %all-gather.5.cloned.1.call-update) | async-done | bytes 8388624 | tf_op jit(solution)/shard_map/all_gather | solution.py:61
  154.3 71.7 %while.18 = (s32[]{:T(128)}, f32[2,512]{1,0:T(2,128)S(1)}, f32[2,512]{1,0:T(2,128)S(1)}, f32[2,512,128]{2,1,0:T(8,128)S(1)}, s32[]{:T(128)}, /*index=5*/bf16[163...) while((s32[]{:T(128)}, f32[2,512]{1,0:T(2,128)S(1)}, ...), condition=%wide.region_11.12_spmd.clone, body=%wide.region_4.11_spmd.clone.sunk | while | flops 275912704 | bytes 13466134 | solution.py:81
  154.7 6.3 %conditional.3 = ((f32[2,512]{1,0:T(2,128)S(1)}, f32[2,512]{1,0:T(2,128)S(1)}, f32[2,512,128]{2,1,0:T(8,128)S(1)})) conditional(s32[]{:T(128)} %convert_element_type.43, (f32[2,512]{1,0:T(2,128)S(1)}, f32[2,512]{1,0:T(2,128)S(1)}, f32[2,512,128]{2,1,0:T(8,128)S(1)}) %tuple.85, (f32[2,512]{1,0:T(2,128)S(1)}, pred[]{:T(512)}, ...), branch_computations={%region_5.5_spmd, %region_6.10_spmd} | conditional | flops 275912704 | bytes 12144759 | solution.py:74
  154.7 0.6 and_or_fusion
  155.2 1.2 fusion.55
  156.5 1.2 fusion.56
  158.3 1.3 fusion.14
  159.6 1.3 fusion.15
  162.8 6.3 %conditional.3 = ((f32[2,512]{1,0:T(2,128)S(1)}, f32[2,512]{1,0:T(2,128)S(1)}, f32[2,512,128]{2,1,0:T(8,128)S(1)})) conditional(s32[]{:T(128)} %convert_element_type.43, (f32[2,512]{1,0:T(2,128)S(1)}, f32[2,512]{1,0:T(2,128)S(1)}, f32[2,512,128]{2,1,0:T(8,128)S(1)}) %tuple.85, (f32[2,512]{1,0:T(2,128)S(1)}, pred[]{:T(512)}, ...), branch_computations={%region_5.5_spmd, %region_6.10_spmd} | conditional | flops 275912704 | bytes 12144759 | solution.py:74
  162.8 0.6 and_or_fusion
  163.4 1.2 fusion.55
  164.7 1.2 fusion.56
  166.4 1.3 fusion.14
  167.8 1.3 fusion.15
  170.1 6.3 %conditional.3 = ((f32[2,512]{1,0:T(2,128)S(1)}, f32[2,512]{1,0:T(2,128)S(1)}, f32[2,512,128]{2,1,0:T(8,128)S(1)})) conditional(s32[]{:T(128)} %convert_element_type.43, (f32[2,512]{1,0:T(2,128)S(1)}, f32[2,512]{1,0:T(2,128)S(1)}, f32[2,512,128]{2,1,0:T(8,128)S(1)}) %tuple.85, (f32[2,512]{1,0:T(2,128)S(1)}, pred[]{:T(512)}, ...), branch_computations={%region_5.5_spmd, %region_6.10_spmd} | conditional | flops 275912704 | bytes 12144759 | solution.py:74
  170.1 0.6 and_or_fusion
  170.6 1.2 fusion.55
  171.9 1.3 fusion.56
  173.7 1.3 fusion.14
  175.0 1.3 fusion.15
  176.8 6.3 %conditional.3 = ((f32[2,512]{1,0:T(2,128)S(1)}, f32[2,512]{1,0:T(2,128)S(1)}, f32[2,512,128]{2,1,0:T(8,128)S(1)})) conditional(s32[]{:T(128)} %convert_element_type.43, (f32[2,512]{1,0:T(2,128)S(1)}, f32[2,512]{1,0:T(2,128)S(1)}, f32[2,512,128]{2,1,0:T(8,128)S(1)}) %tuple.85, (f32[2,512]{1,0:T(2,128)S(1)}, pred[]{:T(512)}, ...), branch_computations={%region_5.5_spmd, %region_6.10_spmd} | conditional | flops 275912704 | bytes 12144759 | solution.py:74
  176.9 0.6 and_or_fusion
  177.4 1.2 fusion.55
  178.7 1.2 fusion.56
  180.4 1.3 fusion.14
  181.8 1.3 fusion.15
  184.1 6.3 %conditional.3 = ((f32[2,512]{1,0:T(2,128)S(1)}, f32[2,512]{1,0:T(2,128)S(1)}, f32[2,512,128]{2,1,0:T(8,128)S(1)})) conditional(s32[]{:T(128)} %convert_element_type.43, (f32[2,512]{1,0:T(2,128)S(1)}, f32[2,512]{1,0:T(2,128)S(1)}, f32[2,512,128]{2,1,0:T(8,128)S(1)}) %tuple.85, (f32[2,512]{1,0:T(2,128)S(1)}, pred[]{:T(512)}, ...), branch_computations={%region_5.5_spmd, %region_6.10_spmd} | conditional | flops 275912704 | bytes 12144759 | solution.py:74
  184.1 0.6 and_or_fusion
  184.7 1.2 fusion.55
  185.9 1.2 fusion.56
  187.7 1.3 fusion.14
  189.0 1.3 fusion.15
  190.8 6.3 %conditional.3 = ((f32[2,512]{1,0:T(2,128)S(1)}, f32[2,512]{1,0:T(2,128)S(1)}, f32[2,512,128]{2,1,0:T(8,128)S(1)})) conditional(s32[]{:T(128)} %convert_element_type.43, (f32[2,512]{1,0:T(2,128)S(1)}, f32[2,512]{1,0:T(2,128)S(1)}, f32[2,512,128]{2,1,0:T(8,128)S(1)}) %tuple.85, (f32[2,512]{1,0:T(2,128)S(1)}, pred[]{:T(512)}, ...), branch_computations={%region_5.5_spmd, %region_6.10_spmd} | conditional | flops 275912704 | bytes 12144759 | solution.py:74
  190.9 0.6 and_or_fusion
  191.4 1.2 fusion.55
  192.7 1.2 fusion.56
  194.4 1.3 fusion.14
  195.8 1.3 fusion.15
  198.1 6.3 %conditional.3 = ((f32[2,512]{1,0:T(2,128)S(1)}, f32[2,512]{1,0:T(2,128)S(1)}, f32[2,512,128]{2,1,0:T(8,128)S(1)})) conditional(s32[]{:T(128)} %convert_element_type.43, (f32[2,512]{1,0:T(2,128)S(1)}, f32[2,512]{1,0:T(2,128)S(1)}, f32[2,512,128]{2,1,0:T(8,128)S(1)}) %tuple.85, (f32[2,512]{1,0:T(2,128)S(1)}, pred[]{:T(512)}, ...), branch_computations={%region_5.5_spmd, %region_6.10_spmd} | conditional | flops 275912704 | bytes 12144759 | solution.py:74
  198.7 1.2 fusion.55
  199.9 1.2 fusion.56
  201.7 1.3 fusion.14
  203.0 1.3 fusion.15
  206.2 6.3 %conditional.3 = ((f32[2,512]{1,0:T(2,128)S(1)}, f32[2,512]{1,0:T(2,128)S(1)}, f32[2,512,128]{2,1,0:T(8,128)S(1)})) conditional(s32[]{:T(128)} %convert_element_type.43, (f32[2,512]{1,0:T(2,128)S(1)}, f32[2,512]{1,0:T(2,128)S(1)}, f32[2,512,128]{2,1,0:T(8,128)S(1)}) %tuple.85, (f32[2,512]{1,0:T(2,128)S(1)}, pred[]{:T(512)}, ...), branch_computations={%region_5.5_spmd, %region_6.10_spmd} | conditional | flops 275912704 | bytes 12144759 | solution.py:74
  206.8 1.2 fusion.55
  208.1 1.2 fusion.56
  209.9 1.3 fusion.14
  211.2 1.3 fusion.15
  216.3 6.3 %conditional.3 = ((f32[2,512]{1,0:T(2,128)S(1)}, f32[2,512]{1,0:T(2,128)S(1)}, f32[2,512,128]{2,1,0:T(8,128)S(1)})) conditional(s32[]{:T(128)} %convert_element_type.43, (f32[2,512]{1,0:T(2,128)S(1)}, f32[2,512]{1,0:T(2,128)S(1)}, f32[2,512,128]{2,1,0:T(8,128)S(1)}) %tuple.85, (f32[2,512]{1,0:T(2,128)S(1)}, pred[]{:T(512)}, ...), branch_computations={%region_5.5_spmd, %region_6.10_spmd} | conditional | flops 275912704 | bytes 12144759 | solution.py:74
  216.9 1.2 fusion.55
  218.1 1.2 fusion.56
  219.9 1.3 fusion.14
  221.2 1.3 fusion.15
  226.2 2.4 convolution_convert_fusion
  228.5 74.2 %reduce-scatter.2.cloned.1.call-done = bf16[32,2560]{1,0:T(8,128)(2,1)} async-done(((bf16[512,2560]{1,0:T(8,128)(2,1)}), bf16[32,2560]{1,0:T(8,128)(2,1)}) %reduce-scatter.2.cloned.1.call-update) | async-done | bytes 163856 | tf_op jit(solution)/shard_map/reduce_scatter | solution.py:86
  (281 shorter events, 20.0 us)
Async XLA Ops:
  6.5 219.6 %copy-start = (bf16[256,2560]{1,0:T(8,128)(2,1)S(1)}, bf16[256,2560]{1,0:T(8,128)(2,1)}, u32[]{:S(2)}) copy-start(bf16[256,2560]{1,0:T(8,128)(2,1)} %param.13) | copy-start | bytes 3932164
  6.5 147.7 %copy-start.1 = (bf16[512,256]{1,0:T(8,128)(2,1)S(1)}, bf16[512,256]{1,0:T(8,128)(2,1)}, u32[]{:S(2)}) copy-start(bf16[512,256]{1,0:T(8,128)(2,1)} %param.9) | copy-start | bytes 786436
  6.5 76.6 %all-gather.3.cloned.1.call-start = ((), (), s32[]{:S(2)}) async-start(), calls=%async_computation.1 | async-start | bytes 8650752 | tf_op jit(solution)/shard_map/all_gather | solution.py:60
  7.3 147.0 %all-gather.5.cloned.1.call-start = ((), (), s32[]{:S(2)}) async-start(), calls=%async_computation.2 | async-start | bytes 8650752 | tf_op jit(solution)/shard_map/all_gather | solution.py:61
  8.0 294.8 %reduce-scatter.2.cloned.1.call-start = ((), (), s32[]{:S(2)}) async-start(), calls=%async_computation.3 | async-start | bytes 2785280 | tf_op jit(solution)/shard_map/reduce_scatter | solution.py:86
Sparse Core Ops, SparseCore 0:
  10.5 72.6 all-gather.2
  86.3 67.8 all-gather.4
  228.7 74.0 reduce-scatter.1
where the time goes:
time: 310 us; the launch traced here: 309 us
  waiting for transfers between devices  212 us (68%)
  matrix products  54.7 us (18%)
  between operations  13.2 us (4%)
  local copies, waits for them, and re-layouts  12.9 us (4%)
  other arithmetic  12.5 us (4%)
  loops' own time  4.06 us (1%)
    reduce_scatter x1, waiting for transfers between devices, shards(): lax.psum_scatter(jnp.dot(attended, out_weight, preferred_element_type=jnp...  74.2 us
    all_gather x1, waiting for transfers between devices, shards(): value_piece = lax.all_gather(values, 'tm', axis=0, tiled=True)  71.1 us
    all_gather x1, waiting for transfers between devices, shards(): key_piece = lax.all_gather(keys, 'tm', axis=0, tiled=True)  65.1 us
    dot_general x20, matrix products, absorb(): jnp.dot(weights.astype(jnp.bfloat16), value_head, preferred_element_type=...  26.4 us
    dot_general x20, matrix products, absorb(): lax.dot_general(query_head, key_head, (((1,), (1,)), ((), ())), preferred...  25.9 us
    broadcast_in_dim x160, local copies, waits for them, and re-layouts, expand_mask(): return jnp.repeat(jnp.repeat(table, BLK, axis=0), BLK, axis=1) > 0  11.6 us
  transfers between devices with their start and end apart: 3, of which 3 were waited for; matrix products, arithmetic and copies ran while one was open for 3% of the time, Pallas kernels for 0%

commit v1 on v0

v1 whole, which is shorter than its diff:
```python
import functools
import math

import jax
import jax.numpy as jnp
from jax import lax
from jax.experimental import pallas as pl
from jax.experimental.pallas import tpu as pltpu
from jax.sharding import PartitionSpec as P

HD = 128
BLK = 128
FT = 512
NB = 4
ROWS = 32
DOUT = 2560
HIDDEN = -1e30
SCALE = math.log2(math.e) / math.sqrt(HD)
VMEM = 40 * 1024 * 1024


def tile_scores(q, kv_ref, frame, bias_ref, base):
    scores = lax.dot_general(
        q, kv_ref[2 * frame], (((1,), (1,)), ((), ())), preferred_element_type=jnp.float32
    )
    return [scores[:, b * BLK : (b + 1) * BLK] + bias_ref[base + b] for b in range(NB)]


def attend_kernel(sources, n_kv, first, last, *refs):
    bias_ref, q_ref = refs[:2]
    kv_refs = refs[2 : 2 + n_kv]
    rest = refs[2 + n_kv :]
    if first:
        outs = rest
    else:
        state_in, outs = rest[:3], rest[3:]

    def tile(step, carry):
        frame = step // NB
        block = step % NB
        rows = pl.ds(pl.multiple_of(block * BLK, BLK), BLK)
        q = q_ref[frame, rows, :]
        pieces = []
        for kv_no, cross, bias_no in sources:
            key_frame = 1 - frame if cross else frame
            base = ((bias_no * 2 + frame) * NB + block) * NB
            pieces.append(tile_scores(q, kv_refs[kv_no], key_frame, bias_ref, base))
        top = functools.reduce(jnp.maximum, [s for piece in pieces for s in piece])
        peak = jnp.max(top, axis=1, keepdims=True)
        if not first:
            old = state_in[0][frame, rows, :]
            peak = jnp.maximum(old, peak)
            shrink = jnp.exp2((old - peak) * SCALE)
            total = state_in[1][frame, rows, :] * shrink
            acc = state_in[2][frame, rows, :] * shrink
        else:
            peak = jnp.broadcast_to(peak, (BLK, BLK))
            total = jnp.zeros((BLK, BLK), jnp.float32)
            acc = jnp.zeros((BLK, HD), jnp.float32)
        for (kv_no, cross, _), piece in zip(sources, pieces):
            key_frame = 1 - frame if cross else frame
            weights = [jnp.exp2((s - peak) * SCALE) for s in piece]
            total = total + sum(weights)
            packed = jnp.concatenate([w.astype(jnp.bfloat16) for w in weights], axis=1)
            acc = acc + jnp.dot(
                packed, kv_refs[kv_no][2 * key_frame + 1], preferred_element_type=jnp.float32
            )
        if last:
            denom = jnp.sum(total, axis=1, keepdims=True)
            attended = (acc / denom).astype(jnp.bfloat16)
            for i in range(BLK // ROWS):
                outs[0][block * (BLK // ROWS) + i, frame] = attended[i * ROWS : (i + 1) * ROWS]
        else:
            outs[0][frame, rows, :] = peak
            outs[1][frame, rows, :] = total
            outs[2][frame, rows, :] = acc
        return carry

    lax.fori_loop(0, 2 * NB, tile, 0)


def attend(bias, q, kvs, sources, state, last):
    first = state is None
    held = jax.ShapeDtypeStruct((2, FT, HD), jnp.float32)
    if last:
        out_shape = (jax.ShapeDtypeStruct((FT // ROWS, 2, ROWS, HD), jnp.bfloat16),)
    else:
        out_shape = (held,) * 3
    vmem = pl.BlockSpec(memory_space=pltpu.VMEM)
    smem = pl.BlockSpec(memory_space=pltpu.SMEM)
    states = () if first else tuple(state)
    pairs = len(sources) * 2
    out = pl.pallas_call(
        functools.partial(attend_kernel, sources, len(kvs), first, last),
        out_shape=out_shape,
        in_specs=[smem] + [vmem] * (1 + len(kvs) + len(states)),
        out_specs=(vmem,) * len(out_shape),
        compiler_params=pltpu.CompilerParams(vmem_limit_bytes=VMEM),
        cost_estimate=pl.CostEstimate(
            flops=pairs * 4 * FT * FT * HD,
            bytes_accessed=len(kvs) * 4 * FT * HD * 2,
            transcendentals=pairs * FT * FT,
        ),
    )(bias, q, *kvs, *states)
    return out[0] if last else out


def project_kernel(place_ref, own_ref, other_ref, w_ref, out_ref, lhs_ref):
    @pl.when(pl.program_id(0) == 0)
    def _():
        for z in range(own_ref.shape[0]):
            cols = slice(z * HD, (z + 1) * HD)
            lhs_ref[: 2 * ROWS, cols] = own_ref[z]
            lhs_ref[2 * ROWS :, cols] = other_ref[z]

    part = jnp.dot(lhs_ref[...], w_ref[...], preferred_element_type=jnp.float32)
    part = part.astype(jnp.bfloat16)
    for k in range(4):
        out_ref[place_ref[k]] = part[k * ROWS : (k + 1) * ROWS]


def project(place, own, other, weight):
    groups = own.shape[0]
    depth, width = weight.shape
    step = 256
    return pl.pallas_call(
        project_kernel,
        grid=(width // step,),
        out_shape=jax.ShapeDtypeStruct((4, ROWS, width), jnp.bfloat16),
        in_specs=[
            pl.BlockSpec(memory_space=pltpu.SMEM),
            pl.BlockSpec((groups, 2 * ROWS, HD), lambda n: (0, 0, 0)),
            pl.BlockSpec((groups, 2 * ROWS, HD), lambda n: (0, 0, 0)),
            pl.BlockSpec((depth, step), lambda n: (0, n)),
        ],
        out_specs=pl.BlockSpec((4, ROWS, step), lambda n: (0, 0, n)),
        scratch_shapes=[pltpu.VMEM((4 * ROWS, depth), jnp.bfloat16)],
        compiler_params=pltpu.CompilerParams(vmem_limit_bytes=VMEM),
        cost_estimate=pl.CostEstimate(
            flops=8 * ROWS * depth * width, bytes_accessed=depth * width * 2, transcendentals=0
        ),
    )(place, own, other, weight)


def add_kernel(in_ref, out_ref):
    half = in_ref.shape[2]
    for p in range(2):
        both = in_ref[2 * p].astype(jnp.float32) + in_ref[2 * p + 1].astype(jnp.float32)
        out_ref[:, p * half : (p + 1) * half] = both.astype(jnp.bfloat16)


def add_cores(parts):
    return pl.pallas_call(
        add_kernel,
        out_shape=jax.ShapeDtypeStruct((ROWS, 2 * parts.shape[2]), jnp.bfloat16),
        in_specs=[pl.BlockSpec(memory_space=pltpu.VMEM)],
        out_specs=pl.BlockSpec(memory_space=pltpu.VMEM),
        compiler_params=pltpu.CompilerParams(vmem_limit_bytes=VMEM),
    )(parts)


def shards(queries, keys, values, block_mask, out_weight):
    me = lax.axis_index("tm")
    core = me % 2
    y = (me // 2) % 4
    x = me // 8
    side = y % 2

    def chips(go):
        pairs = []
        for i in range(32):
            to = go(i // 8, (i // 2) % 4)
            if to is not None:
                pairs.append((i, to[0] * 8 + to[1] * 2 + i % 2))
        return pairs

    def send(array, pairs):
        return lax.ppermute(array, "tm", pairs)

    half = DOUT // 2
    weight = lax.dynamic_slice(out_weight, (core * HD, side * half), (HD, half))
    weight = lax.all_gather(weight, "head", axis=0, tiled=True)

    def split(array):
        low, high = array[:, :HD], array[:, HD:]
        return jnp.where(core == 0, low, high), jnp.where(core == 0, high, low)

    (q_own, q_give), (k_own, k_give), (v_own, v_give) = map(split, (queries, keys, values))
    swap = [(i, i ^ 1) for i in range(32)]
    kv_got = send(jnp.stack([k_give, v_give]), swap)
    q_got = send(q_give, swap)
    local = jnp.concatenate([jnp.stack([k_own, v_own]), kv_got], axis=0)
    q = jnp.stack([q_own, q_got])

    above = send(local, chips(lambda x, y: (x + 1, y) if x < 3 else None))
    below = send(local, chips(lambda x, y: (x - 1, y) if x > 0 else None))
    across = send(local, chips(lambda x, y: (x, y ^ 2)))
    beside = send(local, chips(lambda x, y: (x, y ^ 1)))
    far = send(local, chips(lambda x, y: (x ^ 2, y)))
    turned = jnp.where((y == 1) | (y == 2), local, jnp.where(y == 3, above, below))
    other = send(turned, chips(lambda x, y: (x, 3 - y)))
    across_row = send(jnp.where(y >= 2, above, below), chips(lambda x, y: (x, y ^ 2)))

    always = jnp.array([True, True])
    parity = jnp.stack([core, 1 - core])
    even = y % 2 == 0
    has_above, has_below = x > 0, x < 3
    row_end = jnp.where(y == 0, has_above, jnp.where(y == 3, has_below, True))
    row_cross = jnp.where(y < 2, has_above, has_below)
    upper = parity == 1
    levels = [0, 1, 2, 1, 2, 1, 3, 3, 4, 4, 5]
    valid = [
        always,
        always,
        always,
        jnp.where(even, upper, ~upper),
        always & row_end,
        jnp.where(even, ~upper, upper) & row_end,
        always,
        always & row_cross,
        always & has_above,
        always & has_below,
        always,
    ]
    seen = (block_mask[jnp.array(levels)] > 0)[:, None] & jnp.stack(valid)[:, :, None, None]
    bias = jnp.where(seen, jnp.float32(0.0), jnp.float32(HIDDEN)).reshape(-1)

    state = attend(bias, q, [local], [(0, False, 0), (0, True, 1)], None, False)
    state = attend(
        bias,
        q,
        [beside, across, above, below, far],
        [
            (0, False, 2),
            (0, True, 3),
            (1, False, 6),
            (2, False, 8),
            (3, False, 9),
            (4, False, 10),
        ],
        state,
        False,
    )
    attended = attend(
        bias,
        q,
        [other, across_row],
        [(0, False, 4), (0, True, 5), (1, False, 7)],
        state,
        True,
    )

    rows = lax.all_to_all(
        attended.reshape(FT // ROWS, 2 * ROWS, HD), "head", 0, 0, tiled=True
    )
    partner = send(rows, [(i, i ^ 2) for i in range(32)])
    here = me % 4
    place = jnp.stack([here, here ^ 1, here ^ 2, here ^ 3]).astype(jnp.int32)
    parts = project(place, rows, partner, weight)
    quads = [[4 * j + k for k in range(4)] for j in range(8)]
    parts = lax.all_to_all(parts, "tm", 0, 0, tiled=True, axis_index_groups=quads)
    return add_cores(parts)


def solution(mesh):
    return jax.shard_map(
        shards,
        mesh=mesh,
        in_specs=(P("tm", "head"), P("tm", "head"), P("tm", "head"), P(), P("head", None)),
        out_specs=P(("tm", "head"), None),
        check_vma=False,
    )
```

time: 310 us -> 147 us (0.47)
  the two profiles are of different devices: /device:TPU:2 before, /device:TPU:1 now
where the time goes in v1:
time: 147 us; the launch traced here: 145 us
  blocking collectives  43.4 us (30%)
  starting transfers between devices  31.3 us (21%)
  waiting for transfers between devices  25.1 us (17%)
  Pallas kernels  21.9 us (15%)
  between operations  13.7 us (9%)
  local copies, waits for them, and re-layouts  5.95 us (4%)
  other arithmetic  4.2 us (3%)
    ppermute x10, starting transfers between devices, send(): return lax.ppermute(array, 'tm', pairs)  31.3 us
    all_to_all x1, blocking collectives, shards(): lax.all_to_all(attended.reshape(FT // ROWS, 2 * ROWS, HD), 'head', 0, 0,...  28.7 us
    ppermute x10, waiting for transfers between devices, send(): return lax.ppermute(array, 'tm', pairs)  25.1 us
    pallas_call x3, Pallas kernels, attend(): pl.pallas_call(functools.partial(attend_kernel, sources, len(kvs), first,...  18.5 us
    all_to_all x1, blocking collectives, shards(): lax.all_to_all(parts, 'tm', 0, 0, tiled=True, axis_index_groups=quads)  14.7 us
    unnamed x3, local copies, waits for them, and re-layouts  3.29 us
  transfers between devices with their start and end apart: 11, of which 4 were waited for; matrix products, arithmetic and copies ran while one was open for 4% of the time, Pallas kernels for 13%

profile of v1, /device:TPU:1, one launch (start us, length us, event | category | flops | bytes accessed | tf_op | source)
XLA Modules:
  0.0 145.5 jit_solution(7691078057215399313)
XLA Ops:
  6.5 0.0 all-gather.2.cloned.1.call-start
  6.5 1.7 %dynamic_slice.3 = bf16[128,1280]{1,0:T(8,128)(2,1)} dynamic-slice(bf16[256,2560]{1,0:T(8,128)(2,1)} %param.11, s32[]{:T(128)S(6)} %select_n.158, s32[]{:T(128)S(6)} %select_n.159), dynamic_slice_sizes={128,1280} | dynamic-slice | bytes 655364 | tf_op jit(solution)/shard_map/dynamic_slice | solution.py:181
  8.2 0.0 all-gather.2.cloned.1.call-update
  8.3 1.1 select_bitcast_fusion.2
  9.5 8.8 %collective-permute-start.1 = (bf16[2,512,128]{2,1,0:T(8,128)(2,1)S(1)}, bf16[2,512,128]{2,1,0:T(8,128)(2,1)S(1)}, u32[]{:S(2)}, u32[]{:S(2)}) collective-permute-start(bf16[2,512,128]{2,1,0:T(8,128)(2,1)S(1)} %pad_maximum_fusion.2), channel_id=1, source_target_pairs={{0,16},{16,0},{32,48},{48,32},{64,80},{80,64},{96,112},{112,96},{1... | collective-permute-start | bytes 786440 | tf_op jit(solution)/shard_map/ppermute | solution.py:178
  18.2 1.1 collective-permute-done.1
  19.4 0.1 pad_maximum_fusion.refs_2_
  19.4 1.3 collective-permute-start.2
  20.8 1.3 collective-permute-start.3
  22.1 1.0 select_bitcast_fusion.4
  23.1 2.3 %collective-permute-start = (bf16[512,128]{1,0:T(8,128)(2,1)S(1)}, bf16[512,128]{1,0:T(8,128)(2,1)S(1)}, u32[]{:S(2)}, u32[]{:S(2)}) collective-permute-start(bf16[512,128]{1,0:T(8,128)(2,1)S(1)} %get-tuple-element.24), channel_id=1, source_target_pairs={{0,16},{16,0},{32,48},{48,32},{64,80},{80,64},{96,112},{112,96},{1... | collective-permute-start | bytes 393224 | tf_op jit(solution)/shard_map/ppermute | solution.py:178
  25.5 0.1 stack.85
  25.6 0.1 copy.11
  25.7 0.8 copy.10
  26.5 0.7 pad_clamp_fusion
  27.2 0.6 gather_fusion
  27.8 1.9 %collective-permute-start.6 = (bf16[4,512,128]{2,1,0:T(8,128)(2,1)S(1)}, bf16[4,512,128]{2,1,0:T(8,128)(2,1)S(1)}, u32[]{:S(2)}, u32[]{:S(2)}) collective-permute-start(bf16[4,512,128]{2,1,0:T(8,128)(2,1)S(1)} %pad_maximum_fusion.refs_2_), channel_id=1, source_target_pairs={{0,32},{16,48},{32,0},{48,16},{64,96},{80,112},{96,64},{112,80},{1... | collective-permute-start | bytes 1572872 | tf_op jit(solution)/shard_map/ppermute | solution.py:178
  29.7 2.5 %collective-permute-start.7 = (bf16[4,512,128]{2,1,0:T(8,128)(2,1)S(1)}, bf16[4,512,128]{2,1,0:T(8,128)(2,1)}, u32[]{:S(2)}, u32[]{:S(2)}) collective-permute-start(bf16[4,512,128]{2,1,0:T(8,128)(2,1)S(1)} %pad_maximum_fusion.refs_2_), channel_id=1, source_target_pairs={{0,64},{16,80},{32,96},{48,112},{64,0},{80,16},{96,32},{112,48},{1... | collective-permute-start | bytes 1572872 | tf_op jit(solution)/shard_map/ppermute | solution.py:178
  32.3 0.0 collective-permute-done.2.refs_4_
  32.3 5.8 %collective-permute-start.8 = (bf16[4,512,128]{2,1,0:T(8,128)(2,1)S(1)}, bf16[4,512,128]{2,1,0:T(8,128)(2,1)}, u32[]{:S(2)}, u32[]{:S(2)}) collective-permute-start(bf16[4,512,128]{2,1,0:T(8,128)(2,1)S(1)} %pad_maximum_fusion.refs_2_), channel_id=1, source_target_pairs={{0,256},{16,272},{32,288},{48,304},{64,320},{80,336},{96,352},{112... | collective-permute-start | bytes 1572872 | tf_op jit(solution)/shard_map/ppermute | solution.py:178
  38.1 0.0 collective-permute-done.3.refs_5_
  38.1 1.1 broadcast_select_fusion
  39.2 1.9 %collective-permute-start.4 = (bf16[4,512,128]{2,1,0:T(8,128)(2,1)}, bf16[4,512,128]{2,1,0:T(8,128)(2,1)S(1)}, u32[]{:S(2)}, u32[]{:S(2)}) collective-permute-start(bf16[4,512,128]{2,1,0:T(8,128)(2,1)} %get-tuple-element.18), channel_id=1, source_target_pairs={{0,96},{16,112},{32,64},{48,80},{64,32},{80,48},{96,0},{112,16},{1... | collective-permute-start | bytes 1572872 | tf_op jit(solution)/shard_map/ppermute | solution.py:178
  41.1 0.0 collective-permute-done
  41.1 3.5 %collective-permute-start.5 = (bf16[4,512,128]{2,1,0:T(8,128)(2,1)}, bf16[4,512,128]{2,1,0:T(8,128)(2,1)S(1)}, u32[]{:S(2)}, u32[]{:S(2)}) collective-permute-start(bf16[4,512,128]{2,1,0:T(8,128)(2,1)} %get-tuple-element.17), channel_id=1, source_target_pairs={{0,64},{16,80},{32,96},{48,112},{64,0},{80,16},{96,32},{112,48},{1... | collective-permute-start | bytes 1572872 | tf_op jit(solution)/shard_map/ppermute | solution.py:178
  44.7 0.1 and_select_fusion
  44.8 0.1 select_n.144.refs_0_
  44.9 4.6 %shard_map.73 = (f32[2,512,128]{2,1,0:T(8,128)S(1)}, f32[2,512,128]{2,1,0:T(8,128)S(1)}, f32[2,512,128]{2,1,0:T(8,128)S(1)}) custom-call(f32[352]{0:T(512)S(1)} %select_n.144.refs_0_, bf16[2,512,128]{2,1,0:T(8,128)(2,1)S(1)} %pad_maximum_fusion.1.refs_1_, bf16[4,512,128]{2,1,0:T(8,128)(2,1)S(1)} %pad_maximum_fusion.refs_2_), custom_call_target="tpu_custom_call" | custom-call | flops 536870912 | bytes 524288 | tf_op jit(solution)/shard_map/pallas_call | solution.py:93
  49.5 0.0 collective-permute-done.6.refs_2_
  49.5 4.3 %collective-permute-done.7.refs_3_ = bf16[4,512,128]{2,1,0:T(8,128)(2,1)} collective-permute-done((bf16[4,512,128]{2,1,0:T(8,128)(2,1)S(1)}, bf16[4,512,128]{2,1,0:T(8,128)(2,1)}, u32[]{:S(2)}, u32[]{:S(2)}) %collective-permute-start.7) | collective-permute-done | bytes 524320 | tf_op jit(solution)/shard_map/ppermute | solution.py:178
  53.8 0.0 collective-permute-done.8.refs_6_
  53.8 8.2 %shard_map.74 = (f32[2,512,128]{2,1,0:T(8,128)S(1)}, f32[2,512,128]{2,1,0:T(8,128)S(1)}, f32[2,512,128]{2,1,0:T(8,128)S(1)}) custom-call(f32[352]{0:T(512)S(1)} %select_n.144.refs_0_, bf16[2,512,128]{2,1,0:T(8,128)(2,1)S(1)} %pad_maximum_fusion.1.refs_1_, bf16[4,512,128]{2,1,0:T(8,128)(2,1)S(1)} %collective-permute-done.6.refs_2_, ...), custom_call_target="tpu_custom_call" | custom-call | flops 1610612736 | bytes 2621440 | tf_op jit(solution)/shard_map/pallas_call | solution.py:93
  62.0 14.6 %collective-permute-done.4.refs_2_ = bf16[4,512,128]{2,1,0:T(8,128)(2,1)S(1)} collective-permute-done((bf16[4,512,128]{2,1,0:T(8,128)(2,1)}, bf16[4,512,128]{2,1,0:T(8,128)(2,1)S(1)}, u32[]{:S(2)}, u32[]{:S(2)}) %collective-permute-start.4) | collective-permute-done | bytes 524320 | tf_op jit(solution)/shard_map/ppermute | solution.py:178
  76.5 0.0 collective-permute-done.5.refs_3_
  76.5 5.7 %shard_map.75 = bf16[16,2,32,128]{3,2,1,0:T(8,128)(2,1)S(1)} custom-call(f32[352]{0:T(512)S(1)} %select_n.144.refs_0_, bf16[2,512,128]{2,1,0:T(8,128)(2,1)S(1)} %pad_maximum_fusion.1.refs_1_, bf16[4,512,128]{2,1,0:T(8,128)(2,1)S(1)} %collective-permute-done.4.refs_2_, bf16[4,512,128]{2,1,0:T(8,128)(2,1)S(1)} %collective-permute-done.5.refs_3_, ...), custom_call_target="tpu_custom_call" | custom-call | flops 805306368 | bytes 1048576 | tf_op jit(solution)/shard_map/pallas_call | solution.py:93
  82.3 28.7 %all_to_all.10.own_ref = bf16[16,64,128]{2,1,0:T(8,128)(2,1)S(1)} all-to-all(bf16[16,64,128]{2,1,0:T(8,128)(2,1)S(1)} %bitcast.18), channel_id=1, replica_groups=mesh['tm'=32,'head'=16] {'head'}, dimensions={0} | all-to-all | bytes 524288 | tf_op jit(solution)/shard_map/all_to_all | solution.py:253
  111.0 1.9 %collective-permute-start.9 = (bf16[16,64,128]{2,1,0:T(8,128)(2,1)S(1)}, bf16[16,64,128]{2,1,0:T(8,128)(2,1)S(1)}, u32[]{:S(2)}, u32[]{:S(2)}) collective-permute-start(bf16[16,64,128]{2,1,0:T(8,128)(2,1)S(1)} %all_to_all.10.own_ref), channel_id=1, source_target_pairs={{0,32},{16,48},{32,0},{48,16},{64,96},{80,112},{96,64},{112,80},{1... | collective-permute-start | bytes 786440 | tf_op jit(solution)/shard_map/ppermute | solution.py:178
  112.9 0.1 pad_add_fusion.place_ref
  113.0 5.1 %collective-permute-done.9.other_ref = bf16[16,64,128]{2,1,0:T(8,128)(2,1)S(1)} collective-permute-done((bf16[16,64,128]{2,1,0:T(8,128)(2,1)S(1)}, bf16[16,64,128]{2,1,0:T(8,128)(2,1)S(1)}, u32[]{:S(2)}, u32[]{:S(2)}) %collective-permute-start.9) | collective-permute-done | bytes 262176 | tf_op jit(solution)/shard_map/ppermute | solution.py:178
  118.1 0.0 all-gather.2.cloned.1.call-done.w_ref
  118.1 0.0 copy-start
  118.1 2.5 %copy-done = bf16[2048,1280]{1,0:T(8,128)(2,1)S(1)} copy-done((bf16[2048,1280]{1,0:T(8,128)(2,1)S(1)}, bf16[2048,1280]{1,0:T(8,128)(2,1)}, u32[]{:S(2)}) %copy-start) | copy-done | bytes 5242904
  120.6 2.7 %shard_map.76 = bf16[4,32,1280]{2,1,0:T(8,128)(2,1)S(1)} custom-call(s32[4]{0:T(128)S(1)} %pad_add_fusion.place_ref, bf16[16,64,128]{2,1,0:T(8,128)(2,1)S(1)} %all_to_all.10.own_ref, bf16[16,64,128]{2,1,0:T(8,128)(2,1)S(1)} %collective-permute-done.9.other_ref, bf16[2048,1280]{1,0:T(8,128)(2,1)S(1)} %copy-done), custom_call_target="tpu_custom_call" | custom-call | flops 671088640 | bytes 5242880 | tf_op jit(solution)/shard_map/pallas_call | solution.py:126
  123.2 14.7 %all_to_all.11.in_ref = bf16[4,32,1280]{2,1,0:T(8,128)(2,1)S(1)} all-to-all(bf16[4,32,1280]{2,1,0:T(8,128)(2,1)S(1)} %shard_map.76), channel_id=1, replica_groups={{0,16,32,48},{64,80,96,112},{128,144,160,176},{192,208,224,240},{256,27..., dimensions={0} | all-to-all | bytes 655360 | tf_op jit(solution)/shard_map/all_to_all | solution.py:261
  137.9 0.7 shard_map.77
  (9 shorter events, 0.1 us)
Async XLA Ops:
  6.5 111.5 %all-gather.2.cloned.1.call-start = ((), (), s32[]{:S(2)}) async-start(), calls=%async_computation.2 | async-start | bytes 5570560 | tf_op jit(solution)/shard_map/all_gather | solution.py:182
  9.5 9.9 %collective-permute-start.1 = (bf16[2,512,128]{2,1,0:T(8,128)(2,1)S(1)}, bf16[2,512,128]{2,1,0:T(8,128)(2,1)S(1)}, u32[]{:S(2)}, u32[]{:S(2)}) collective-permute-start(bf16[2,512,128]{2,1,0:T(8,128)(2,1)S(1)} %pad_maximum_fusion.2), channel_id=1, source_target_pairs={{0,16},{16,0},{32,48},{48,32},{64,80},{80,64},{96,112},{112,96},{1... | collective-permute-start | bytes 786440 | tf_op jit(solution)/shard_map/ppermute | solution.py:178
  19.4 12.8 %collective-permute-start.2 = (bf16[4,512,128]{2,1,0:T(8,128)(2,1)S(1)}, bf16[4,512,128]{2,1,0:T(8,128)(2,1)S(1)}, u32[]{:S(2)}, u32[]{:S(2)}) collective-permute-start(bf16[4,512,128]{2,1,0:T(8,128)(2,1)S(1)} %pad_maximum_fusion.refs_2_), channel_id=1, source_target_pairs={{0,128},{16,144},{32,160},{48,176},{64,192},{80,208},{96,224},{112... | collective-permute-start | bytes 1572872 | tf_op jit(solution)/shard_map/ppermute | solution.py:178
  20.8 17.3 %collective-permute-start.3 = (bf16[4,512,128]{2,1,0:T(8,128)(2,1)S(1)}, bf16[4,512,128]{2,1,0:T(8,128)(2,1)S(1)}, u32[]{:S(2)}, u32[]{:S(2)}) collective-permute-start(bf16[4,512,128]{2,1,0:T(8,128)(2,1)S(1)} %pad_maximum_fusion.refs_2_), channel_id=1, source_target_pairs={{128,0},{144,16},{160,32},{176,48},{192,64},{208,80},{224,96},{240... | collective-permute-start | bytes 1572872 | tf_op jit(solution)/shard_map/ppermute | solution.py:178
  23.1 18.0 %collective-permute-start = (bf16[512,128]{1,0:T(8,128)(2,1)S(1)}, bf16[512,128]{1,0:T(8,128)(2,1)S(1)}, u32[]{:S(2)}, u32[]{:S(2)}) collective-permute-start(bf16[512,128]{1,0:T(8,128)(2,1)S(1)} %get-tuple-element.24), channel_id=1, source_target_pairs={{0,16},{16,0},{32,48},{48,32},{64,80},{80,64},{96,112},{112,96},{1... | collective-permute-start | bytes 393224 | tf_op jit(solution)/shard_map/ppermute | solution.py:178
  27.8 21.7 %collective-permute-start.6 = (bf16[4,512,128]{2,1,0:T(8,128)(2,1)S(1)}, bf16[4,512,128]{2,1,0:T(8,128)(2,1)S(1)}, u32[]{:S(2)}, u32[]{:S(2)}) collective-permute-start(bf16[4,512,128]{2,1,0:T(8,128)(2,1)S(1)} %pad_maximum_fusion.refs_2_), channel_id=1, source_target_pairs={{0,32},{16,48},{32,0},{48,16},{64,96},{80,112},{96,64},{112,80},{1... | collective-permute-start | bytes 1572872 | tf_op jit(solution)/shard_map/ppermute | solution.py:178
  29.7 24.1 %collective-permute-start.7 = (bf16[4,512,128]{2,1,0:T(8,128)(2,1)S(1)}, bf16[4,512,128]{2,1,0:T(8,128)(2,1)}, u32[]{:S(2)}, u32[]{:S(2)}) collective-permute-start(bf16[4,512,128]{2,1,0:T(8,128)(2,1)S(1)} %pad_maximum_fusion.refs_2_), channel_id=1, source_target_pairs={{0,64},{16,80},{32,96},{48,112},{64,0},{80,16},{96,32},{112,48},{1... | collective-permute-start | bytes 1572872 | tf_op jit(solution)/shard_map/ppermute | solution.py:178
  32.3 21.5 %collective-permute-start.8 = (bf16[4,512,128]{2,1,0:T(8,128)(2,1)S(1)}, bf16[4,512,128]{2,1,0:T(8,128)(2,1)}, u32[]{:S(2)}, u32[]{:S(2)}) collective-permute-start(bf16[4,512,128]{2,1,0:T(8,128)(2,1)S(1)} %pad_maximum_fusion.refs_2_), channel_id=1, source_target_pairs={{0,256},{16,272},{32,288},{48,304},{64,320},{80,336},{96,352},{112... | collective-permute-start | bytes 1572872 | tf_op jit(solution)/shard_map/ppermute | solution.py:178
  39.2 37.3 %collective-permute-start.4 = (bf16[4,512,128]{2,1,0:T(8,128)(2,1)}, bf16[4,512,128]{2,1,0:T(8,128)(2,1)S(1)}, u32[]{:S(2)}, u32[]{:S(2)}) collective-permute-start(bf16[4,512,128]{2,1,0:T(8,128)(2,1)} %get-tuple-element.18), channel_id=1, source_target_pairs={{0,96},{16,112},{32,64},{48,80},{64,32},{80,48},{96,0},{112,16},{1... | collective-permute-start | bytes 1572872 | tf_op jit(solution)/shard_map/ppermute | solution.py:178
  41.1 35.4 %collective-permute-start.5 = (bf16[4,512,128]{2,1,0:T(8,128)(2,1)}, bf16[4,512,128]{2,1,0:T(8,128)(2,1)S(1)}, u32[]{:S(2)}, u32[]{:S(2)}) collective-permute-start(bf16[4,512,128]{2,1,0:T(8,128)(2,1)} %get-tuple-element.17), channel_id=1, source_target_pairs={{0,64},{16,80},{32,96},{48,112},{64,0},{80,16},{96,32},{112,48},{1... | collective-permute-start | bytes 1572872 | tf_op jit(solution)/shard_map/ppermute | solution.py:178
  111.0 7.1 %collective-permute-start.9 = (bf16[16,64,128]{2,1,0:T(8,128)(2,1)S(1)}, bf16[16,64,128]{2,1,0:T(8,128)(2,1)S(1)}, u32[]{:S(2)}, u32[]{:S(2)}) collective-permute-start(bf16[16,64,128]{2,1,0:T(8,128)(2,1)S(1)} %all_to_all.10.own_ref), channel_id=1, source_target_pairs={{0,32},{16,48},{32,0},{48,16},{64,96},{80,112},{96,64},{112,80},{1... | collective-permute-start | bytes 786440 | tf_op jit(solution)/shard_map/ppermute | solution.py:178
  118.1 2.5 %copy-start = (bf16[2048,1280]{1,0:T(8,128)(2,1)S(1)}, bf16[2048,1280]{1,0:T(8,128)(2,1)}, u32[]{:S(2)}) copy-start(bf16[2048,1280]{1,0:T(8,128)(2,1)} %all-gather.2.cloned.1.call-done.w_ref) | copy-start | bytes 15728644
Sparse Core Ops, SparseCore 0:
  9.4 79.7 all-gather.1

commit v2 on v1

v2 whole, which is shorter than its diff:
```python
import functools
import math

import jax
import jax.numpy as jnp
from jax import lax
from jax.experimental import pallas as pl
from jax.experimental.pallas import tpu as pltpu
from jax.sharding import PartitionSpec as P

HD = 128
BLK = 128
FT = 512
NB = 4
ROWS = 32
TILE = 256
DOUT = 2560
HIDDEN = -1e30
SCALE = math.log2(math.e) / math.sqrt(HD)
VMEM = 40 * 1024 * 1024


def attend_kernel(sources, split, n_kv, first, last, *refs):
    info_ref, mask_ref, q_ref = refs[:3]
    kv_refs = refs[3 : 3 + n_kv]
    rest = refs[3 + n_kv :]
    state_in, outs = ((), rest) if first else (rest[:3], rest[3:])
    tiles = FT // TILE
    blocks = TILE // BLK

    def fold(frame, tile, seen):
        rows = pl.ds(pl.multiple_of(tile * TILE, TILE), TILE)
        q = q_ref[frame, rows, :]
        pieces = []
        for kv_no, cross, level, valid in seen:
            key_frame = 1 - frame if cross else frame
            scores = lax.dot_general(
                q,
                kv_refs[kv_no][2 * key_frame],
                (((1,), (1,)), ((), ())),
                preferred_element_type=jnp.float32,
            )
            here = info_ref[valid] > 0
            piece = []
            for a in range(blocks):
                row = []
                for b in range(NB):
                    shown = mask_ref[(level * NB + tile * blocks + a) * NB + b] > 0
                    bias = jnp.where(here & shown, jnp.float32(0.0), jnp.float32(HIDDEN))
                    block = scores[a * BLK : (a + 1) * BLK, b * BLK : (b + 1) * BLK]
                    row.append(block + bias)
                piece.append(row)
            pieces.append(piece)
        peaks, totals, accs, places = [], [], [], []
        for a in range(blocks):
            place = pl.ds(pl.multiple_of(tile * TILE + a * BLK, BLK), BLK)
            top = functools.reduce(jnp.maximum, [s for piece in pieces for s in piece[a]])
            peak = jnp.max(top, axis=1, keepdims=True)
            if first:
                peak = jnp.broadcast_to(peak, (BLK, BLK))
                totals.append(jnp.zeros((BLK, BLK), jnp.float32))
                accs.append(jnp.zeros((BLK, HD), jnp.float32))
            else:
                old = state_in[0][frame, place, :]
                peak = jnp.maximum(old, peak)
                shrink = jnp.exp2((old - peak) * SCALE)
                totals.append(state_in[1][frame, place, :] * shrink)
                accs.append(state_in[2][frame, place, :] * shrink)
            peaks.append(peak)
            places.append(place)
        acc = jnp.concatenate(accs, axis=0)
        for (kv_no, cross, _, _), piece in zip(seen, pieces):
            key_frame = 1 - frame if cross else frame
            packed = []
            for a in range(blocks):
                weights = [jnp.exp2((s - peaks[a]) * SCALE) for s in piece[a]]
                totals[a] = totals[a] + sum(weights)
                packed.append(
                    jnp.concatenate([w.astype(jnp.bfloat16) for w in weights], axis=1)
                )
            acc = acc + jnp.dot(
                jnp.concatenate(packed, axis=0),
                kv_refs[kv_no][2 * key_frame + 1],
                preferred_element_type=jnp.float32,
            )
        for a in range(blocks):
            part = acc[a * BLK : (a + 1) * BLK]
            if last:
                denom = jnp.sum(totals[a], axis=1, keepdims=True)
                attended = (part / denom).astype(jnp.bfloat16)
                chunk = (tile * blocks + a) * (BLK // ROWS)
                for i in range(BLK // ROWS):
                    outs[0][chunk + i, frame] = attended[i * ROWS : (i + 1) * ROWS]
            else:
                outs[0][frame, places[a], :] = peaks[a]
                outs[1][frame, places[a], :] = totals[a]
                outs[2][frame, places[a], :] = part

    if split is None:

        @pl.loop(0, 2 * tiles)
        def _(step):
            fold(step // tiles, step % tiles, sources)

    else:
        favoured = info_ref[split]

        @pl.loop(0, tiles)
        def _(tile):
            fold(favoured, tile, sources)
            fold(1 - favoured, tile, [s for s in sources if not s[1]])


def attend(info, mask, q, kvs, sources, split, state, last):
    first = state is None
    held = jax.ShapeDtypeStruct((2, FT, HD), jnp.float32)
    if last:
        out_shape = (jax.ShapeDtypeStruct((FT // ROWS, 2, ROWS, HD), jnp.bfloat16),)
    else:
        out_shape = (held,) * 3
    vmem = pl.BlockSpec(memory_space=pltpu.VMEM)
    smem = pl.BlockSpec(memory_space=pltpu.SMEM)
    states = () if first else tuple(state)
    pairs = len(sources) * 2 - (split is not None)
    out = pl.pallas_call(
        functools.partial(attend_kernel, sources, split, len(kvs), first, last),
        out_shape=out_shape,
        in_specs=[smem, smem] + [vmem] * (1 + len(kvs) + len(states)),
        out_specs=(vmem,) * len(out_shape),
        compiler_params=pltpu.CompilerParams(vmem_limit_bytes=VMEM),
        cost_estimate=pl.CostEstimate(
            flops=pairs * 4 * FT * FT * HD,
            bytes_accessed=len(kvs) * 4 * FT * HD * 2,
            transcendentals=pairs * FT * FT,
        ),
    )(info, mask, q, *kvs, *states)
    return out[0] if last else out


def trade_kernel(place_ref, q_ref, k_ref, v_ref, w_ref, kv_out, q_out, give_out, w_out, sems):
    core, side = place_ref[0], place_ref[1]
    mine = pl.ds(pl.multiple_of(core * HD, HD), HD)
    yours = pl.ds(pl.multiple_of((1 - core) * HD, HD), HD)
    half = w_out.shape[1]
    columns = pl.ds(pl.multiple_of(side * half, HD), half)
    moves = [
        (k_ref.at[:, yours], give_out.at[0]),
        (v_ref.at[:, yours], give_out.at[1]),
        (q_ref.at[:, yours], give_out.at[2]),
        (k_ref.at[:, mine], kv_out.at[0]),
        (v_ref.at[:, mine], kv_out.at[1]),
        (q_ref.at[:, mine], q_out.at[0]),
        (w_ref.at[mine, columns], w_out),
    ]
    copies = [
        pltpu.make_async_copy(src, dst, sems.at[n]) for n, (src, dst) in enumerate(moves)
    ]
    for copy in copies:
        copy.start()
    for copy in copies:
        copy.wait()


def trade(place, queries, keys, values, out_weight):
    hbm = pl.BlockSpec(memory_space=pl.ANY)
    smem = pl.BlockSpec(memory_space=pltpu.SMEM)
    kind = queries.dtype
    return pl.pallas_call(
        trade_kernel,
        out_shape=(
            jax.ShapeDtypeStruct((4, FT, HD), kind),
            jax.ShapeDtypeStruct((2, FT, HD), kind),
            jax.ShapeDtypeStruct((3, FT, HD), kind),
            jax.ShapeDtypeStruct((HD, DOUT // 2), kind),
        ),
        in_specs=[smem, hbm, hbm, hbm, hbm],
        out_specs=(hbm,) * 4,
        scratch_shapes=[pltpu.SemaphoreType.DMA((7,))],
        compiler_params=pltpu.CompilerParams(vmem_limit_bytes=56 * 1024 * 1024),
    )(place, queries, keys, values, out_weight)


def project_kernel(place_ref, own_ref, other_ref, w_ref, out_ref, lhs_ref):
    @pl.when(pl.program_id(0) == 0)
    def _():
        for z in range(own_ref.shape[0]):
            cols = slice(z * HD, (z + 1) * HD)
            lhs_ref[: 2 * ROWS, cols] = own_ref[z]
            lhs_ref[2 * ROWS :, cols] = other_ref[z]

    part = jnp.dot(lhs_ref[...], w_ref[...], preferred_element_type=jnp.float32)
    part = part.astype(jnp.bfloat16)
    for k in range(4):
        out_ref[place_ref[k]] = part[k * ROWS : (k + 1) * ROWS]


def project(place, own, other, weight):
    groups = own.shape[0]
    depth, width = weight.shape
    step = 256
    return pl.pallas_call(
        project_kernel,
        grid=(width // step,),
        out_shape=jax.ShapeDtypeStruct((4, ROWS, width), jnp.bfloat16),
        in_specs=[
            pl.BlockSpec(memory_space=pltpu.SMEM),
            pl.BlockSpec((groups, 2 * ROWS, HD), lambda n: (0, 0, 0)),
            pl.BlockSpec((groups, 2 * ROWS, HD), lambda n: (0, 0, 0)),
            pl.BlockSpec((depth, step), lambda n: (0, n)),
        ],
        out_specs=pl.BlockSpec((4, ROWS, step), lambda n: (0, 0, n)),
        scratch_shapes=[pltpu.VMEM((4 * ROWS, depth), jnp.bfloat16)],
        compiler_params=pltpu.CompilerParams(vmem_limit_bytes=56 * 1024 * 1024),
        cost_estimate=pl.CostEstimate(
            flops=8 * ROWS * depth * width, bytes_accessed=depth * width * 2, transcendentals=0
        ),
    )(place, own, other, weight)


def add_kernel(in_ref, out_ref):
    half = in_ref.shape[2]
    for p in range(2):
        both = in_ref[2 * p].astype(jnp.float32) + in_ref[2 * p + 1].astype(jnp.float32)
        out_ref[:, p * half : (p + 1) * half] = both.astype(jnp.bfloat16)


def add_cores(parts):
    return pl.pallas_call(
        add_kernel,
        out_shape=jax.ShapeDtypeStruct((ROWS, 2 * parts.shape[2]), jnp.bfloat16),
        in_specs=[pl.BlockSpec(memory_space=pltpu.VMEM)],
        out_specs=pl.BlockSpec(memory_space=pltpu.VMEM),
        compiler_params=pltpu.CompilerParams(vmem_limit_bytes=VMEM),
    )(parts)


def shards(queries, keys, values, block_mask, out_weight):
    me = lax.axis_index("tm")
    core = me % 2
    y = (me // 2) % 4
    x = me // 8
    side = y % 2

    def chips(go):
        pairs = []
        for i in range(32):
            to = go(i // 8, (i // 2) % 4)
            if to is not None:
                pairs.append((i, to[0] * 8 + to[1] * 2 + i % 2))
        return pairs

    def send(array, pairs):
        return lax.ppermute(array, "tm", pairs)

    place = jnp.stack([core, side]).astype(jnp.int32)
    kv_own, q_own, give, weight = trade(place, queries, keys, values, out_weight)
    weight = lax.all_gather(weight, "head", axis=0, tiled=True)
    got = send(give, [(i, i ^ 1) for i in range(32)])
    local = lax.dynamic_update_slice(kv_own, got[:2], (2, 0, 0))
    q = lax.dynamic_update_slice(q_own, got[2:], (1, 0, 0))

    above = send(local, chips(lambda x, y: (x + 1, y) if x < 3 else None))
    across = send(local, chips(lambda x, y: (x, y ^ 2)))
    below = send(local, chips(lambda x, y: (x - 1, y) if x > 0 else None))
    beside = send(local, chips(lambda x, y: (x, y ^ 1)))
    far = send(local, chips(lambda x, y: (x ^ 2, y)))
    turned = jnp.where((y == 1) | (y == 2), local, jnp.where(y == 3, above, below))
    other = send(turned, chips(lambda x, y: (x, 3 - y)))

    def next_row(x, y):
        to = x + 1 if y < 2 else x - 1
        return (to, y) if 0 <= to < 4 else None

    across_row = send(across, chips(next_row))

    odd = y % 2
    has_above, has_below = x > 0, x < 3
    row_end = jnp.where(y == 0, has_above, jnp.where(y == 3, has_below, True))
    row_cross = jnp.where(y < 2, has_above, has_below)
    info = jnp.stack(
        [
            core ^ odd ^ 1,
            core ^ odd,
            jnp.int32(1),
            row_end.astype(jnp.int32),
            row_cross.astype(jnp.int32),
            has_above.astype(jnp.int32),
            has_below.astype(jnp.int32),
        ]
    ).astype(jnp.int32)
    mask = block_mask.reshape(-1)

    state = attend(info, mask, q, [local], [(0, False, 0, 2), (0, True, 1, 2)], None, None, False)
    state = attend(
        info,
        mask,
        q,
        [beside, across, above, below, far],
        [
            (0, False, 2, 2),
            (0, True, 1, 2),
            (1, False, 3, 2),
            (2, False, 4, 5),
            (3, False, 4, 6),
            (4, False, 5, 2),
        ],
        0,
        state,
        False,
    )
    attended = attend(
        info,
        mask,
        q,
        [other, across_row],
        [(0, False, 2, 3), (0, True, 1, 3), (1, False, 3, 4)],
        1,
        state,
        True,
    )

    rows = lax.all_to_all(
        attended.reshape(FT // ROWS, 2 * ROWS, HD), "head", 0, 0, tiled=True
    )
    partner = send(rows, [(i, i ^ 2) for i in range(32)])
    here = me % 4
    place = jnp.stack([here, here ^ 1, here ^ 2, here ^ 3]).astype(jnp.int32)
    parts = project(place, rows, partner, weight)
    quads = [[4 * j + k for k in range(4)] for j in range(8)]
    parts = lax.all_to_all(parts, "tm", 0, 0, tiled=True, axis_index_groups=quads)
    return add_cores(parts)


def solution(mesh):
    return jax.shard_map(
        shards,
        mesh=mesh,
        in_specs=(P("tm", "head"), P("tm", "head"), P("tm", "head"), P(), P("head", None)),
        out_specs=P(("tm", "head"), None),
        check_vma=False,
    )
```

time: 147 us -> 164 us (1.12)
  Pallas kernels: 21.9 us -> 54.1 us
  waiting for transfers between devices: 25.1 us -> 13 us
  blocking collectives: 43.4 us -> 46 us
  other arithmetic: 4.2 us -> 2.13 us
  starting transfers between devices: 31.3 us -> 29.5 us
    pallas_call x3 -> x4, Pallas kernels: 18.5 us -> 47.6 us  [the longest x1 35.6 us: trade(): pl.pallas_call(trade_kernel, out_shape=(jax.ShapeDtypeStruct((4, FT, HD),...]
    ppermute x10 -> x9, waiting for transfers between devices: 25.1 us -> 10.1 us  [send(): return lax.ppermute(array, 'tm', pairs)]
    pallas_call x1, Pallas kernels: 2.65 us -> 5.75 us  [project(): pl.pallas_call(project_kernel, grid=(width // step,), out_shape=jax.Shape...]
    all_gather x1, waiting for transfers between devices: 0.01 us -> 2.93 us  [shards(): weight = lax.all_gather(weight, 'head', axis=0, tiled=True)]
    ppermute x10 -> x9, starting transfers between devices: 31.3 us -> 29.4 us  [send(): return lax.ppermute(array, 'tm', pairs)]
    dynamic_slice x1 -> x0, local copies, waits for them, and re-layouts: 1.71 us -> none  [shards(): weight = lax.dynamic_slice(out_weight, (core * HD, side * half), (HD, half))]
    all_to_all x1, blocking collectives: 28.7 us -> 30.4 us  [shards(): lax.all_to_all(attended.reshape(FT // ROWS, 2 * ROWS, HD), 'head', 0, 0,...]
    unnamed x3 -> x11, local copies, waits for them, and re-layouts: 3.29 us -> 3.75 us
  transfers between devices with their start and end apart: 11 -> 10, of which waited for: 4 -> 5; matrix products, arithmetic and copies ran while one was open for 4% -> 2% of each run, Pallas kernels for 13% -> 7%
where the time goes in v2:
time: 164 us
  Pallas kernels  54.1 us (33%)
  blocking collectives  46 us (28%)
  starting transfers between devices  29.5 us (18%)
  between operations  13.6 us (8%)
  waiting for transfers between devices  13 us (8%)
  local copies, waits for them, and re-layouts  5.32 us (3%)
  other arithmetic  2.13 us (1%)
    pallas_call x1, Pallas kernels, trade(): pl.pallas_call(trade_kernel, out_shape=(jax.ShapeDtypeStruct((4, FT, HD),...  35.6 us
    all_to_all x1, blocking collectives, shards(): lax.all_to_all(attended.reshape(FT // ROWS, 2 * ROWS, HD), 'head', 0, 0,...  30.4 us
    ppermute x9, starting transfers between devices, send(): return lax.ppermute(array, 'tm', pairs)  29.4 us
    all_to_all x1, blocking collectives, shards(): lax.all_to_all(parts, 'tm', 0, 0, tiled=True, axis_index_groups=quads)  15.6 us
    pallas_call x3, Pallas kernels, attend(): pl.pallas_call(functools.partial(attend_kernel, sources, split, len(kvs),...  12.1 us
    ppermute x9, waiting for transfers between devices, send(): return lax.ppermute(array, 'tm', pairs)  10.1 us
    pallas_call x1, Pallas kernels, project(): pl.pallas_call(project_kernel, grid=(width // step,), out_shape=jax.Shape...  5.75 us
    unnamed x11, local copies, waits for them, and re-layouts  3.75 us
  transfers between devices with their start and end apart: 10, of which 5 were waited for; matrix products, arithmetic and copies ran while one was open for 2% of the time, Pallas kernels for 7%

profile of v2, /device:TPU:1, one launch (start us, length us, event | category | flops | bytes accessed | tf_op | source)
XLA Modules:
  0.0 163.6 jit_solution(4526254743278710141)
XLA Ops:
  6.5 0.0 all-gather.2.cloned.1.call-start
  6.5 0.7 pad_add_fusion.1.place_ref
  7.2 35.6 %shard_map.55 = (bf16[4,512,128]{2,1,0:T(8,128)(2,1)}, bf16[2,512,128]{2,1,0:T(8,128)(2,1)}, bf16[3,512,128]{2,1,0:T(8,128)(2,1)}, bf16[128,1280]{1,0:T(8,128)(2,1)}) custom-call(s32[2]{0:T(128)} %pad_add_fusion.1.place_ref, bf16[512,256]{1,0:T(8,128)(2,1)} %q_ref.1, bf16[512,256]{1,0:T(8,128)(2,1)} %k_ref.1, bf16[512,256]{1,0:T(8,128)(2,1)} %v_ref.1, ...), custom_call_target="tpu_custom_call" | custom-call | tf_op jit(solution)/shard_map/pallas_call | solution.py:168
  42.8 0.0 all-gather.2.cloned.1.call-update
  42.8 8.8 %collective-permute-start = (bf16[3,512,128]{2,1,0:T(8,128)(2,1)}, bf16[3,512,128]{2,1,0:T(8,128)(2,1)S(1)}, u32[]{:S(2)}, u32[]{:S(2)}) collective-permute-start(bf16[3,512,128]{2,1,0:T(8,128)(2,1)} %get-tuple-element.16), channel_id=1, source_target_pairs={{0,16},{16,0},{32,48},{48,32},{64,80},{80,64},{96,112},{112,96},{1... | collective-permute-start | bytes 1179656 | tf_op jit(solution)/shard_map/ppermute | solution.py:253
  51.6 1.5 collective-permute-done
  53.1 0.7 slice_dynamic-update-slice_fusion.refs_3_
  53.9 1.3 collective-permute-start.1
  55.2 1.3 collective-permute-start.2
  56.5 1.9 %collective-permute-start.4 = (bf16[4,512,128]{2,1,0:T(8,128)(2,1)}, bf16[4,512,128]{2,1,0:T(8,128)(2,1)S(1)}, u32[]{:S(2)}, u32[]{:S(2)}) collective-permute-start(bf16[4,512,128]{2,1,0:T(8,128)(2,1)} %slice_dynamic-update-slice_fusion.refs_3_), channel_id=1, source_target_pairs={{0,64},{16,80},{32,96},{48,112},{64,0},{80,16},{96,32},{112,48},{1... | collective-permute-start | bytes 1572872 | tf_op jit(solution)/shard_map/ppermute | solution.py:253
  58.4 1.9 %collective-permute-start.6 = (bf16[4,512,128]{2,1,0:T(8,128)(2,1)}, bf16[4,512,128]{2,1,0:T(8,128)(2,1)S(1)}, u32[]{:S(2)}, u32[]{:S(2)}) collective-permute-start(bf16[4,512,128]{2,1,0:T(8,128)(2,1)} %slice_dynamic-update-slice_fusion.refs_3_), channel_id=1, source_target_pairs={{0,32},{16,48},{32,0},{48,16},{64,96},{80,112},{96,64},{112,80},{1... | collective-permute-start | bytes 1572872 | tf_op jit(solution)/shard_map/ppermute | solution.py:253
  60.4 5.2 %collective-permute-start.7 = (bf16[4,512,128]{2,1,0:T(8,128)(2,1)}, bf16[4,512,128]{2,1,0:T(8,128)(2,1)}, u32[]{:S(2)}, u32[]{:S(2)}) collective-permute-start(bf16[4,512,128]{2,1,0:T(8,128)(2,1)} %slice_dynamic-update-slice_fusion.refs_3_), channel_id=1, source_target_pairs={{0,256},{16,272},{32,288},{48,304},{64,320},{80,336},{96,352},{112... | collective-permute-start | bytes 1572872 | tf_op jit(solution)/shard_map/ppermute | solution.py:253
  65.6 1.1 collective-permute-done.1.refs_5_
  66.7 3.8 %collective-permute-done.2.refs_6_ = bf16[4,512,128]{2,1,0:T(8,128)(2,1)S(1)} collective-permute-done((bf16[4,512,128]{2,1,0:T(8,128)(2,1)}, bf16[4,512,128]{2,1,0:T(8,128)(2,1)S(1)}, u32[]{:S(2)}, u32[]{:S(2)}) %collective-permute-start.2) | collective-permute-done | bytes 524320 | tf_op jit(solution)/shard_map/ppermute | solution.py:253
  70.5 0.9 select_select_fusion
  71.4 1.9 %collective-permute-start.3 = (bf16[4,512,128]{2,1,0:T(8,128)(2,1)}, bf16[4,512,128]{2,1,0:T(8,128)(2,1)S(1)}, u32[]{:S(2)}, u32[]{:S(2)}) collective-permute-start(bf16[4,512,128]{2,1,0:T(8,128)(2,1)} %select_select_fusion), channel_id=1, source_target_pairs={{0,96},{16,112},{32,64},{48,80},{64,32},{80,48},{96,0},{112,16},{1... | collective-permute-start | bytes 1572872 | tf_op jit(solution)/shard_map/ppermute | solution.py:253
  73.4 0.0 collective-permute-done.4.refs_4_
  73.4 3.5 %collective-permute-start.5 = (bf16[4,512,128]{2,1,0:T(8,128)(2,1)S(1)}, bf16[4,512,128]{2,1,0:T(8,128)(2,1)S(1)}, u32[]{:S(2)}, u32[]{:S(2)}) collective-permute-start(bf16[4,512,128]{2,1,0:T(8,128)(2,1)S(1)} %collective-permute-done.4.refs_4_), channel_id=1, source_target_pairs={{0,128},{16,144},{32,160},{48,176},{128,256},{144,272},{160,288},{... | collective-permute-start | bytes 1572872 | tf_op jit(solution)/shard_map/ppermute | solution.py:253
  77.0 0.8 copy.7
  77.8 0.1 reshape.6.refs_1_
  77.9 0.1 stack.72.refs_0_
  78.0 0.7 slice_dynamic-update-slice_fusion.1.refs_2_
  78.6 0.0 copy-start
  78.6 1.0 copy-done
  79.7 0.0 copy-start.1
  79.7 1.0 copy-done.1
  80.6 3.0 %shard_map.56 = (f32[2,512,128]{2,1,0:T(8,128)S(1)}, f32[2,512,128]{2,1,0:T(8,128)S(1)}, f32[2,512,128]{2,1,0:T(8,128)S(1)}) custom-call(s32[7]{0:T(128)S(1)} %stack.72.refs_0_, s32[96]{0:T(128)S(1)} %reshape.6.refs_1_, bf16[2,512,128]{2,1,0:T(8,128)(2,1)S(1)} %copy-done.1, bf16[4,512,128]{2,1,0:T(8,128)(2,1)S(1)} %copy-done), custom_call_target="tpu_custom_call" | custom-call | flops 536870912 | bytes 524288 | tf_op jit(solution)/shard_map/pallas_call | solution.py:125
  83.6 0.0 collective-permute-done.6.refs_3_
  83.6 0.0 collective-permute-done.7.refs_7_
  83.7 0.0 copy-start.2
  83.7 0.9 copy-done.2
  84.6 5.9 %shard_map.57 = (f32[2,512,128]{2,1,0:T(8,128)S(1)}, f32[2,512,128]{2,1,0:T(8,128)S(1)}, f32[2,512,128]{2,1,0:T(8,128)S(1)}) custom-call(s32[7]{0:T(128)S(1)} %stack.72.refs_0_, s32[96]{0:T(128)S(1)} %reshape.6.refs_1_, bf16[2,512,128]{2,1,0:T(8,128)(2,1)S(1)} %copy-done.2, bf16[4,512,128]{2,1,0:T(8,128)(2,1)S(1)} %collective-permute-done.6.refs_3_, ...), custom_call_target="tpu_custom_call" | custom-call | flops 1476395008 | bytes 2621440 | tf_op jit(solution)/shard_map/pallas_call | solution.py:125
  90.5 0.0 collective-permute-done.3.refs_3_
  90.5 0.0 collective-permute-done.5.refs_4_
  90.5 3.2 %shard_map.58 = bf16[16,2,32,128]{3,2,1,0:T(8,128)(2,1)S(1)} custom-call(s32[7]{0:T(128)S(1)} %stack.72.refs_0_, s32[96]{0:T(128)S(1)} %reshape.6.refs_1_, bf16[2,512,128]{2,1,0:T(8,128)(2,1)S(1)} %copy-done.2, bf16[4,512,128]{2,1,0:T(8,128)(2,1)S(1)} %collective-permute-done.3.refs_3_, bf16[4,512,128]{2,1,0:T(8,128)(2,1)S(1)} %collective-permute-done.5.refs_4_, ...), custom_call_target="tpu_custom_call" | custom-call | flops 671088640 | bytes 1048576 | tf_op jit(solution)/shard_map/pallas_call | solution.py:125
  93.7 30.4 %all_to_all.10.own_ref = bf16[16,64,128]{2,1,0:T(8,128)(2,1)S(1)} all-to-all(bf16[16,64,128]{2,1,0:T(8,128)(2,1)S(1)} %bitcast.13), channel_id=1, replica_groups=mesh['tm'=32,'head'=16] {'head'}, dimensions={0} | all-to-all | bytes 524288 | tf_op jit(solution)/shard_map/all_to_all | solution.py:322
  124.1 0.0 copy-start.3
  124.1 3.5 %collective-permute-start.8 = (bf16[16,64,128]{2,1,0:T(8,128)(2,1)S(1)}, bf16[16,64,128]{2,1,0:T(8,128)(2,1)S(1)}, u32[]{:S(2)}, u32[]{:S(2)}) collective-permute-start(bf16[16,64,128]{2,1,0:T(8,128)(2,1)S(1)} %all_to_all.10.own_ref), channel_id=1, source_target_pairs={{0,32},{16,48},{32,0},{48,16},{64,96},{80,112},{96,64},{112,80},{1... | collective-permute-start | bytes 786440 | tf_op jit(solution)/shard_map/ppermute | solution.py:253
  127.6 0.6 pad_add_fusion.place_ref
  128.2 3.6 %collective-permute-done.8.other_ref = bf16[16,64,128]{2,1,0:T(8,128)(2,1)S(1)} collective-permute-done((bf16[16,64,128]{2,1,0:T(8,128)(2,1)S(1)}, bf16[16,64,128]{2,1,0:T(8,128)(2,1)S(1)}, u32[]{:S(2)}, u32[]{:S(2)}) %collective-permute-start.8) | collective-permute-done | bytes 262176 | tf_op jit(solution)/shard_map/ppermute | solution.py:253
  131.8 0.0 copy-start.4
  131.8 2.9 %all-gather.2.cloned.1.call-done.w_ref = bf16[2048,1280]{1,0:T(8,128)(2,1)} async-done(((bf16[128,1280]{1,0:T(8,128)(2,1)}), bf16[2048,1280]{1,0:T(8,128)(2,1)}) %all-gather.2.cloned.1.call-update) | async-done | bytes 5242896 | tf_op jit(solution)/shard_map/all_gather | solution.py:257
  134.7 0.0 copy-done.3
  134.7 0.0 copy-done.4
  134.7 5.7 %shard_map.59 = bf16[4,32,1280]{2,1,0:T(8,128)(2,1)} custom-call(s32[4]{0:T(128)} %pad_add_fusion.place_ref, bf16[16,64,128]{2,1,0:T(8,128)(2,1)} %copy-done.3, bf16[16,64,128]{2,1,0:T(8,128)(2,1)} %copy-done.4, bf16[2048,1280]{1,0:T(8,128)(2,1)} %all-gather.2.cloned.1.call-done.w_ref), custom_call_target="tpu_custom_call" | custom-call | flops 671088640 | bytes 5242880 | tf_op jit(solution)/shard_map/pallas_call | solution.py:201
  140.5 15.6 %all_to_all.11.in_ref = bf16[4,32,1280]{2,1,0:T(8,128)(2,1)S(1)} all-to-all(bf16[4,32,1280]{2,1,0:T(8,128)(2,1)} %shard_map.59), channel_id=1, replica_groups={{0,16,32,48},{64,80,96,112},{128,144,160,176},{192,208,224,240},{256,27..., dimensions={0} | all-to-all | bytes 655360 | tf_op jit(solution)/shard_map/all_to_all | solution.py:330
  156.0 0.7 shard_map.60
Async XLA Ops:
  6.5 128.2 %all-gather.2.cloned.1.call-start = ((), (), s32[]{:S(2)}) async-start(), calls=%async_computation.2 | async-start | bytes 5570560 | tf_op jit(solution)/shard_map/all_gather | solution.py:257
  42.8 10.3 %collective-permute-start = (bf16[3,512,128]{2,1,0:T(8,128)(2,1)}, bf16[3,512,128]{2,1,0:T(8,128)(2,1)S(1)}, u32[]{:S(2)}, u32[]{:S(2)}) collective-permute-start(bf16[3,512,128]{2,1,0:T(8,128)(2,1)} %get-tuple-element.16), channel_id=1, source_target_pairs={{0,16},{16,0},{32,48},{48,32},{64,80},{80,64},{96,112},{112,96},{1... | collective-permute-start | bytes 1179656 | tf_op jit(solution)/shard_map/ppermute | solution.py:253
  53.9 12.8 %collective-permute-start.1 = (bf16[4,512,128]{2,1,0:T(8,128)(2,1)}, bf16[4,512,128]{2,1,0:T(8,128)(2,1)S(1)}, u32[]{:S(2)}, u32[]{:S(2)}) collective-permute-start(bf16[4,512,128]{2,1,0:T(8,128)(2,1)} %slice_dynamic-update-slice_fusion.refs_3_), channel_id=1, source_target_pairs={{0,128},{16,144},{32,160},{48,176},{64,192},{80,208},{96,224},{112... | collective-permute-start | bytes 1572872 | tf_op jit(solution)/shard_map/ppermute | solution.py:253
  55.2 15.3 %collective-permute-start.2 = (bf16[4,512,128]{2,1,0:T(8,128)(2,1)}, bf16[4,512,128]{2,1,0:T(8,128)(2,1)S(1)}, u32[]{:S(2)}, u32[]{:S(2)}) collective-permute-start(bf16[4,512,128]{2,1,0:T(8,128)(2,1)} %slice_dynamic-update-slice_fusion.refs_3_), channel_id=1, source_target_pairs={{128,0},{144,16},{160,32},{176,48},{192,64},{208,80},{224,96},{240... | collective-permute-start | bytes 1572872 | tf_op jit(solution)/shard_map/ppermute | solution.py:253
  56.5 16.9 %collective-permute-start.4 = (bf16[4,512,128]{2,1,0:T(8,128)(2,1)}, bf16[4,512,128]{2,1,0:T(8,128)(2,1)S(1)}, u32[]{:S(2)}, u32[]{:S(2)}) collective-permute-start(bf16[4,512,128]{2,1,0:T(8,128)(2,1)} %slice_dynamic-update-slice_fusion.refs_3_), channel_id=1, source_target_pairs={{0,64},{16,80},{32,96},{48,112},{64,0},{80,16},{96,32},{112,48},{1... | collective-permute-start | bytes 1572872 | tf_op jit(solution)/shard_map/ppermute | solution.py:253
  58.4 25.2 %collective-permute-start.6 = (bf16[4,512,128]{2,1,0:T(8,128)(2,1)}, bf16[4,512,128]{2,1,0:T(8,128)(2,1)S(1)}, u32[]{:S(2)}, u32[]{:S(2)}) collective-permute-start(bf16[4,512,128]{2,1,0:T(8,128)(2,1)} %slice_dynamic-update-slice_fusion.refs_3_), channel_id=1, source_target_pairs={{0,32},{16,48},{32,0},{48,16},{64,96},{80,112},{96,64},{112,80},{1... | collective-permute-start | bytes 1572872 | tf_op jit(solution)/shard_map/ppermute | solution.py:253
  60.4 23.3 %collective-permute-start.7 = (bf16[4,512,128]{2,1,0:T(8,128)(2,1)}, bf16[4,512,128]{2,1,0:T(8,128)(2,1)}, u32[]{:S(2)}, u32[]{:S(2)}) collective-permute-start(bf16[4,512,128]{2,1,0:T(8,128)(2,1)} %slice_dynamic-update-slice_fusion.refs_3_), channel_id=1, source_target_pairs={{0,256},{16,272},{32,288},{48,304},{64,320},{80,336},{96,352},{112... | collective-permute-start | bytes 1572872 | tf_op jit(solution)/shard_map/ppermute | solution.py:253
  71.4 19.0 %collective-permute-start.3 = (bf16[4,512,128]{2,1,0:T(8,128)(2,1)}, bf16[4,512,128]{2,1,0:T(8,128)(2,1)S(1)}, u32[]{:S(2)}, u32[]{:S(2)}) collective-permute-start(bf16[4,512,128]{2,1,0:T(8,128)(2,1)} %select_select_fusion), channel_id=1, source_target_pairs={{0,96},{16,112},{32,64},{48,80},{64,32},{80,48},{96,0},{112,16},{1... | collective-permute-start | bytes 1572872 | tf_op jit(solution)/shard_map/ppermute | solution.py:253
  73.4 17.1 %collective-permute-start.5 = (bf16[4,512,128]{2,1,0:T(8,128)(2,1)S(1)}, bf16[4,512,128]{2,1,0:T(8,128)(2,1)S(1)}, u32[]{:S(2)}, u32[]{:S(2)}) collective-permute-start(bf16[4,512,128]{2,1,0:T(8,128)(2,1)S(1)} %collective-permute-done.4.refs_4_), channel_id=1, source_target_pairs={{0,128},{16,144},{32,160},{48,176},{128,256},{144,272},{160,288},{... | collective-permute-start | bytes 1572872 | tf_op jit(solution)/shard_map/ppermute | solution.py:253
  78.6 1.0 copy-start
  79.7 1.0 copy-start.1
  83.7 1.0 copy-start.2
  124.1 10.6 %copy-start.3 = (bf16[16,64,128]{2,1,0:T(8,128)(2,1)}, bf16[16,64,128]{2,1,0:T(8,128)(2,1)S(1)}, u32[]{:S(2)}) copy-start(bf16[16,64,128]{2,1,0:T(8,128)(2,1)S(1)} %all_to_all.10.own_ref) | copy-start | bytes 786436
  124.1 7.7 %collective-permute-start.8 = (bf16[16,64,128]{2,1,0:T(8,128)(2,1)S(1)}, bf16[16,64,128]{2,1,0:T(8,128)(2,1)S(1)}, u32[]{:S(2)}, u32[]{:S(2)}) collective-permute-start(bf16[16,64,128]{2,1,0:T(8,128)(2,1)S(1)} %all_to_all.10.own_ref), channel_id=1, source_target_pairs={{0,32},{16,48},{32,0},{48,16},{64,96},{80,112},{96,64},{112,80},{1... | collective-permute-start | bytes 786440 | tf_op jit(solution)/shard_map/ppermute | solution.py:253
  131.8 2.9 %copy-start.4 = (bf16[16,64,128]{2,1,0:T(8,128)(2,1)}, bf16[16,64,128]{2,1,0:T(8,128)(2,1)S(1)}, u32[]{:S(2)}) copy-start(bf16[16,64,128]{2,1,0:T(8,128)(2,1)S(1)} %collective-permute-done.8.other_ref) | copy-start | bytes 786436
Sparse Core Ops, SparseCore 0:
  42.9 91.7 all-gather.1

commit v3 on v2

--- a/solution.py
+++ b/solution.py
@@ -137,79 +137,89 @@
     return out[0] if last else out
 
 
-def trade_kernel(place_ref, q_ref, k_ref, v_ref, w_ref, kv_out, q_out, give_out, w_out, sems):
-    core, side = place_ref[0], place_ref[1]
-    mine = pl.ds(pl.multiple_of(core * HD, HD), HD)
-    yours = pl.ds(pl.multiple_of((1 - core) * HD, HD), HD)
-    half = w_out.shape[1]
-    columns = pl.ds(pl.multiple_of(side * half, HD), half)
-    moves = [
-        (k_ref.at[:, yours], give_out.at[0]),
-        (v_ref.at[:, yours], give_out.at[1]),
-        (q_ref.at[:, yours], give_out.at[2]),
-        (k_ref.at[:, mine], kv_out.at[0]),
-        (v_ref.at[:, mine], kv_out.at[1]),
-        (q_ref.at[:, mine], q_out.at[0]),
-        (w_ref.at[mine, columns], w_out),
-    ]
-    copies = [
-        pltpu.make_async_copy(src, dst, sems.at[n]) for n, (src, dst) in enumerate(moves)
-    ]
-    for copy in copies:
-        copy.start()
-    for copy in copies:
-        copy.wait()
+def trade_kernel(place_ref, *refs):
+    k_mine, v_mine, q_mine, k_yours, v_yours, q_yours, w_block = refs[:7]
+    kv_out, q_out, give_out, w_out = refs[7:]
+    kv_out[0] = k_mine[...]
+    kv_out[1] = v_mine[...]
+    q_out[0] = q_mine[...]
+    give_out[0] = k_yours[...]
+    give_out[1] = v_yours[...]
+    give_out[2] = q_yours[...]
+    w_out[...] = w_block[...]
 
 
 def trade(place, queries, keys, values, out_weight):
-    hbm = pl.BlockSpec(memory_space=pl.ANY)
-    smem = pl.BlockSpec(memory_space=pltpu.SMEM)
     kind = queries.dtype
+    half = DOUT // 2
+    mine = pl.BlockSpec((FT, HD), lambda n, place: (0, place[0]))
+    yours = pl.BlockSpec((FT, HD), lambda n, place: (0, 1 - place[0]))
     return pl.pallas_call(
         trade_kernel,
         out_shape=(
             jax.ShapeDtypeStruct((4, FT, HD), kind),
             jax.ShapeDtypeStruct((2, FT, HD), kind),
             jax.ShapeDtypeStruct((3, FT, HD), kind),
-            jax.ShapeDtypeStruct((HD, DOUT // 2), kind),
+            jax.ShapeDtypeStruct((HD, half), kind),
         ),
-        in_specs=[smem, hbm, hbm, hbm, hbm],
-        out_specs=(hbm,) * 4,
-        scratch_shapes=[pltpu.SemaphoreType.DMA((7,))],
+        grid_spec=pltpu.PrefetchScalarGridSpec(
+            num_scalar_prefetch=1,
+            grid=(1,),
+            in_specs=[mine] * 3
+            + [yours] * 3
+            + [pl.BlockSpec((HD, half), lambda n, place: (place[0], place[1]))],
+            out_specs=(
+                pl.BlockSpec((2, FT, HD), lambda n, place: (0, 0, 0)),
+                pl.BlockSpec((1, FT, HD), lambda n, place: (0, 0, 0)),
+                pl.BlockSpec((3, FT, HD), lambda n, place: (0, 0, 0)),
+                pl.BlockSpec((HD, half), lambda n, place: (0, 0)),
+            ),
+        ),
         compiler_params=pltpu.CompilerParams(vmem_limit_bytes=56 * 1024 * 1024),
-    )(place, queries, keys, values, out_weight)
-
-
-def project_kernel(place_ref, own_ref, other_ref, w_ref, out_ref, lhs_ref):
-    @pl.when(pl.program_id(0) == 0)
+    )(place, keys, values, queries, keys, values, queries, out_weight)
+
+
+def project_kernel(place_ref, own_ref, other_ref, w_ref, out_ref, acc_ref):
+    step = pl.program_id(0)
+    rows = [
+        jnp.concatenate([ref[z] for z in range(own_ref.shape[0])], axis=1)
+        for ref in (own_ref, other_ref)
+    ]
+    part = jnp.dot(
+        jnp.concatenate(rows, axis=0), w_ref[...], preferred_element_type=jnp.float32
+    )
+
+    @pl.when(step == 0)
     def _():
-        for z in range(own_ref.shape[0]):
-            cols = slice(z * HD, (z + 1) * HD)
-            lhs_ref[: 2 * ROWS, cols] = own_ref[z]
-            lhs_ref[2 * ROWS :, cols] = other_ref[z]
-
-    part = jnp.dot(lhs_ref[...], w_ref[...], preferred_element_type=jnp.float32)
-    part = part.astype(jnp.bfloat16)
-    for k in range(4):
-        out_ref[place_ref[k]] = part[k * ROWS : (k + 1) * ROWS]
+        acc_ref[...] = part
+
+    @pl.when(step > 0)
+    def _():
+        acc_ref[...] += part
+
+    @pl.when(step == pl.num_programs(0) - 1)
+    def _():
+        for k in range(4):
+            out_ref[place_ref[k]] = acc_ref[k * ROWS : (k + 1) * ROWS].astype(jnp.bfloat16)
 
 
 def project(place, own, other, weight):
     groups = own.shape[0]
     depth, width = weight.shape
-    step = 256
+    steps = 4
+    rows = pl.BlockSpec((groups // steps, 2 * ROWS, HD), lambda n: (n, 0, 0))
     return pl.pallas_call(
         project_kernel,
-        grid=(width // step,),
+        grid=(steps,),
         out_shape=jax.ShapeDtypeStruct((4, ROWS, width), jnp.bfloat16),
         in_specs=[
             pl.BlockSpec(memory_space=pltpu.SMEM),
-            pl.BlockSpec((groups, 2 * ROWS, HD), lambda n: (0, 0, 0)),
-            pl.BlockSpec((groups, 2 * ROWS, HD), lambda n: (0, 0, 0)),
-            pl.BlockSpec((depth, step), lambda n: (0, n)),
+            rows,
+            rows,
+            pl.BlockSpec((depth // steps, width), lambda n: (n, 0)),
         ],
-        out_specs=pl.BlockSpec((4, ROWS, step), lambda n: (0, 0, n)),
-        scratch_shapes=[pltpu.VMEM((4 * ROWS, depth), jnp.bfloat16)],
+        out_specs=pl.BlockSpec((4, ROWS, width), lambda n: (0, 0, 0)),
+        scratch_shapes=[pltpu.VMEM((4 * ROWS, width), jnp.float32)],
         compiler_params=pltpu.CompilerParams(vmem_limit_bytes=56 * 1024 * 1024),
         cost_estimate=pl.CostEstimate(
             flops=8 * ROWS * depth * width, bytes_accessed=depth * width * 2, transcendentals=0

time: 164 us -> 131 us (0.80)
  Pallas kernels: 54.1 us -> 20.7 us
    pallas_call x1, Pallas kernels: 35.6 us -> 3.04 us  [trade(): pl.pallas_call(trade_kernel, out_shape=(jax.ShapeDtypeStruct((4, FT, HD),...]
  transfers between devices with their start and end apart: 10 -> 10, of which waited for: 5 -> 5; matrix products, arithmetic and copies ran while one was open for 2% -> 3% of each run, Pallas kernels for 7% -> 9%
where the time goes in v3:
time: 131 us; the launch traced here: 130 us
  blocking collectives  46.9 us (36%)
  starting transfers between devices  28.7 us (22%)
  Pallas kernels  20.7 us (16%)
  between operations  13.6 us (10%)
  waiting for transfers between devices  12.8 us (10%)
  local copies, waits for them, and re-layouts  5.32 us (4%)
  other arithmetic  2.13 us (2%)
    all_to_all x1, blocking collectives, shards(): lax.all_to_all(attended.reshape(FT // ROWS, 2 * ROWS, HD), 'head', 0, 0,...  31.1 us
    ppermute x9, starting transfers between devices, send(): return lax.ppermute(array, 'tm', pairs)  28.7 us
    all_to_all x1, blocking collectives, shards(): lax.all_to_all(parts, 'tm', 0, 0, tiled=True, axis_index_groups=quads)  15.8 us
    pallas_call x3, Pallas kernels, attend(): pl.pallas_call(functools.partial(attend_kernel, sources, split, len(kvs),...  12.1 us
    ppermute x9, waiting for transfers between devices, send(): return lax.ppermute(array, 'tm', pairs)  10.6 us
    pallas_call x1, Pallas kernels, project(): pl.pallas_call(project_kernel, grid=(steps,), out_shape=jax.ShapeDtypeStr...  4.89 us
    unnamed x11, local copies, waits for them, and re-layouts  3.75 us
    pallas_call x1, Pallas kernels, trade(): pl.pallas_call(trade_kernel, out_shape=(jax.ShapeDtypeStruct((4, FT, HD),...  3.04 us
  transfers between devices with their start and end apart: 10, of which 5 were waited for; matrix products, arithmetic and copies ran while one was open for 3% of the time, Pallas kernels for 9%

profile of v3, /device:TPU:1, one launch (start us, length us, event | category | flops | bytes accessed | tf_op | source)
XLA Modules:
  0.0 130.2 jit_solution(10909471527630980638)
XLA Ops:
  6.5 0.0 all-gather.2.cloned.1.call-start
  6.5 0.7 pad_add_fusion.1.place_ref
  7.2 3.0 %shard_map.55 = (bf16[4,512,128]{2,1,0:T(8,128)(2,1)}, bf16[2,512,128]{2,1,0:T(8,128)(2,1)}, bf16[3,512,128]{2,1,0:T(8,128)(2,1)}, bf16[128,1280]{1,0:T(8,128)(2,1)}) custom-call(s32[2]{0:T(128)} %pad_add_fusion.1.place_ref, bf16[512,256]{1,0:T(8,128)(2,1)} %refs_3_.1, bf16[512,256]{1,0:T(8,128)(2,1)} %refs_4_.1, bf16[512,256]{1,0:T(8,128)(2,1)} %refs_5_.1, ...), custom_call_target="tpu_custom_call" | custom-call | tf_op jit(solution)/shard_map/pallas_call | solution.py:157
  10.2 0.0 all-gather.2.cloned.1.call-update
  10.3 8.8 %collective-permute-start = (bf16[3,512,128]{2,1,0:T(8,128)(2,1)}, bf16[3,512,128]{2,1,0:T(8,128)(2,1)S(1)}, u32[]{:S(2)}, u32[]{:S(2)}) collective-permute-start(bf16[3,512,128]{2,1,0:T(8,128)(2,1)} %get-tuple-element.16), channel_id=1, source_target_pairs={{0,16},{16,0},{32,48},{48,32},{64,80},{80,64},{96,112},{112,96},{1... | collective-permute-start | bytes 1179656 | tf_op jit(solution)/shard_map/ppermute | solution.py:263
  19.1 1.5 %collective-permute-done = bf16[3,512,128]{2,1,0:T(8,128)(2,1)S(1)} collective-permute-done((bf16[3,512,128]{2,1,0:T(8,128)(2,1)}, bf16[3,512,128]{2,1,0:T(8,128)(2,1)S(1)}, u32[]{:S(2)}, u32[]{:S(2)}) %collective-permute-start) | collective-permute-done | bytes 393248 | tf_op jit(solution)/shard_map/ppermute | solution.py:263
  20.6 0.7 slice_dynamic-update-slice_fusion.refs_3_
  21.3 1.3 %collective-permute-start.1 = (bf16[4,512,128]{2,1,0:T(8,128)(2,1)}, bf16[4,512,128]{2,1,0:T(8,128)(2,1)S(1)}, u32[]{:S(2)}, u32[]{:S(2)}) collective-permute-start(bf16[4,512,128]{2,1,0:T(8,128)(2,1)} %slice_dynamic-update-slice_fusion.refs_3_), channel_id=1, source_target_pairs={{0,128},{16,144},{32,160},{48,176},{64,192},{80,208},{96,224},{112... | collective-permute-start | bytes 1572872 | tf_op jit(solution)/shard_map/ppermute | solution.py:263
  22.6 1.3 collective-permute-start.2
  23.9 1.9 %collective-permute-start.4 = (bf16[4,512,128]{2,1,0:T(8,128)(2,1)}, bf16[4,512,128]{2,1,0:T(8,128)(2,1)S(1)}, u32[]{:S(2)}, u32[]{:S(2)}) collective-permute-start(bf16[4,512,128]{2,1,0:T(8,128)(2,1)} %slice_dynamic-update-slice_fusion.refs_3_), channel_id=1, source_target_pairs={{0,64},{16,80},{32,96},{48,112},{64,0},{80,16},{96,32},{112,48},{1... | collective-permute-start | bytes 1572872 | tf_op jit(solution)/shard_map/ppermute | solution.py:263
  25.9 1.9 %collective-permute-start.6 = (bf16[4,512,128]{2,1,0:T(8,128)(2,1)}, bf16[4,512,128]{2,1,0:T(8,128)(2,1)S(1)}, u32[]{:S(2)}, u32[]{:S(2)}) collective-permute-start(bf16[4,512,128]{2,1,0:T(8,128)(2,1)} %slice_dynamic-update-slice_fusion.refs_3_), channel_id=1, source_target_pairs={{0,32},{16,48},{32,0},{48,16},{64,96},{80,112},{96,64},{112,80},{1... | collective-permute-start | bytes 1572872 | tf_op jit(solution)/shard_map/ppermute | solution.py:263
  27.8 5.2 %collective-permute-start.7 = (bf16[4,512,128]{2,1,0:T(8,128)(2,1)}, bf16[4,512,128]{2,1,0:T(8,128)(2,1)}, u32[]{:S(2)}, u32[]{:S(2)}) collective-permute-start(bf16[4,512,128]{2,1,0:T(8,128)(2,1)} %slice_dynamic-update-slice_fusion.refs_3_), channel_id=1, source_target_pairs={{0,256},{16,272},{32,288},{48,304},{64,320},{80,336},{96,352},{112... | collective-permute-start | bytes 1572872 | tf_op jit(solution)/shard_map/ppermute | solution.py:263
  33.1 1.1 collective-permute-done.1.refs_5_
  34.2 3.8 %collective-permute-done.2.refs_6_ = bf16[4,512,128]{2,1,0:T(8,128)(2,1)S(1)} collective-permute-done((bf16[4,512,128]{2,1,0:T(8,128)(2,1)}, bf16[4,512,128]{2,1,0:T(8,128)(2,1)S(1)}, u32[]{:S(2)}, u32[]{:S(2)}) %collective-permute-start.2) | collective-permute-done | bytes 524320 | tf_op jit(solution)/shard_map/ppermute | solution.py:263
  38.0 0.9 select_select_fusion
  38.9 1.9 %collective-permute-start.3 = (bf16[4,512,128]{2,1,0:T(8,128)(2,1)}, bf16[4,512,128]{2,1,0:T(8,128)(2,1)S(1)}, u32[]{:S(2)}, u32[]{:S(2)}) collective-permute-start(bf16[4,512,128]{2,1,0:T(8,128)(2,1)} %select_select_fusion), channel_id=1, source_target_pairs={{0,96},{16,112},{32,64},{48,80},{64,32},{80,48},{96,0},{112,16},{1... | collective-permute-start | bytes 1572872 | tf_op jit(solution)/shard_map/ppermute | solution.py:263
  40.8 0.0 collective-permute-done.4.refs_4_
  40.8 3.5 %collective-permute-start.5 = (bf16[4,512,128]{2,1,0:T(8,128)(2,1)S(1)}, bf16[4,512,128]{2,1,0:T(8,128)(2,1)S(1)}, u32[]{:S(2)}, u32[]{:S(2)}) collective-permute-start(bf16[4,512,128]{2,1,0:T(8,128)(2,1)S(1)} %collective-permute-done.4.refs_4_), channel_id=1, source_target_pairs={{0,128},{16,144},{32,160},{48,176},{128,256},{144,272},{160,288},{... | collective-permute-start | bytes 1572872 | tf_op jit(solution)/shard_map/ppermute | solution.py:263
  44.4 0.8 copy.7
  45.2 0.1 reshape.6.refs_1_
  45.3 0.1 stack.72.refs_0_
  45.4 0.7 slice_dynamic-update-slice_fusion.1.refs_2_
  46.1 0.0 copy-start
  46.1 1.0 copy-done
  47.1 0.0 copy-start.1
  47.1 1.0 copy-done.1
  48.1 3.0 %shard_map.56 = (f32[2,512,128]{2,1,0:T(8,128)S(1)}, f32[2,512,128]{2,1,0:T(8,128)S(1)}, f32[2,512,128]{2,1,0:T(8,128)S(1)}) custom-call(s32[7]{0:T(128)S(1)} %stack.72.refs_0_, s32[96]{0:T(128)S(1)} %reshape.6.refs_1_, bf16[2,512,128]{2,1,0:T(8,128)(2,1)S(1)} %copy-done.1, bf16[4,512,128]{2,1,0:T(8,128)(2,1)S(1)} %copy-done), custom_call_target="tpu_custom_call" | custom-call | flops 536870912 | bytes 524288 | tf_op jit(solution)/shard_map/pallas_call | solution.py:125
  51.1 0.0 collective-permute-done.6.refs_3_
  51.1 0.0 collective-permute-done.7.refs_7_
  51.1 0.0 copy-start.2
  51.1 0.9 copy-done.2
  52.1 5.9 %shard_map.57 = (f32[2,512,128]{2,1,0:T(8,128)S(1)}, f32[2,512,128]{2,1,0:T(8,128)S(1)}, f32[2,512,128]{2,1,0:T(8,128)S(1)}) custom-call(s32[7]{0:T(128)S(1)} %stack.72.refs_0_, s32[96]{0:T(128)S(1)} %reshape.6.refs_1_, bf16[2,512,128]{2,1,0:T(8,128)(2,1)S(1)} %copy-done.2, bf16[4,512,128]{2,1,0:T(8,128)(2,1)S(1)} %collective-permute-done.6.refs_3_, ...), custom_call_target="tpu_custom_call" | custom-call | flops 1476395008 | bytes 2621440 | tf_op jit(solution)/shard_map/pallas_call | solution.py:125
  57.9 0.0 collective-permute-done.3.refs_3_
  57.9 0.0 collective-permute-done.5.refs_4_
  57.9 3.2 %shard_map.58 = bf16[16,2,32,128]{3,2,1,0:T(8,128)(2,1)S(1)} custom-call(s32[7]{0:T(128)S(1)} %stack.72.refs_0_, s32[96]{0:T(128)S(1)} %reshape.6.refs_1_, bf16[2,512,128]{2,1,0:T(8,128)(2,1)S(1)} %copy-done.2, bf16[4,512,128]{2,1,0:T(8,128)(2,1)S(1)} %collective-permute-done.3.refs_3_, bf16[4,512,128]{2,1,0:T(8,128)(2,1)S(1)} %collective-permute-done.5.refs_4_, ...), custom_call_target="tpu_custom_call" | custom-call | flops 671088640 | bytes 1048576 | tf_op jit(solution)/shard_map/pallas_call | solution.py:125
  61.2 31.1 %all_to_all.10.own_ref = bf16[16,64,128]{2,1,0:T(8,128)(2,1)S(1)} all-to-all(bf16[16,64,128]{2,1,0:T(8,128)(2,1)S(1)} %bitcast.13), channel_id=1, replica_groups=mesh['tm'=32,'head'=16] {'head'}, dimensions={0} | all-to-all | bytes 524288 | tf_op jit(solution)/shard_map/all_to_all | solution.py:332
  92.3 0.0 copy-start.3
  92.3 2.8 %collective-permute-start.8 = (bf16[16,64,128]{2,1,0:T(8,128)(2,1)S(1)}, bf16[16,64,128]{2,1,0:T(8,128)(2,1)S(1)}, u32[]{:S(2)}, u32[]{:S(2)}) collective-permute-start(bf16[16,64,128]{2,1,0:T(8,128)(2,1)S(1)} %all_to_all.10.own_ref), channel_id=1, source_target_pairs={{0,32},{16,48},{32,0},{48,16},{64,96},{80,112},{96,64},{112,80},{1... | collective-permute-start | bytes 786440 | tf_op jit(solution)/shard_map/ppermute | solution.py:263
  95.1 0.6 pad_add_fusion.place_ref
  95.6 4.1 %collective-permute-done.8.other_ref = bf16[16,64,128]{2,1,0:T(8,128)(2,1)S(1)} collective-permute-done((bf16[16,64,128]{2,1,0:T(8,128)(2,1)S(1)}, bf16[16,64,128]{2,1,0:T(8,128)(2,1)S(1)}, u32[]{:S(2)}, u32[]{:S(2)}) %collective-permute-start.8) | collective-permute-done | bytes 262176 | tf_op jit(solution)/shard_map/ppermute | solution.py:263
  99.7 0.0 copy-start.4
  99.8 2.2 %all-gather.2.cloned.1.call-done.w_ref = bf16[2048,1280]{1,0:T(8,128)(2,1)} async-done(((bf16[128,1280]{1,0:T(8,128)(2,1)}), bf16[2048,1280]{1,0:T(8,128)(2,1)}) %all-gather.2.cloned.1.call-update) | async-done | bytes 5242896 | tf_op jit(solution)/shard_map/all_gather | solution.py:267
  101.9 0.0 copy-done.3
  101.9 0.0 copy-done.4
  101.9 4.9 %shard_map.59 = bf16[4,32,1280]{2,1,0:T(8,128)(2,1)} custom-call(s32[4]{0:T(128)} %pad_add_fusion.place_ref, bf16[16,64,128]{2,1,0:T(8,128)(2,1)} %copy-done.3, bf16[16,64,128]{2,1,0:T(8,128)(2,1)} %copy-done.4, bf16[2048,1280]{1,0:T(8,128)(2,1)} %all-gather.2.cloned.1.call-done.w_ref), custom_call_target="tpu_custom_call" | custom-call | flops 671088640 | bytes 5242880 | tf_op jit(solution)/shard_map/pallas_call | solution.py:211
  106.8 15.8 %all_to_all.11.in_ref = bf16[4,32,1280]{2,1,0:T(8,128)(2,1)S(1)} all-to-all(bf16[4,32,1280]{2,1,0:T(8,128)(2,1)} %shard_map.59), channel_id=1, replica_groups={{0,16,32,48},{64,80,96,112},{128,144,160,176},{192,208,224,240},{256,27..., dimensions={0} | all-to-all | bytes 655360 | tf_op jit(solution)/shard_map/all_to_all | solution.py:340
  122.6 0.7 shard_map.60
Async XLA Ops:
  6.5 95.4 %all-gather.2.cloned.1.call-start = ((), (), s32[]{:S(2)}) async-start(), calls=%async_computation.2 | async-start | bytes 5570560 | tf_op jit(solution)/shard_map/all_gather | solution.py:267
  10.3 10.3 %collective-permute-start = (bf16[3,512,128]{2,1,0:T(8,128)(2,1)}, bf16[3,512,128]{2,1,0:T(8,128)(2,1)S(1)}, u32[]{:S(2)}, u32[]{:S(2)}) collective-permute-start(bf16[3,512,128]{2,1,0:T(8,128)(2,1)} %get-tuple-element.16), channel_id=1, source_target_pairs={{0,16},{16,0},{32,48},{48,32},{64,80},{80,64},{96,112},{112,96},{1... | collective-permute-start | bytes 1179656 | tf_op jit(solution)/shard_map/ppermute | solution.py:263
  21.3 12.8 %collective-permute-start.1 = (bf16[4,512,128]{2,1,0:T(8,128)(2,1)}, bf16[4,512,128]{2,1,0:T(8,128)(2,1)S(1)}, u32[]{:S(2)}, u32[]{:S(2)}) collective-permute-start(bf16[4,512,128]{2,1,0:T(8,128)(2,1)} %slice_dynamic-update-slice_fusion.refs_3_), channel_id=1, source_target_pairs={{0,128},{16,144},{32,160},{48,176},{64,192},{80,208},{96,224},{112... | collective-permute-start | bytes 1572872 | tf_op jit(solution)/shard_map/ppermute | solution.py:263
  22.6 15.3 %collective-permute-start.2 = (bf16[4,512,128]{2,1,0:T(8,128)(2,1)}, bf16[4,512,128]{2,1,0:T(8,128)(2,1)S(1)}, u32[]{:S(2)}, u32[]{:S(2)}) collective-permute-start(bf16[4,512,128]{2,1,0:T(8,128)(2,1)} %slice_dynamic-update-slice_fusion.refs_3_), channel_id=1, source_target_pairs={{128,0},{144,16},{160,32},{176,48},{192,64},{208,80},{224,96},{240... | collective-permute-start | bytes 1572872 | tf_op jit(solution)/shard_map/ppermute | solution.py:263
  23.9 16.9 %collective-permute-start.4 = (bf16[4,512,128]{2,1,0:T(8,128)(2,1)}, bf16[4,512,128]{2,1,0:T(8,128)(2,1)S(1)}, u32[]{:S(2)}, u32[]{:S(2)}) collective-permute-start(bf16[4,512,128]{2,1,0:T(8,128)(2,1)} %slice_dynamic-update-slice_fusion.refs_3_), channel_id=1, source_target_pairs={{0,64},{16,80},{32,96},{48,112},{64,0},{80,16},{96,32},{112,48},{1... | collective-permute-start | bytes 1572872 | tf_op jit(solution)/shard_map/ppermute | solution.py:263
  25.9 25.2 %collective-permute-start.6 = (bf16[4,512,128]{2,1,0:T(8,128)(2,1)}, bf16[4,512,128]{2,1,0:T(8,128)(2,1)S(1)}, u32[]{:S(2)}, u32[]{:S(2)}) collective-permute-start(bf16[4,512,128]{2,1,0:T(8,128)(2,1)} %slice_dynamic-update-slice_fusion.refs_3_), channel_id=1, source_target_pairs={{0,32},{16,48},{32,0},{48,16},{64,96},{80,112},{96,64},{112,80},{1... | collective-permute-start | bytes 1572872 | tf_op jit(solution)/shard_map/ppermute | solution.py:263
  27.8 23.3 %collective-permute-start.7 = (bf16[4,512,128]{2,1,0:T(8,128)(2,1)}, bf16[4,512,128]{2,1,0:T(8,128)(2,1)}, u32[]{:S(2)}, u32[]{:S(2)}) collective-permute-start(bf16[4,512,128]{2,1,0:T(8,128)(2,1)} %slice_dynamic-update-slice_fusion.refs_3_), channel_id=1, source_target_pairs={{0,256},{16,272},{32,288},{48,304},{64,320},{80,336},{96,352},{112... | collective-permute-start | bytes 1572872 | tf_op jit(solution)/shard_map/ppermute | solution.py:263
  38.9 19.0 %collective-permute-start.3 = (bf16[4,512,128]{2,1,0:T(8,128)(2,1)}, bf16[4,512,128]{2,1,0:T(8,128)(2,1)S(1)}, u32[]{:S(2)}, u32[]{:S(2)}) collective-permute-start(bf16[4,512,128]{2,1,0:T(8,128)(2,1)} %select_select_fusion), channel_id=1, source_target_pairs={{0,96},{16,112},{32,64},{48,80},{64,32},{80,48},{96,0},{112,16},{1... | collective-permute-start | bytes 1572872 | tf_op jit(solution)/shard_map/ppermute | solution.py:263
  40.8 17.1 %collective-permute-start.5 = (bf16[4,512,128]{2,1,0:T(8,128)(2,1)S(1)}, bf16[4,512,128]{2,1,0:T(8,128)(2,1)S(1)}, u32[]{:S(2)}, u32[]{:S(2)}) collective-permute-start(bf16[4,512,128]{2,1,0:T(8,128)(2,1)S(1)} %collective-permute-done.4.refs_4_), channel_id=1, source_target_pairs={{0,128},{16,144},{32,160},{48,176},{128,256},{144,272},{160,288},{... | collective-permute-start | bytes 1572872 | tf_op jit(solution)/shard_map/ppermute | solution.py:263
  46.1 1.0 copy-start
  47.1 1.0 copy-start.1
  51.1 1.0 copy-start.2
  92.3 9.7 %copy-start.3 = (bf16[16,64,128]{2,1,0:T(8,128)(2,1)}, bf16[16,64,128]{2,1,0:T(8,128)(2,1)S(1)}, u32[]{:S(2)}) copy-start(bf16[16,64,128]{2,1,0:T(8,128)(2,1)S(1)} %all_to_all.10.own_ref) | copy-start | bytes 786436
  92.3 7.5 %collective-permute-start.8 = (bf16[16,64,128]{2,1,0:T(8,128)(2,1)S(1)}, bf16[16,64,128]{2,1,0:T(8,128)(2,1)S(1)}, u32[]{:S(2)}, u32[]{:S(2)}) collective-permute-start(bf16[16,64,128]{2,1,0:T(8,128)(2,1)S(1)} %all_to_all.10.own_ref), channel_id=1, source_target_pairs={{0,32},{16,48},{32,0},{48,16},{64,96},{80,112},{96,64},{112,80},{1... | collective-permute-start | bytes 786440 | tf_op jit(solution)/shard_map/ppermute | solution.py:263
  99.7 2.2 %copy-start.4 = (bf16[16,64,128]{2,1,0:T(8,128)(2,1)}, bf16[16,64,128]{2,1,0:T(8,128)(2,1)S(1)}, u32[]{:S(2)}) copy-start(bf16[16,64,128]{2,1,0:T(8,128)(2,1)S(1)} %collective-permute-done.8.other_ref) | copy-start | bytes 786436
Sparse Core Ops, SparseCore 0:
  10.4 91.4 all-gather.1

commit v4 on v3

--- a/solution.py
+++ b/solution.py
@@ -18,6 +18,8 @@
 HIDDEN = -1e30
 SCALE = math.log2(math.e) / math.sqrt(HD)
 VMEM = 40 * 1024 * 1024
+WIDE = 56 * 1024 * 1024
+QUARTER = DOUT // 4
 
 
 def attend_kernel(sources, split, n_kv, first, last, *refs):
@@ -137,107 +139,93 @@
     return out[0] if last else out
 
 
-def trade_kernel(place_ref, *refs):
-    k_mine, v_mine, q_mine, k_yours, v_yours, q_yours, w_block = refs[:7]
-    kv_out, q_out, give_out, w_out = refs[7:]
-    kv_out[0] = k_mine[...]
-    kv_out[1] = v_mine[...]
-    q_out[0] = q_mine[...]
-    give_out[0] = k_yours[...]
-    give_out[1] = v_yours[...]
-    give_out[2] = q_yours[...]
-    w_out[...] = w_block[...]
-
-
-def trade(place, queries, keys, values, out_weight):
-    kind = queries.dtype
-    half = DOUT // 2
-    mine = pl.BlockSpec((FT, HD), lambda n, place: (0, place[0]))
-    yours = pl.BlockSpec((FT, HD), lambda n, place: (0, 1 - place[0]))
+def pick_kernel(core_ref, *refs):
+    ins, outs = list(refs), []
+    while ins and len(ins[-1].shape) == 3:
+        outs.insert(0, ins.pop())
+    places = [(out, n) for out in outs for n in range(out.shape[0])]
+    for block, (out, n) in zip(ins, places):
+        out[n] = block[...]
+
+
+def pick(core, arrays, other, sizes):
+    maps = [
+        (lambda n, core: (0, 1 - core[0])) if other else (lambda n, core: (0, core[0]))
+        for _ in arrays
+    ]
     return pl.pallas_call(
-        trade_kernel,
-        out_shape=(
-            jax.ShapeDtypeStruct((4, FT, HD), kind),
-            jax.ShapeDtypeStruct((2, FT, HD), kind),
-            jax.ShapeDtypeStruct((3, FT, HD), kind),
-            jax.ShapeDtypeStruct((HD, half), kind),
+        pick_kernel,
+        out_shape=tuple(
+            jax.ShapeDtypeStruct((room, FT, HD), arrays[0].dtype) for _, room in sizes
         ),
         grid_spec=pltpu.PrefetchScalarGridSpec(
             num_scalar_prefetch=1,
             grid=(1,),
-            in_specs=[mine] * 3
-            + [yours] * 3
-            + [pl.BlockSpec((HD, half), lambda n, place: (place[0], place[1]))],
-            out_specs=(
-                pl.BlockSpec((2, FT, HD), lambda n, place: (0, 0, 0)),
-                pl.BlockSpec((1, FT, HD), lambda n, place: (0, 0, 0)),
-                pl.BlockSpec((3, FT, HD), lambda n, place: (0, 0, 0)),
-                pl.BlockSpec((HD, half), lambda n, place: (0, 0)),
+            in_specs=[pl.BlockSpec((FT, HD), index) for index in maps],
+            out_specs=tuple(
+                pl.BlockSpec((used, FT, HD), lambda n, core: (0, 0, 0)) for used, _ in sizes
             ),
         ),
-        compiler_params=pltpu.CompilerParams(vmem_limit_bytes=56 * 1024 * 1024),
-    )(place, keys, values, queries, keys, values, queries, out_weight)
-
-
-def project_kernel(place_ref, own_ref, other_ref, w_ref, out_ref, acc_ref):
-    step = pl.program_id(0)
+        compiler_params=pltpu.CompilerParams(vmem_limit_bytes=WIDE),
+    )(core, *arrays)
+
+
+def cut_kernel(place_ref, w_ref, out_ref):
+    out_ref[...] = w_ref[...]
+
+
+def cut(place, out_weight):
+    return pl.pallas_call(
+        cut_kernel,
+        out_shape=jax.ShapeDtypeStruct((HD, QUARTER), out_weight.dtype),
+        grid_spec=pltpu.PrefetchScalarGridSpec(
+            num_scalar_prefetch=1,
+            grid=(1,),
+            in_specs=[pl.BlockSpec((HD, QUARTER), lambda n, place: (place[0], place[1]))],
+            out_specs=pl.BlockSpec((HD, QUARTER), lambda n, place: (0, 0)),
+        ),
+        compiler_params=pltpu.CompilerParams(vmem_limit_bytes=WIDE),
+    )(place, out_weight)
+
+
+def project_kernel(place_ref, *refs):
+    row_refs, (w_ref, out_ref) = refs[:4], refs[4:]
     rows = [
-        jnp.concatenate([ref[z] for z in range(own_ref.shape[0])], axis=1)
-        for ref in (own_ref, other_ref)
+        jnp.concatenate([ref[z] for z in range(ref.shape[0])], axis=1) for ref in row_refs
     ]
     part = jnp.dot(
         jnp.concatenate(rows, axis=0), w_ref[...], preferred_element_type=jnp.float32
-    )
-
-    @pl.when(step == 0)
-    def _():
-        acc_ref[...] = part
-
-    @pl.when(step > 0)
-    def _():
-        acc_ref[...] += part
-
-    @pl.when(step == pl.num_programs(0) - 1)
-    def _():
-        for k in range(4):
-            out_ref[place_ref[k]] = acc_ref[k * ROWS : (k + 1) * ROWS].astype(jnp.bfloat16)
-
-
-def project(place, own, other, weight):
-    groups = own.shape[0]
+    ).astype(jnp.bfloat16)
+    for k in range(8):
+        out_ref[place_ref[k]] = part[k * ROWS : (k + 1) * ROWS]
+
+
+def project(place, rows, weight):
     depth, width = weight.shape
-    steps = 4
-    rows = pl.BlockSpec((groups // steps, 2 * ROWS, HD), lambda n: (n, 0, 0))
+    vmem = pl.BlockSpec(memory_space=pltpu.VMEM)
     return pl.pallas_call(
         project_kernel,
-        grid=(steps,),
-        out_shape=jax.ShapeDtypeStruct((4, ROWS, width), jnp.bfloat16),
-        in_specs=[
-            pl.BlockSpec(memory_space=pltpu.SMEM),
-            rows,
-            rows,
-            pl.BlockSpec((depth // steps, width), lambda n: (n, 0)),
-        ],
-        out_specs=pl.BlockSpec((4, ROWS, width), lambda n: (0, 0, 0)),
-        scratch_shapes=[pltpu.VMEM((4 * ROWS, width), jnp.float32)],
-        compiler_params=pltpu.CompilerParams(vmem_limit_bytes=56 * 1024 * 1024),
+        out_shape=jax.ShapeDtypeStruct((8, ROWS, width), jnp.bfloat16),
+        in_specs=[pl.BlockSpec(memory_space=pltpu.SMEM)] + [vmem] * 5,
+        out_specs=vmem,
+        compiler_params=pltpu.CompilerParams(vmem_limit_bytes=VMEM),
         cost_estimate=pl.CostEstimate(
-            flops=8 * ROWS * depth * width, bytes_accessed=depth * width * 2, transcendentals=0
-        ),
-    )(place, own, other, weight)
+            flops=16 * ROWS * depth * width, bytes_accessed=depth * width * 2, transcendentals=0
+        ),
+    )(place, *rows, weight)
 
 
 def add_kernel(in_ref, out_ref):
-    half = in_ref.shape[2]
-    for p in range(2):
+    width = in_ref.shape[2]
+    for p in range(in_ref.shape[0] // 2):
         both = in_ref[2 * p].astype(jnp.float32) + in_ref[2 * p + 1].astype(jnp.float32)
-        out_ref[:, p * half : (p + 1) * half] = both.astype(jnp.bfloat16)
+        out_ref[:, p * width : (p + 1) * width] = both.astype(jnp.bfloat16)
 
 
 def add_cores(parts):
     return pl.pallas_call(
         add_kernel,
-        out_shape=jax.ShapeDtypeStruct((ROWS, 2 * parts.shape[2]), jnp.bfloat16),
+        out_shape=jax.ShapeDtypeStruct((ROWS, parts.shape[0] // 2 * parts.shape[2]), parts.dtype),
         in_specs=[pl.BlockSpec(memory_space=pltpu.VMEM)],
         out_specs=pl.BlockSpec(memory_space=pltpu.VMEM),
         compiler_params=pltpu.CompilerParams(vmem_limit_bytes=VMEM),
@@ -246,44 +234,42 @@
 
 def shards(queries, keys, values, block_mask, out_weight):
     me = lax.axis_index("tm")
-    core = me % 2
-    y = (me // 2) % 4
-    x = me // 8
-    side = y % 2
+    core = me & 1
+    y = (me >> 1) & 3
+    x = me >> 3
 
     def chips(go):
         pairs = []
         for i in range(32):
             to = go(i // 8, (i // 2) % 4)
-            if to is not None:
+            if to is not None and 0 <= to[0] < 4:
                 pairs.append((i, to[0] * 8 + to[1] * 2 + i % 2))
         return pairs
 
     def send(array, pairs):
         return lax.ppermute(array, "tm", pairs)
 
-    place = jnp.stack([core, side]).astype(jnp.int32)
-    kv_own, q_own, give, weight = trade(place, queries, keys, values, out_weight)
+    at_core = core.reshape(1)
+    (give,) = pick(at_core, [keys, values, queries], True, [(3, 3)])
+    got = send(give, [(i, i ^ 1) for i in range(32)])
+    kv_own, q_own = pick(at_core, [keys, values, queries], False, [(2, 4), (1, 2)])
+    weight = cut(jnp.stack([core, y]), out_weight)
     weight = lax.all_gather(weight, "head", axis=0, tiled=True)
-    got = send(give, [(i, i ^ 1) for i in range(32)])
     local = lax.dynamic_update_slice(kv_own, got[:2], (2, 0, 0))
     q = lax.dynamic_update_slice(q_own, got[2:], (1, 0, 0))
 
-    above = send(local, chips(lambda x, y: (x + 1, y) if x < 3 else None))
+    def neighbour(x, y):
+        chip = 4 * x + y + (1 if y % 2 else -1)
+        return (chip // 4, chip % 4) if 0 <= chip < 16 else None
+
     across = send(local, chips(lambda x, y: (x, y ^ 2)))
-    below = send(local, chips(lambda x, y: (x - 1, y) if x > 0 else None))
+    above = send(local, chips(lambda x, y: (x + 1, y)))
+    below = send(local, chips(lambda x, y: (x - 1, y)))
     beside = send(local, chips(lambda x, y: (x, y ^ 1)))
     far = send(local, chips(lambda x, y: (x ^ 2, y)))
-    turned = jnp.where((y == 1) | (y == 2), local, jnp.where(y == 3, above, below))
-    other = send(turned, chips(lambda x, y: (x, 3 - y)))
-
-    def next_row(x, y):
-        to = x + 1 if y < 2 else x - 1
-        return (to, y) if 0 <= to < 4 else None
-
-    across_row = send(across, chips(next_row))
-
-    odd = y % 2
+    other = send(local, chips(neighbour))
+
+    odd = y & 1
     has_above, has_below = x > 0, x < 3
     row_end = jnp.where(y == 0, has_above, jnp.where(y == 3, has_below, True))
     row_cross = jnp.where(y < 2, has_above, has_below)
@@ -301,6 +287,10 @@
     mask = block_mask.reshape(-1)
 
     state = attend(info, mask, q, [local], [(0, False, 0, 2), (0, True, 1, 2)], None, None, False)
+
+    across, state = lax.optimization_barrier((across, state))
+    across_row = send(across, chips(lambda x, y: (x + 1 if y < 2 else x - 1, y)))
+
     state = attend(
         info,
         mask,
@@ -332,12 +322,12 @@
     rows = lax.all_to_all(
         attended.reshape(FT // ROWS, 2 * ROWS, HD), "head", 0, 0, tiled=True
     )
-    partner = send(rows, [(i, i ^ 2) for i in range(32)])
-    here = me % 4
-    place = jnp.stack([here, here ^ 1, here ^ 2, here ^ 3]).astype(jnp.int32)
-    parts = project(place, rows, partner, weight)
-    quads = [[4 * j + k for k in range(4)] for j in range(8)]
-    parts = lax.all_to_all(parts, "tm", 0, 0, tiled=True, axis_index_groups=quads)
+    rows = [rows] + [send(rows, [(i, i ^ (2 * k)) for i in range(32)]) for k in (1, 2, 3)]
+    here = me & 7
+    place = jnp.stack([here ^ k for k in range(8)])
+    parts = project(place, rows, weight)
+    rings = [[8 * j + k for k in range(8)] for j in range(4)]
+    parts = lax.all_to_all(parts, "tm", 0, 0, tiled=True, axis_index_groups=rings)
     return add_cores(parts)
 
 

time: 131 us -> 144 us (1.099)
  the two profiles are of different devices: /device:TPU:1 before, /device:TPU:34 now
where the time goes in v4:
time: 144 us; the launch traced here: 143 us
  blocking collectives  44.9 us (31%)
  starting transfers between devices  38.2 us (27%)
  waiting for transfers between devices  20.5 us (14%)
  Pallas kernels  20.2 us (14%)
  between operations  13.6 us (9%)
  local copies, waits for them, and re-layouts  5.43 us (4%)
    ppermute x11, starting transfers between devices, send(): return lax.ppermute(array, 'tm', pairs)  38.1 us
    all_to_all x1, blocking collectives, shards(): lax.all_to_all(attended.reshape(FT // ROWS, 2 * ROWS, HD), 'head', 0, 0,...  32.7 us
    ppermute x11, waiting for transfers between devices, send(): return lax.ppermute(array, 'tm', pairs)  20.4 us
    all_to_all x1, blocking collectives, shards(): lax.all_to_all(parts, 'tm', 0, 0, tiled=True, axis_index_groups=rings)  12.3 us
    pallas_call x3, Pallas kernels, attend(): pl.pallas_call(functools.partial(attend_kernel, sources, split, len(kvs),...  12.1 us
    unnamed x9, local copies, waits for them, and re-layouts  3.75 us
    pallas_call x2, Pallas kernels, pick(): pl.pallas_call(pick_kernel, out_shape=tuple((jax.ShapeDtypeStruct((room,...  3.64 us
  transfers between devices with their start and end apart: 12, of which 6 were waited for; matrix products, arithmetic and copies ran while one was open for 1% of the time, Pallas kernels for 11%

profile of v4, /device:TPU:34, one launch (start us, length us, event | category | flops | bytes accessed | tf_op | source)
XLA Modules:
  0.0 143.3 jit_solution(9890054622238399530)
XLA Ops:
  6.5 0.0 copy-start.3
  6.5 0.0 all-gather.2.cloned.1.call-start
  6.5 0.6 pad_add_fusion.place_ref
  7.1 2.3 %shard_map.60 = bf16[128,640]{1,0:T(8,128)(2,1)} custom-call(s32[2]{0:T(128)} %pad_add_fusion.place_ref, bf16[256,2560]{1,0:T(8,128)(2,1)} %w_ref.1), custom_call_target="tpu_custom_call" | custom-call | tf_op jit(solution)/shard_map/pallas_call | solution.py:178
  9.4 0.0 all-gather.2.cloned.1.call-update
  9.4 1.8 %shard_map.56 = bf16[3,512,128]{2,1,0:T(8,128)(2,1)} custom-call(s32[1]{0:T(128)} %bitcast.14.core_ref, bf16[512,256]{1,0:T(8,128)(2,1)} %refs_0_.3, bf16[512,256]{1,0:T(8,128)(2,1)} %refs_1_.3, bf16[512,256]{1,0:T(8,128)(2,1)} %refs_2_.3), custom_call_target="tpu_custom_call" | custom-call | tf_op jit(solution)/shard_map/pallas_call | solution.py:156
  11.2 1.9 %collective-permute-start = (bf16[3,512,128]{2,1,0:T(8,128)(2,1)}, bf16[3,512,128]{2,1,0:T(8,128)(2,1)S(1)}, u32[]{:S(2)}, u32[]{:S(2)}) collective-permute-start(bf16[3,512,128]{2,1,0:T(8,128)(2,1)} %shard_map.56), channel_id=1, source_target_pairs={{0,16},{16,0},{32,48},{48,32},{64,80},{80,64},{96,112},{112,96},{1... | collective-permute-start | bytes 1179656 | tf_op jit(solution)/shard_map/ppermute | solution.py:250
  13.2 1.8 %shard_map.55 = (bf16[4,512,128]{2,1,0:T(8,128)(2,1)}, bf16[2,512,128]{2,1,0:T(8,128)(2,1)}) custom-call(s32[1]{0:T(128)} %bitcast.14.core_ref, bf16[512,256]{1,0:T(8,128)(2,1)} %refs_0_.3, bf16[512,256]{1,0:T(8,128)(2,1)} %refs_1_.3, bf16[512,256]{1,0:T(8,128)(2,1)} %refs_2_.3), custom_call_target="tpu_custom_call" | custom-call | tf_op jit(solution)/shard_map/pallas_call | solution.py:156
  15.0 0.1 collective-permute-done
  15.1 0.7 slice_dynamic-update-slice_fusion.refs_3_
  15.8 5.1 %collective-permute-start.2 = (bf16[4,512,128]{2,1,0:T(8,128)(2,1)}, bf16[4,512,128]{2,1,0:T(8,128)(2,1)S(1)}, u32[]{:S(2)}, u32[]{:S(2)}) collective-permute-start(bf16[4,512,128]{2,1,0:T(8,128)(2,1)} %slice_dynamic-update-slice_fusion.refs_3_), channel_id=1, source_target_pairs={{0,64},{16,80},{32,96},{48,112},{64,0},{80,16},{96,32},{112,48},{1... | collective-permute-start | bytes 1572872 | tf_op jit(solution)/shard_map/ppermute | solution.py:250
  20.9 2.6 %collective-permute-start.4 = (bf16[4,512,128]{2,1,0:T(8,128)(2,1)}, bf16[4,512,128]{2,1,0:T(8,128)(2,1)S(1)}, u32[]{:S(2)}, u32[]{:S(2)}) collective-permute-start(bf16[4,512,128]{2,1,0:T(8,128)(2,1)} %slice_dynamic-update-slice_fusion.refs_3_), channel_id=1, source_target_pairs={{0,32},{16,48},{32,0},{48,16},{64,96},{80,112},{96,64},{112,80},{1... | collective-permute-start | bytes 1572872 | tf_op jit(solution)/shard_map/ppermute | solution.py:250
  23.5 0.0 copy-done.3
  23.5 0.1 copy.7
  23.6 0.1 reshape.9.refs_1_
  23.7 0.1 stack.86.refs_0_
  23.8 3.4 %collective-permute-start.5 = (bf16[4,512,128]{2,1,0:T(8,128)(2,1)}, bf16[4,512,128]{2,1,0:T(8,128)(2,1)S(1)}, u32[]{:S(2)}, u32[]{:S(2)}) collective-permute-start(bf16[4,512,128]{2,1,0:T(8,128)(2,1)} %slice_dynamic-update-slice_fusion.refs_3_), channel_id=1, source_target_pairs={{0,128},{16,144},{32,160},{48,176},{64,192},{80,208},{96,224},{112... | collective-permute-start | bytes 1572872 | tf_op jit(solution)/shard_map/ppermute | solution.py:250
  27.2 2.5 %collective-permute-start.6 = (bf16[4,512,128]{2,1,0:T(8,128)(2,1)}, bf16[4,512,128]{2,1,0:T(8,128)(2,1)S(1)}, u32[]{:S(2)}, u32[]{:S(2)}) collective-permute-start(bf16[4,512,128]{2,1,0:T(8,128)(2,1)} %slice_dynamic-update-slice_fusion.refs_3_), channel_id=1, source_target_pairs={{128,0},{144,16},{160,32},{176,48},{192,64},{208,80},{224,96},{240... | collective-permute-start | bytes 1572872 | tf_op jit(solution)/shard_map/ppermute | solution.py:250
  29.7 4.0 %collective-permute-start.7 = (bf16[4,512,128]{2,1,0:T(8,128)(2,1)}, bf16[4,512,128]{2,1,0:T(8,128)(2,1)S(1)}, u32[]{:S(2)}, u32[]{:S(2)}) collective-permute-start(bf16[4,512,128]{2,1,0:T(8,128)(2,1)} %slice_dynamic-update-slice_fusion.refs_3_), channel_id=1, source_target_pairs={{0,256},{16,272},{32,288},{48,304},{64,320},{80,336},{96,352},{112... | collective-permute-start | bytes 1572872 | tf_op jit(solution)/shard_map/ppermute | solution.py:250
  33.7 0.7 slice_dynamic-update-slice_fusion.1.refs_2_
  34.4 0.0 copy-start.1
  34.4 0.9 copy-done.1
  35.4 3.5 %shard_map.57 = (f32[2,512,128]{2,1,0:T(8,128)S(1)}, f32[2,512,128]{2,1,0:T(8,128)S(1)}, f32[2,512,128]{2,1,0:T(8,128)S(1)}) custom-call(s32[7]{0:T(128)S(1)} %stack.86.refs_0_, s32[96]{0:T(128)S(1)} %reshape.9.refs_1_, bf16[2,512,128]{2,1,0:T(8,128)(2,1)S(1)} %copy-done.1, bf16[4,512,128]{2,1,0:T(8,128)(2,1)} %slice_dynamic-update-slice_fusion.refs_3_), custom_call_target="tpu_custom_call" | custom-call | flops 536870912 | bytes 524288 | tf_op jit(solution)/shard_map/pallas_call | solution.py:127
  38.9 0.0 collective-permute-done.2.refs_4_
  38.9 3.1 %collective-permute-start.1 = (bf16[4,512,128]{2,1,0:T(8,128)(2,1)}, bf16[4,512,128]{2,1,0:T(8,128)(2,1)S(1)}, u32[]{:S(2)}, u32[]{:S(2)}) collective-permute-start(bf16[4,512,128]{2,1,0:T(8,128)(2,1)} %slice_dynamic-update-slice_fusion.refs_3_), channel_id=1, source_target_pairs={{32,64},{48,80},{64,32},{80,48},{96,128},{112,144},{128,96},{144,1... | collective-permute-start | bytes 1572872 | tf_op jit(solution)/shard_map/ppermute | solution.py:250
  42.1 3.2 %collective-permute-done.4.refs_3_ = bf16[4,512,128]{2,1,0:T(8,128)(2,1)S(1)} collective-permute-done((bf16[4,512,128]{2,1,0:T(8,128)(2,1)}, bf16[4,512,128]{2,1,0:T(8,128)(2,1)S(1)}, u32[]{:S(2)}, u32[]{:S(2)}) %collective-permute-start.4) | collective-permute-done | bytes 524320 | tf_op jit(solution)/shard_map/ppermute | solution.py:250
  45.2 3.4 %collective-permute-start.3 = (bf16[4,512,128]{2,1,0:T(8,128)(2,1)S(1)}, bf16[4,512,128]{2,1,0:T(8,128)(2,1)S(1)}, u32[]{:S(2)}, u32[]{:S(2)}) collective-permute-start(bf16[4,512,128]{2,1,0:T(8,128)(2,1)S(1)} %collective-permute-done.2.refs_4_), channel_id=1, source_target_pairs={{0,128},{16,144},{32,160},{48,176},{128,256},{144,272},{160,288},{... | collective-permute-start | bytes 1572872 | tf_op jit(solution)/shard_map/ppermute | solution.py:250
  48.6 0.0 collective-permute-done.5.refs_5_
  48.6 0.0 collective-permute-done.6.refs_6_
  48.6 7.5 %collective-permute-done.7.refs_7_ = bf16[4,512,128]{2,1,0:T(8,128)(2,1)S(1)} collective-permute-done((bf16[4,512,128]{2,1,0:T(8,128)(2,1)}, bf16[4,512,128]{2,1,0:T(8,128)(2,1)S(1)}, u32[]{:S(2)}, u32[]{:S(2)}) %collective-permute-start.7) | collective-permute-done | bytes 524320 | tf_op jit(solution)/shard_map/ppermute | solution.py:250
  56.1 0.0 copy-start.2
  56.1 0.9 copy-done.2
  57.0 5.3 %shard_map.58 = (f32[2,512,128]{2,1,0:T(8,128)S(1)}, f32[2,512,128]{2,1,0:T(8,128)S(1)}, f32[2,512,128]{2,1,0:T(8,128)S(1)}) custom-call(s32[7]{0:T(128)S(1)} %stack.86.refs_0_, s32[96]{0:T(128)S(1)} %reshape.9.refs_1_, bf16[2,512,128]{2,1,0:T(8,128)(2,1)S(1)} %copy-done.2, bf16[4,512,128]{2,1,0:T(8,128)(2,1)S(1)} %collective-permute-done.4.refs_3_, ...), custom_call_target="tpu_custom_call" | custom-call | flops 1476395008 | bytes 2621440 | tf_op jit(solution)/shard_map/pallas_call | solution.py:127
  62.4 1.0 collective-permute-done.1.refs_3_
  63.4 0.0 collective-permute-done.3.refs_4_
  63.4 3.2 %shard_map.59 = bf16[16,2,32,128]{3,2,1,0:T(8,128)(2,1)S(1)} custom-call(s32[7]{0:T(128)S(1)} %stack.86.refs_0_, s32[96]{0:T(128)S(1)} %reshape.9.refs_1_, bf16[2,512,128]{2,1,0:T(8,128)(2,1)S(1)} %copy-done.2, bf16[4,512,128]{2,1,0:T(8,128)(2,1)S(1)} %collective-permute-done.1.refs_3_, bf16[4,512,128]{2,1,0:T(8,128)(2,1)S(1)} %collective-permute-done.3.refs_4_, ...), custom_call_target="tpu_custom_call" | custom-call | flops 671088640 | bytes 1048576 | tf_op jit(solution)/shard_map/pallas_call | solution.py:127
  66.6 32.7 %all_to_all.10.refs_0_ = bf16[16,64,128]{2,1,0:T(8,128)(2,1)S(1)} all-to-all(bf16[16,64,128]{2,1,0:T(8,128)(2,1)S(1)} %bitcast.17), channel_id=1, replica_groups=mesh['tm'=32,'head'=16] {'head'}, dimensions={0} | all-to-all | bytes 524288 | tf_op jit(solution)/shard_map/all_to_all | solution.py:322
  99.3 6.8 %collective-permute-start.10 = (bf16[16,64,128]{2,1,0:T(8,128)(2,1)S(1)}, bf16[16,64,128]{2,1,0:T(8,128)(2,1)S(1)}, u32[]{:S(2)}, u32[]{:S(2)}) collective-permute-start(bf16[16,64,128]{2,1,0:T(8,128)(2,1)S(1)} %all_to_all.10.refs_0_), channel_id=1, source_target_pairs={{0,96},{16,112},{32,64},{48,80},{64,32},{80,48},{96,0},{112,16},{1... | collective-permute-start | bytes 786440 | tf_op jit(solution)/shard_map/ppermute | solution.py:250
  106.1 2.4 %collective-permute-start.8 = (bf16[16,64,128]{2,1,0:T(8,128)(2,1)S(1)}, bf16[16,64,128]{2,1,0:T(8,128)(2,1)S(1)}, u32[]{:S(2)}, u32[]{:S(2)}) collective-permute-start(bf16[16,64,128]{2,1,0:T(8,128)(2,1)S(1)} %all_to_all.10.refs_0_), channel_id=1, source_target_pairs={{0,32},{16,48},{32,0},{48,16},{64,96},{80,112},{96,64},{112,80},{1... | collective-permute-start | bytes 786440 | tf_op jit(solution)/shard_map/ppermute | solution.py:250
  108.6 2.9 %collective-permute-start.9 = (bf16[16,64,128]{2,1,0:T(8,128)(2,1)S(1)}, bf16[16,64,128]{2,1,0:T(8,128)(2,1)S(1)}, u32[]{:S(2)}, u32[]{:S(2)}) collective-permute-start(bf16[16,64,128]{2,1,0:T(8,128)(2,1)S(1)} %all_to_all.10.refs_0_), channel_id=1, source_target_pairs={{0,64},{16,80},{32,96},{48,112},{64,0},{80,16},{96,32},{112,48},{1... | collective-permute-start | bytes 786440 | tf_op jit(solution)/shard_map/ppermute | solution.py:250
  111.5 0.1 stack.75.place_ref
  111.5 0.0 collective-permute-done.10.refs_3_
  111.6 5.7 %collective-permute-done.8.refs_1_ = bf16[16,64,128]{2,1,0:T(8,128)(2,1)S(1)} collective-permute-done((bf16[16,64,128]{2,1,0:T(8,128)(2,1)S(1)}, bf16[16,64,128]{2,1,0:T(8,128)(2,1)S(1)}, u32[]{:S(2)}, u32[]{:S(2)}) %collective-permute-start.8) | collective-permute-done | bytes 262176 | tf_op jit(solution)/shard_map/ppermute | solution.py:250
  117.3 3.0 %collective-permute-done.9.refs_2_ = bf16[16,64,128]{2,1,0:T(8,128)(2,1)S(1)} collective-permute-done((bf16[16,64,128]{2,1,0:T(8,128)(2,1)S(1)}, bf16[16,64,128]{2,1,0:T(8,128)(2,1)S(1)}, u32[]{:S(2)}, u32[]{:S(2)}) %collective-permute-start.9) | collective-permute-done | bytes 262176 | tf_op jit(solution)/shard_map/ppermute | solution.py:250
  120.3 0.0 all-gather.2.cloned.1.call-done.refs_4_
  120.3 0.0 copy-start
  120.3 1.7 %copy-done = bf16[2048,640]{1,0:T(8,128)(2,1)S(1)} copy-done((bf16[2048,640]{1,0:T(8,128)(2,1)S(1)}, bf16[2048,640]{1,0:T(8,128)(2,1)}, u32[]{:S(2)}) %copy-start) | copy-done | bytes 2621464
  122.0 1.5 %shard_map.61 = bf16[8,32,640]{2,1,0:T(8,128)(2,1)S(1)} custom-call(s32[8]{0:T(128)S(1)} %stack.75.place_ref, bf16[16,64,128]{2,1,0:T(8,128)(2,1)S(1)} %all_to_all.10.refs_0_, bf16[16,64,128]{2,1,0:T(8,128)(2,1)S(1)} %collective-permute-done.8.refs_1_, bf16[16,64,128]{2,1,0:T(8,128)(2,1)S(1)} %collective-permute-done.9.refs_2_, ...), custom_call_target="tpu_custom_call" | custom-call | flops 671088640 | bytes 2621440 | tf_op jit(solution)/shard_map/pallas_call | solution.py:206
  123.5 12.3 %all_to_all.11.in_ref = bf16[8,32,640]{2,1,0:T(8,128)(2,1)S(1)} all-to-all(bf16[8,32,640]{2,1,0:T(8,128)(2,1)S(1)} %shard_map.61), channel_id=1, replica_groups={{0,16,32,48,64,80,96,112},{128,144,160,176,192,208,224,240},{256,272,28..., dimensions={0} | all-to-all | bytes 655360 | tf_op jit(solution)/shard_map/all_to_all | solution.py:330
  135.8 0.7 shard_map.62
Async XLA Ops:
  6.5 17.0 %copy-start.3 = (s32[6,4,4]{0,2,1:T(4,128)S(1)}, s32[6,4,4]{0,2,1:T(4,128)}, u32[]{:S(2)}) copy-start(s32[6,4,4]{0,2,1:T(4,128)} %param.8) | copy-start | bytes 1156
  6.5 113.7 %all-gather.2.cloned.1.call-start = ((), (), s32[]{:S(2)}) async-start(), calls=%async_computation.2 | async-start | bytes 2785280 | tf_op jit(solution)/shard_map/all_gather | solution.py:257
  11.2 3.8 %collective-permute-start = (bf16[3,512,128]{2,1,0:T(8,128)(2,1)}, bf16[3,512,128]{2,1,0:T(8,128)(2,1)S(1)}, u32[]{:S(2)}, u32[]{:S(2)}) collective-permute-start(bf16[3,512,128]{2,1,0:T(8,128)(2,1)} %shard_map.56), channel_id=1, source_target_pairs={{0,16},{16,0},{32,48},{48,32},{64,80},{80,64},{96,112},{112,96},{1... | collective-permute-start | bytes 1179656 | tf_op jit(solution)/shard_map/ppermute | solution.py:250
  15.8 23.1 %collective-permute-start.2 = (bf16[4,512,128]{2,1,0:T(8,128)(2,1)}, bf16[4,512,128]{2,1,0:T(8,128)(2,1)S(1)}, u32[]{:S(2)}, u32[]{:S(2)}) collective-permute-start(bf16[4,512,128]{2,1,0:T(8,128)(2,1)} %slice_dynamic-update-slice_fusion.refs_3_), channel_id=1, source_target_pairs={{0,64},{16,80},{32,96},{48,112},{64,0},{80,16},{96,32},{112,48},{1... | collective-permute-start | bytes 1572872 | tf_op jit(solution)/shard_map/ppermute | solution.py:250
  20.9 24.3 %collective-permute-start.4 = (bf16[4,512,128]{2,1,0:T(8,128)(2,1)}, bf16[4,512,128]{2,1,0:T(8,128)(2,1)S(1)}, u32[]{:S(2)}, u32[]{:S(2)}) collective-permute-start(bf16[4,512,128]{2,1,0:T(8,128)(2,1)} %slice_dynamic-update-slice_fusion.refs_3_), channel_id=1, source_target_pairs={{0,32},{16,48},{32,0},{48,16},{64,96},{80,112},{96,64},{112,80},{1... | collective-permute-start | bytes 1572872 | tf_op jit(solution)/shard_map/ppermute | solution.py:250
  23.8 24.8 %collective-permute-start.5 = (bf16[4,512,128]{2,1,0:T(8,128)(2,1)}, bf16[4,512,128]{2,1,0:T(8,128)(2,1)S(1)}, u32[]{:S(2)}, u32[]{:S(2)}) collective-permute-start(bf16[4,512,128]{2,1,0:T(8,128)(2,1)} %slice_dynamic-update-slice_fusion.refs_3_), channel_id=1, source_target_pairs={{0,128},{16,144},{32,160},{48,176},{64,192},{80,208},{96,224},{112... | collective-permute-start | bytes 1572872 | tf_op jit(solution)/shard_map/ppermute | solution.py:250
  27.2 21.4 %collective-permute-start.6 = (bf16[4,512,128]{2,1,0:T(8,128)(2,1)}, bf16[4,512,128]{2,1,0:T(8,128)(2,1)S(1)}, u32[]{:S(2)}, u32[]{:S(2)}) collective-permute-start(bf16[4,512,128]{2,1,0:T(8,128)(2,1)} %slice_dynamic-update-slice_fusion.refs_3_), channel_id=1, source_target_pairs={{128,0},{144,16},{160,32},{176,48},{192,64},{208,80},{224,96},{240... | collective-permute-start | bytes 1572872 | tf_op jit(solution)/shard_map/ppermute | solution.py:250
  29.7 26.4 %collective-permute-start.7 = (bf16[4,512,128]{2,1,0:T(8,128)(2,1)}, bf16[4,512,128]{2,1,0:T(8,128)(2,1)S(1)}, u32[]{:S(2)}, u32[]{:S(2)}) collective-permute-start(bf16[4,512,128]{2,1,0:T(8,128)(2,1)} %slice_dynamic-update-slice_fusion.refs_3_), channel_id=1, source_target_pairs={{0,256},{16,272},{32,288},{48,304},{64,320},{80,336},{96,352},{112... | collective-permute-start | bytes 1572872 | tf_op jit(solution)/shard_map/ppermute | solution.py:250
  34.4 0.9 copy-start.1
  38.9 24.5 %collective-permute-start.1 = (bf16[4,512,128]{2,1,0:T(8,128)(2,1)}, bf16[4,512,128]{2,1,0:T(8,128)(2,1)S(1)}, u32[]{:S(2)}, u32[]{:S(2)}) collective-permute-start(bf16[4,512,128]{2,1,0:T(8,128)(2,1)} %slice_dynamic-update-slice_fusion.refs_3_), channel_id=1, source_target_pairs={{32,64},{48,80},{64,32},{80,48},{96,128},{112,144},{128,96},{144,1... | collective-permute-start | bytes 1572872 | tf_op jit(solution)/shard_map/ppermute | solution.py:250
  45.2 18.2 %collective-permute-start.3 = (bf16[4,512,128]{2,1,0:T(8,128)(2,1)S(1)}, bf16[4,512,128]{2,1,0:T(8,128)(2,1)S(1)}, u32[]{:S(2)}, u32[]{:S(2)}) collective-permute-start(bf16[4,512,128]{2,1,0:T(8,128)(2,1)S(1)} %collective-permute-done.2.refs_4_), channel_id=1, source_target_pairs={{0,128},{16,144},{32,160},{48,176},{128,256},{144,272},{160,288},{... | collective-permute-start | bytes 1572872 | tf_op jit(solution)/shard_map/ppermute | solution.py:250
  56.1 1.0 copy-start.2
  99.3 12.3 %collective-permute-start.10 = (bf16[16,64,128]{2,1,0:T(8,128)(2,1)S(1)}, bf16[16,64,128]{2,1,0:T(8,128)(2,1)S(1)}, u32[]{:S(2)}, u32[]{:S(2)}) collective-permute-start(bf16[16,64,128]{2,1,0:T(8,128)(2,1)S(1)} %all_to_all.10.refs_0_), channel_id=1, source_target_pairs={{0,96},{16,112},{32,64},{48,80},{64,32},{80,48},{96,0},{112,16},{1... | collective-permute-start | bytes 786440 | tf_op jit(solution)/shard_map/ppermute | solution.py:250
  106.1 11.1 %collective-permute-start.8 = (bf16[16,64,128]{2,1,0:T(8,128)(2,1)S(1)}, bf16[16,64,128]{2,1,0:T(8,128)(2,1)S(1)}, u32[]{:S(2)}, u32[]{:S(2)}) collective-permute-start(bf16[16,64,128]{2,1,0:T(8,128)(2,1)S(1)} %all_to_all.10.refs_0_), channel_id=1, source_target_pairs={{0,32},{16,48},{32,0},{48,16},{64,96},{80,112},{96,64},{112,80},{1... | collective-permute-start | bytes 786440 | tf_op jit(solution)/shard_map/ppermute | solution.py:250
  108.6 11.7 %collective-permute-start.9 = (bf16[16,64,128]{2,1,0:T(8,128)(2,1)S(1)}, bf16[16,64,128]{2,1,0:T(8,128)(2,1)S(1)}, u32[]{:S(2)}, u32[]{:S(2)}) collective-permute-start(bf16[16,64,128]{2,1,0:T(8,128)(2,1)S(1)} %all_to_all.10.refs_0_), channel_id=1, source_target_pairs={{0,64},{16,80},{32,96},{48,112},{64,0},{80,16},{96,32},{112,48},{1... | collective-permute-start | bytes 786440 | tf_op jit(solution)/shard_map/ppermute | solution.py:250
  120.3 1.7 %copy-start = (bf16[2048,640]{1,0:T(8,128)(2,1)S(1)}, bf16[2048,640]{1,0:T(8,128)(2,1)}, u32[]{:S(2)}) copy-start(bf16[2048,640]{1,0:T(8,128)(2,1)} %all-gather.2.cloned.1.call-done.refs_4_) | copy-start | bytes 7864324
Sparse Core Ops, SparseCore 0:
  9.5 83.0 all-gather.1

commit v5 on v3

--- a/solution.py
+++ b/solution.py
@@ -18,6 +18,8 @@
 HIDDEN = -1e30
 SCALE = math.log2(math.e) / math.sqrt(HD)
 VMEM = 40 * 1024 * 1024
+WIDE = 56 * 1024 * 1024
+NARROW = 24 * 1024 * 1024
 
 
 def attend_kernel(sources, split, n_kv, first, last, *refs):
@@ -137,119 +139,117 @@
     return out[0] if last else out
 
 
-def trade_kernel(place_ref, *refs):
-    k_mine, v_mine, q_mine, k_yours, v_yours, q_yours, w_block = refs[:7]
-    kv_out, q_out, give_out, w_out = refs[7:]
-    kv_out[0] = k_mine[...]
-    kv_out[1] = v_mine[...]
-    q_out[0] = q_mine[...]
-    give_out[0] = k_yours[...]
-    give_out[1] = v_yours[...]
-    give_out[2] = q_yours[...]
-    w_out[...] = w_block[...]
-
-
-def trade(place, queries, keys, values, out_weight):
+def give_kernel(core_ref, side_ref, k_ref, v_ref, q_ref, w_ref, give_out, w_out):
+    give_out[0] = k_ref[...]
+    give_out[1] = v_ref[...]
+    give_out[2] = q_ref[...]
+    w_out[...] = w_ref[...]
+
+
+def keep_kernel(core_ref, k_ref, v_ref, q_ref, kv_out, q_out):
+    kv_out[0] = k_ref[...]
+    kv_out[1] = v_ref[...]
+    q_out[0] = q_ref[...]
+
+
+def give(core, side, queries, keys, values, out_weight):
     kind = queries.dtype
     half = DOUT // 2
-    mine = pl.BlockSpec((FT, HD), lambda n, place: (0, place[0]))
-    yours = pl.BlockSpec((FT, HD), lambda n, place: (0, 1 - place[0]))
+    yours = pl.BlockSpec((FT, HD), lambda n, core, side: (0, 1 - core[0]))
     return pl.pallas_call(
-        trade_kernel,
+        give_kernel,
+        out_shape=(
+            jax.ShapeDtypeStruct((3, FT, HD), kind),
+            jax.ShapeDtypeStruct((HD, half), kind),
+        ),
+        grid_spec=pltpu.PrefetchScalarGridSpec(
+            num_scalar_prefetch=2,
+            grid=(1,),
+            in_specs=[yours] * 3
+            + [pl.BlockSpec((HD, half), lambda n, core, side: (core[0], side[0]))],
+            out_specs=(
+                pl.BlockSpec((3, FT, HD), lambda n, core, side: (0, 0, 0)),
+                pl.BlockSpec((HD, half), lambda n, core, side: (0, 0)),
+            ),
+        ),
+        compiler_params=pltpu.CompilerParams(vmem_limit_bytes=WIDE),
+    )(core, side, keys, values, queries, out_weight)
+
+
+def keep(core, queries, keys, values):
+    kind = queries.dtype
+    mine = pl.BlockSpec((FT, HD), lambda n, core: (0, core[0]))
+    return pl.pallas_call(
+        keep_kernel,
         out_shape=(
             jax.ShapeDtypeStruct((4, FT, HD), kind),
             jax.ShapeDtypeStruct((2, FT, HD), kind),
-            jax.ShapeDtypeStruct((3, FT, HD), kind),
-            jax.ShapeDtypeStruct((HD, half), kind),
         ),
         grid_spec=pltpu.PrefetchScalarGridSpec(
             num_scalar_prefetch=1,
             grid=(1,),
-            in_specs=[mine] * 3
-            + [yours] * 3
-            + [pl.BlockSpec((HD, half), lambda n, place: (place[0], place[1]))],
+            in_specs=[mine] * 3,
             out_specs=(
-                pl.BlockSpec((2, FT, HD), lambda n, place: (0, 0, 0)),
-                pl.BlockSpec((1, FT, HD), lambda n, place: (0, 0, 0)),
-                pl.BlockSpec((3, FT, HD), lambda n, place: (0, 0, 0)),
-                pl.BlockSpec((HD, half), lambda n, place: (0, 0)),
+                pl.BlockSpec((2, FT, HD), lambda n, core: (0, 0, 0)),
+                pl.BlockSpec((1, FT, HD), lambda n, core: (0, 0, 0)),
             ),
         ),
-        compiler_params=pltpu.CompilerParams(vmem_limit_bytes=56 * 1024 * 1024),
-    )(place, keys, values, queries, keys, values, queries, out_weight)
-
-
-def project_kernel(place_ref, own_ref, other_ref, w_ref, out_ref, acc_ref):
-    step = pl.program_id(0)
-    rows = [
-        jnp.concatenate([ref[z] for z in range(own_ref.shape[0])], axis=1)
-        for ref in (own_ref, other_ref)
-    ]
-    part = jnp.dot(
-        jnp.concatenate(rows, axis=0), w_ref[...], preferred_element_type=jnp.float32
-    )
-
-    @pl.when(step == 0)
-    def _():
-        acc_ref[...] = part
-
-    @pl.when(step > 0)
-    def _():
-        acc_ref[...] += part
-
-    @pl.when(step == pl.num_programs(0) - 1)
-    def _():
-        for k in range(4):
-            out_ref[place_ref[k]] = acc_ref[k * ROWS : (k + 1) * ROWS].astype(jnp.bfloat16)
-
-
-def project(place, own, other, weight):
-    groups = own.shape[0]
+        compiler_params=pltpu.CompilerParams(vmem_limit_bytes=WIDE),
+    )(core, keys, values, queries)
+
+
+def product_kernel(rows_ref, w_ref, mine_ref, yours_ref):
+    rows = jnp.concatenate([rows_ref[z] for z in range(rows_ref.shape[0])], axis=1)
+    part = jnp.dot(rows, w_ref[...], preferred_element_type=jnp.float32).astype(jnp.bfloat16)
+    mine_ref[...] = part[:ROWS]
+    yours_ref[...] = part[ROWS:]
+
+
+def product(rows, weight):
     depth, width = weight.shape
-    steps = 4
-    rows = pl.BlockSpec((groups // steps, 2 * ROWS, HD), lambda n: (n, 0, 0))
+    vmem = pl.BlockSpec(memory_space=pltpu.VMEM)
+    part = jax.ShapeDtypeStruct((ROWS, width), rows.dtype)
     return pl.pallas_call(
-        project_kernel,
-        grid=(steps,),
-        out_shape=jax.ShapeDtypeStruct((4, ROWS, width), jnp.bfloat16),
-        in_specs=[
-            pl.BlockSpec(memory_space=pltpu.SMEM),
-            rows,
-            rows,
-            pl.BlockSpec((depth // steps, width), lambda n: (n, 0)),
-        ],
-        out_specs=pl.BlockSpec((4, ROWS, width), lambda n: (0, 0, 0)),
-        scratch_shapes=[pltpu.VMEM((4 * ROWS, width), jnp.float32)],
-        compiler_params=pltpu.CompilerParams(vmem_limit_bytes=56 * 1024 * 1024),
+        product_kernel,
+        out_shape=(part, part),
+        in_specs=[vmem, vmem],
+        out_specs=(vmem, vmem),
+        compiler_params=pltpu.CompilerParams(vmem_limit_bytes=NARROW),
         cost_estimate=pl.CostEstimate(
-            flops=8 * ROWS * depth * width, bytes_accessed=depth * width * 2, transcendentals=0
-        ),
-    )(place, own, other, weight)
-
-
-def add_kernel(in_ref, out_ref):
-    half = in_ref.shape[2]
-    for p in range(2):
-        both = in_ref[2 * p].astype(jnp.float32) + in_ref[2 * p + 1].astype(jnp.float32)
-        out_ref[:, p * half : (p + 1) * half] = both.astype(jnp.bfloat16)
-
-
-def add_cores(parts):
+            flops=4 * ROWS * depth * width, bytes_accessed=depth * width * 2, transcendentals=0
+        ),
+    )(rows, weight)
+
+
+def add_kernel(side_ref, own_ref, got_ref, far_ref, far_other_ref, out_ref):
+    width = own_ref.shape[1]
+    side = side_ref[0]
+
+    def add(place, left, right):
+        both = left[...].astype(jnp.float32) + right[...].astype(jnp.float32)
+        columns = pl.ds(pl.multiple_of(place * width, HD), width)
+        out_ref[:, columns] = both.astype(jnp.bfloat16)
+
+    add(side, own_ref, got_ref)
+    add(1 - side, far_ref, far_other_ref)
+
+
+def add_cores(side, own, got, far, far_other):
+    vmem = pl.BlockSpec(memory_space=pltpu.VMEM)
     return pl.pallas_call(
         add_kernel,
-        out_shape=jax.ShapeDtypeStruct((ROWS, 2 * parts.shape[2]), jnp.bfloat16),
-        in_specs=[pl.BlockSpec(memory_space=pltpu.VMEM)],
-        out_specs=pl.BlockSpec(memory_space=pltpu.VMEM),
-        compiler_params=pltpu.CompilerParams(vmem_limit_bytes=VMEM),
-    )(parts)
+        out_shape=jax.ShapeDtypeStruct((ROWS, 2 * own.shape[1]), own.dtype),
+        in_specs=[pl.BlockSpec(memory_space=pltpu.SMEM)] + [vmem] * 4,
+        out_specs=vmem,
+        compiler_params=pltpu.CompilerParams(vmem_limit_bytes=NARROW),
+    )(side, own, got, far, far_other)
 
 
 def shards(queries, keys, values, block_mask, out_weight):
     me = lax.axis_index("tm")
-    core = me % 2
-    y = (me // 2) % 4
-    x = me // 8
-    side = y % 2
+    core = me & 1
+    y = (me >> 1) & 3
+    x = me >> 3
 
     def chips(go):
         pairs = []
@@ -262,10 +262,13 @@
     def send(array, pairs):
         return lax.ppermute(array, "tm", pairs)
 
-    place = jnp.stack([core, side]).astype(jnp.int32)
-    kv_own, q_own, give, weight = trade(place, queries, keys, values, out_weight)
+    at_core, at_side = core.reshape(1), (y & 1).reshape(1)
+    given, weight = give(at_core, at_side, queries, keys, values, out_weight)
     weight = lax.all_gather(weight, "head", axis=0, tiled=True)
-    got = send(give, [(i, i ^ 1) for i in range(32)])
+    swap = [(i, i ^ 1) for i in range(32)]
+    got = send(given, swap)
+    at_core, _ = lax.optimization_barrier((at_core, given))
+    kv_own, q_own = keep(at_core, queries, keys, values)
     local = lax.dynamic_update_slice(kv_own, got[:2], (2, 0, 0))
     q = lax.dynamic_update_slice(q_own, got[2:], (1, 0, 0))
 
@@ -283,7 +286,7 @@
 
     across_row = send(across, chips(next_row))
 
-    odd = y % 2
+    odd = y & 1
     has_above, has_below = x > 0, x < 3
     row_end = jnp.where(y == 0, has_above, jnp.where(y == 3, has_below, True))
     row_cross = jnp.where(y < 2, has_above, has_below)
@@ -332,13 +335,14 @@
     rows = lax.all_to_all(
         attended.reshape(FT // ROWS, 2 * ROWS, HD), "head", 0, 0, tiled=True
     )
-    partner = send(rows, [(i, i ^ 2) for i in range(32)])
-    here = me % 4
-    place = jnp.stack([here, here ^ 1, here ^ 2, here ^ 3]).astype(jnp.int32)
-    parts = project(place, rows, partner, weight)
-    quads = [[4 * j + k for k in range(4)] for j in range(8)]
-    parts = lax.all_to_all(parts, "tm", 0, 0, tiled=True, axis_index_groups=quads)
-    return add_cores(parts)
+    pair = [(i, i ^ 2) for i in range(32)]
+    partner = send(rows, pair)
+    own, yours = product(rows, weight)
+    got = send(yours, swap)
+    far, far_yours = product(partner, weight)
+    far = send(far, pair)
+    far_other = send(far_yours, [(i, i ^ 3) for i in range(32)])
+    return add_cores(at_side, own, got, far, far_other)
 
 
 def solution(mesh):

time: 131 us -> 129 us (0.985)
  blocking collectives: 46.9 us -> 30.7 us
  starting transfers between devices: 28.7 us -> 43.5 us
  local copies, waits for them, and re-layouts: 5.32 us -> 7.79 us
  Pallas kernels: 20.7 us -> 18.7 us
    all_to_all x1 -> x0, blocking collectives: 15.8 us -> none  [shards(): lax.all_to_all(parts, 'tm', 0, 0, tiled=True, axis_index_groups=quads)]
    ppermute x9 -> x12, starting transfers between devices: 28.7 us -> 43.5 us  [send(): return lax.ppermute(array, 'tm', pairs)]
    unnamed x11, local copies, waits for them, and re-layouts: 3.75 us -> 6.23 us
    pallas_call x3 -> x5, Pallas kernels: 8.64 us -> 6.64 us  [the longest x1 2.08 us: give(): pl.pallas_call(give_kernel, out_shape=(jax.ShapeDtypeStruct((3, FT, HD),...]
    ppermute x9 -> x12, waiting for transfers between devices: 10.6 us -> 10.7 us  [send(): return lax.ppermute(array, 'tm', pairs)]
  transfers between devices with their start and end apart: 10 -> 13, of which waited for: 5 -> 5; matrix products, arithmetic and copies ran while one was open for 3% -> 3% of each run, Pallas kernels for 9% -> 12%
where the time goes in v5:
time: 129 us; the launch traced here: 128 us
  starting transfers between devices  43.5 us (34%)
  blocking collectives  30.7 us (24%)
  Pallas kernels  18.7 us (14%)
  between operations  13.6 us (11%)
  waiting for transfers between devices  13.1 us (10%)
  local copies, waits for them, and re-layouts  7.79 us (6%)
    ppermute x12, starting transfers between devices, send(): return lax.ppermute(array, 'tm', pairs)  43.5 us
    all_to_all x1, blocking collectives, shards(): lax.all_to_all(attended.reshape(FT // ROWS, 2 * ROWS, HD), 'head', 0, 0,...  30.7 us
    pallas_call x3, Pallas kernels, attend(): pl.pallas_call(functools.partial(attend_kernel, sources, split, len(kvs),...  12.1 us
    ppermute x12, waiting for transfers between devices, send(): return lax.ppermute(array, 'tm', pairs)  10.7 us
    unnamed x11, local copies, waits for them, and re-layouts  6.23 us
  transfers between devices with their start and end apart: 13, of which 5 were waited for; matrix products, arithmetic and copies ran while one was open for 3% of the time, Pallas kernels for 12%

profile of v5, /device:TPU:1, one launch (start us, length us, event | category | flops | bytes accessed | tf_op | source)
XLA Modules:
  0.0 128.2 jit_solution(13632039253928364412)
XLA Ops:
  6.5 0.0 all-gather.2.cloned.1.call-start
  6.5 2.1 %shard_map.55 = (bf16[3,512,128]{2,1,0:T(8,128)(2,1)}, bf16[128,1280]{1,0:T(8,128)(2,1)}) custom-call(s32[1]{0:T(128)} %bitcast.7.core_ref, s32[1]{0:T(128)} %bitcast.side_ref, bf16[512,256]{1,0:T(8,128)(2,1)} %k_ref.3, bf16[512,256]{1,0:T(8,128)(2,1)} %v_ref.3, bf16[512,256]{1,0:T(8,128)(2,1)} %q_ref.3, bf16[256,2560]{1,0:T(8,128)(2,1)} %w_ref.1), custom_call_target="tpu_custom_call" | custom-call | tf_op jit(solution)/shard_map/pallas_call | solution.py:159
  8.6 0.0 all-gather.2.cloned.1.call-update
  8.6 8.8 %collective-permute-start = (bf16[3,512,128]{2,1,0:T(8,128)(2,1)}, bf16[3,512,128]{2,1,0:T(8,128)(2,1)S(1)}, u32[]{:S(2)}, u32[]{:S(2)}) collective-permute-start(bf16[3,512,128]{2,1,0:T(8,128)(2,1)} %get-tuple-element.20), channel_id=1, source_target_pairs={{0,16},{16,0},{32,48},{48,32},{64,80},{80,64},{96,112},{112,96},{1... | collective-permute-start | bytes 1179656 | tf_op jit(solution)/shard_map/ppermute | solution.py:263
  17.4 1.8 %shard_map.56 = (bf16[4,512,128]{2,1,0:T(8,128)(2,1)}, bf16[2,512,128]{2,1,0:T(8,128)(2,1)}) custom-call(s32[1]{0:T(128)} %bitcast.7.core_ref, bf16[512,256]{1,0:T(8,128)(2,1)} %k_ref.3, bf16[512,256]{1,0:T(8,128)(2,1)} %v_ref.3, bf16[512,256]{1,0:T(8,128)(2,1)} %q_ref.3), custom_call_target="tpu_custom_call" | custom-call | tf_op jit(solution)/shard_map/pallas_call | solution.py:182
  19.3 0.0 collective-permute-done
  19.3 0.7 slice_dynamic-update-slice_fusion.refs_3_
  20.0 1.3 %collective-permute-start.1 = (bf16[4,512,128]{2,1,0:T(8,128)(2,1)}, bf16[4,512,128]{2,1,0:T(8,128)(2,1)S(1)}, u32[]{:S(2)}, u32[]{:S(2)}) collective-permute-start(bf16[4,512,128]{2,1,0:T(8,128)(2,1)} %slice_dynamic-update-slice_fusion.refs_3_), channel_id=1, source_target_pairs={{0,128},{16,144},{32,160},{48,176},{64,192},{80,208},{96,224},{112... | collective-permute-start | bytes 1572872 | tf_op jit(solution)/shard_map/ppermute | solution.py:263
  21.3 1.3 %collective-permute-start.2 = (bf16[4,512,128]{2,1,0:T(8,128)(2,1)}, bf16[4,512,128]{2,1,0:T(8,128)(2,1)S(1)}, u32[]{:S(2)}, u32[]{:S(2)}) collective-permute-start(bf16[4,512,128]{2,1,0:T(8,128)(2,1)} %slice_dynamic-update-slice_fusion.refs_3_), channel_id=1, source_target_pairs={{128,0},{144,16},{160,32},{176,48},{192,64},{208,80},{224,96},{240... | collective-permute-start | bytes 1572872 | tf_op jit(solution)/shard_map/ppermute | solution.py:263
  22.6 1.9 %collective-permute-start.4 = (bf16[4,512,128]{2,1,0:T(8,128)(2,1)}, bf16[4,512,128]{2,1,0:T(8,128)(2,1)S(1)}, u32[]{:S(2)}, u32[]{:S(2)}) collective-permute-start(bf16[4,512,128]{2,1,0:T(8,128)(2,1)} %slice_dynamic-update-slice_fusion.refs_3_), channel_id=1, source_target_pairs={{0,64},{16,80},{32,96},{48,112},{64,0},{80,16},{96,32},{112,48},{1... | collective-permute-start | bytes 1572872 | tf_op jit(solution)/shard_map/ppermute | solution.py:263
  24.5 1.9 %collective-permute-start.6 = (bf16[4,512,128]{2,1,0:T(8,128)(2,1)}, bf16[4,512,128]{2,1,0:T(8,128)(2,1)S(1)}, u32[]{:S(2)}, u32[]{:S(2)}) collective-permute-start(bf16[4,512,128]{2,1,0:T(8,128)(2,1)} %slice_dynamic-update-slice_fusion.refs_3_), channel_id=1, source_target_pairs={{0,32},{16,48},{32,0},{48,16},{64,96},{80,112},{96,64},{112,80},{1... | collective-permute-start | bytes 1572872 | tf_op jit(solution)/shard_map/ppermute | solution.py:263
  26.5 5.2 %collective-permute-start.7 = (bf16[4,512,128]{2,1,0:T(8,128)(2,1)}, bf16[4,512,128]{2,1,0:T(8,128)(2,1)}, u32[]{:S(2)}, u32[]{:S(2)}) collective-permute-start(bf16[4,512,128]{2,1,0:T(8,128)(2,1)} %slice_dynamic-update-slice_fusion.refs_3_), channel_id=1, source_target_pairs={{0,256},{16,272},{32,288},{48,304},{64,320},{80,336},{96,352},{112... | collective-permute-start | bytes 1572872 | tf_op jit(solution)/shard_map/ppermute | solution.py:263
  31.7 1.3 %collective-permute-done.1.refs_5_ = bf16[4,512,128]{2,1,0:T(8,128)(2,1)S(1)} collective-permute-done((bf16[4,512,128]{2,1,0:T(8,128)(2,1)}, bf16[4,512,128]{2,1,0:T(8,128)(2,1)S(1)}, u32[]{:S(2)}, u32[]{:S(2)}) %collective-permute-start.1) | collective-permute-done | bytes 524320 | tf_op jit(solution)/shard_map/ppermute | solution.py:263
  33.0 4.0 %collective-permute-done.2.refs_6_ = bf16[4,512,128]{2,1,0:T(8,128)(2,1)S(1)} collective-permute-done((bf16[4,512,128]{2,1,0:T(8,128)(2,1)}, bf16[4,512,128]{2,1,0:T(8,128)(2,1)S(1)}, u32[]{:S(2)}, u32[]{:S(2)}) %collective-permute-start.2) | collective-permute-done | bytes 524320 | tf_op jit(solution)/shard_map/ppermute | solution.py:263
  37.0 0.9 select_select_fusion
  37.9 1.9 %collective-permute-start.3 = (bf16[4,512,128]{2,1,0:T(8,128)(2,1)}, bf16[4,512,128]{2,1,0:T(8,128)(2,1)S(1)}, u32[]{:S(2)}, u32[]{:S(2)}) collective-permute-start(bf16[4,512,128]{2,1,0:T(8,128)(2,1)} %select_select_fusion), channel_id=1, source_target_pairs={{0,96},{16,112},{32,64},{48,80},{64,32},{80,48},{96,0},{112,16},{1... | collective-permute-start | bytes 1572872 | tf_op jit(solution)/shard_map/ppermute | solution.py:263
  39.8 0.0 collective-permute-done.4.refs_4_
  39.8 3.6 %collective-permute-start.5 = (bf16[4,512,128]{2,1,0:T(8,128)(2,1)S(1)}, bf16[4,512,128]{2,1,0:T(8,128)(2,1)S(1)}, u32[]{:S(2)}, u32[]{:S(2)}) collective-permute-start(bf16[4,512,128]{2,1,0:T(8,128)(2,1)S(1)} %collective-permute-done.4.refs_4_), channel_id=1, source_target_pairs={{0,128},{16,144},{32,160},{48,176},{128,256},{144,272},{160,288},{... | collective-permute-start | bytes 1572872 | tf_op jit(solution)/shard_map/ppermute | solution.py:263
  43.4 0.8 copy.7
  44.2 0.1 reshape.13.refs_1_
  44.3 0.1 stack.43.refs_0_
  44.4 0.6 slice_dynamic-update-slice_fusion.1.refs_2_
  45.1 0.0 copy-start.2
  45.1 1.0 copy-done.2
  46.1 0.0 copy-start.3
  46.1 0.9 copy-done.3
  47.1 3.0 %shard_map.57 = (f32[2,512,128]{2,1,0:T(8,128)S(1)}, f32[2,512,128]{2,1,0:T(8,128)S(1)}, f32[2,512,128]{2,1,0:T(8,128)S(1)}) custom-call(s32[7]{0:T(128)S(1)} %stack.43.refs_0_, s32[96]{0:T(128)S(1)} %reshape.13.refs_1_, bf16[2,512,128]{2,1,0:T(8,128)(2,1)S(1)} %copy-done.3, bf16[4,512,128]{2,1,0:T(8,128)(2,1)S(1)} %copy-done.2), custom_call_target="tpu_custom_call" | custom-call | flops 536870912 | bytes 524288 | tf_op jit(solution)/shard_map/pallas_call | solution.py:127
  50.1 0.0 collective-permute-done.6.refs_3_
  50.1 0.0 collective-permute-done.7.refs_7_
  50.1 0.0 copy-start.4
  50.1 0.9 copy-done.4
  51.1 5.9 %shard_map.58 = (f32[2,512,128]{2,1,0:T(8,128)S(1)}, f32[2,512,128]{2,1,0:T(8,128)S(1)}, f32[2,512,128]{2,1,0:T(8,128)S(1)}) custom-call(s32[7]{0:T(128)S(1)} %stack.43.refs_0_, s32[96]{0:T(128)S(1)} %reshape.13.refs_1_, bf16[2,512,128]{2,1,0:T(8,128)(2,1)S(1)} %copy-done.4, bf16[4,512,128]{2,1,0:T(8,128)(2,1)S(1)} %collective-permute-done.6.refs_3_, ...), custom_call_target="tpu_custom_call" | custom-call | flops 1476395008 | bytes 2621440 | tf_op jit(solution)/shard_map/pallas_call | solution.py:127
  56.9 0.0 collective-permute-done.3.refs_3_
  56.9 0.0 collective-permute-done.5.refs_4_
  56.9 3.2 %shard_map.59 = bf16[16,2,32,128]{3,2,1,0:T(8,128)(2,1)S(1)} custom-call(s32[7]{0:T(128)S(1)} %stack.43.refs_0_, s32[96]{0:T(128)S(1)} %reshape.13.refs_1_, bf16[2,512,128]{2,1,0:T(8,128)(2,1)S(1)} %copy-done.4, bf16[4,512,128]{2,1,0:T(8,128)(2,1)S(1)} %collective-permute-done.3.refs_3_, bf16[4,512,128]{2,1,0:T(8,128)(2,1)S(1)} %collective-permute-done.5.refs_4_, ...), custom_call_target="tpu_custom_call" | custom-call | flops 671088640 | bytes 1048576 | tf_op jit(solution)/shard_map/pallas_call | solution.py:127
  60.2 30.7 %all_to_all.5.rows_ref = bf16[16,64,128]{2,1,0:T(8,128)(2,1)S(1)} all-to-all(bf16[16,64,128]{2,1,0:T(8,128)(2,1)S(1)} %bitcast.9), channel_id=1, replica_groups=mesh['tm'=32,'head'=16] {'head'}, dimensions={0} | all-to-all | bytes 524288 | tf_op jit(solution)/shard_map/all_to_all | solution.py:335
  90.8 3.6 %collective-permute-start.9 = (bf16[16,64,128]{2,1,0:T(8,128)(2,1)S(1)}, bf16[16,64,128]{2,1,0:T(8,128)(2,1)S(1)}, u32[]{:S(2)}, u32[]{:S(2)}) collective-permute-start(bf16[16,64,128]{2,1,0:T(8,128)(2,1)S(1)} %all_to_all.5.rows_ref), channel_id=1, source_target_pairs={{0,32},{16,48},{32,0},{48,16},{64,96},{80,112},{96,64},{112,80},{1... | collective-permute-start | bytes 786440 | tf_op jit(solution)/shard_map/ppermute | solution.py:263
  94.4 4.1 %collective-permute-done.9.rows_ref = bf16[16,64,128]{2,1,0:T(8,128)(2,1)S(1)} collective-permute-done((bf16[16,64,128]{2,1,0:T(8,128)(2,1)S(1)}, bf16[16,64,128]{2,1,0:T(8,128)(2,1)S(1)}, u32[]{:S(2)}, u32[]{:S(2)}) %collective-permute-start.9) | collective-permute-done | bytes 262176 | tf_op jit(solution)/shard_map/ppermute | solution.py:263
  98.6 2.3 %all-gather.2.cloned.1.call-done.w_ref = bf16[2048,1280]{1,0:T(8,128)(2,1)} async-done(((bf16[128,1280]{1,0:T(8,128)(2,1)}), bf16[2048,1280]{1,0:T(8,128)(2,1)}) %all-gather.2.cloned.1.call-update) | async-done | bytes 5242896 | tf_op jit(solution)/shard_map/all_gather | solution.py:267
  100.9 0.0 copy-start
  100.9 2.5 %copy-done = bf16[2048,1280]{1,0:T(8,128)(2,1)S(1)} copy-done((bf16[2048,1280]{1,0:T(8,128)(2,1)S(1)}, bf16[2048,1280]{1,0:T(8,128)(2,1)}, u32[]{:S(2)}) %copy-start) | copy-done | bytes 5242904
  103.4 0.0 copy-start.1
  103.4 1.0 shard_map.61
  104.4 3.1 %collective-permute-start.10 = (bf16[32,1280]{1,0:T(8,128)(2,1)S(1)}, bf16[32,1280]{1,0:T(8,128)(2,1)S(1)}, u32[]{:S(2)}, u32[]{:S(2)}) collective-permute-start(bf16[32,1280]{1,0:T(8,128)(2,1)S(1)} %get-tuple-element.33), channel_id=1, source_target_pairs={{0,32},{16,48},{32,0},{48,16},{64,96},{80,112},{96,64},{112,80},{1... | collective-permute-start | bytes 245768 | tf_op jit(solution)/shard_map/ppermute | solution.py:263
  107.5 9.0 %collective-permute-start.11 = (bf16[32,1280]{1,0:T(8,128)(2,1)S(1)}, bf16[32,1280]{1,0:T(8,128)(2,1)S(1)}, u32[]{:S(2)}, u32[]{:S(2)}) collective-permute-start(bf16[32,1280]{1,0:T(8,128)(2,1)S(1)} %get-tuple-element.34), channel_id=1, source_target_pairs={{0,48},{16,32},{32,16},{48,0},{64,112},{80,96},{96,80},{112,64},{1... | collective-permute-start | bytes 245768 | tf_op jit(solution)/shard_map/ppermute | solution.py:263
  116.5 0.0 copy-done.1
  116.5 1.0 shard_map.60
  117.5 1.9 %collective-permute-start.8 = (bf16[32,1280]{1,0:T(8,128)(2,1)S(1)}, bf16[32,1280]{1,0:T(8,128)(2,1)S(1)}, u32[]{:S(2)}, u32[]{:S(2)}) collective-permute-start(bf16[32,1280]{1,0:T(8,128)(2,1)S(1)} %get-tuple-element.32), channel_id=1, source_target_pairs={{0,16},{16,0},{32,48},{48,32},{64,80},{80,64},{96,112},{112,96},{1... | collective-permute-start | bytes 245768 | tf_op jit(solution)/shard_map/ppermute | solution.py:263
  119.4 0.0 collective-permute-done.10.far_ref
  119.4 0.0 collective-permute-done.11.far_other_ref
  119.4 1.2 collective-permute-done.8.got_ref
  120.7 0.7 shard_map.62
Async XLA Ops:
  6.5 94.4 %all-gather.2.cloned.1.call-start = ((), (), s32[]{:S(2)}) async-start(), calls=%async_computation.1 | async-start | bytes 5570560 | tf_op jit(solution)/shard_map/all_gather | solution.py:267
  8.6 10.6 %collective-permute-start = (bf16[3,512,128]{2,1,0:T(8,128)(2,1)}, bf16[3,512,128]{2,1,0:T(8,128)(2,1)S(1)}, u32[]{:S(2)}, u32[]{:S(2)}) collective-permute-start(bf16[3,512,128]{2,1,0:T(8,128)(2,1)} %get-tuple-element.20), channel_id=1, source_target_pairs={{0,16},{16,0},{32,48},{48,32},{64,80},{80,64},{96,112},{112,96},{1... | collective-permute-start | bytes 1179656 | tf_op jit(solution)/shard_map/ppermute | solution.py:263
  20.0 13.1 %collective-permute-start.1 = (bf16[4,512,128]{2,1,0:T(8,128)(2,1)}, bf16[4,512,128]{2,1,0:T(8,128)(2,1)S(1)}, u32[]{:S(2)}, u32[]{:S(2)}) collective-permute-start(bf16[4,512,128]{2,1,0:T(8,128)(2,1)} %slice_dynamic-update-slice_fusion.refs_3_), channel_id=1, source_target_pairs={{0,128},{16,144},{32,160},{48,176},{64,192},{80,208},{96,224},{112... | collective-permute-start | bytes 1572872 | tf_op jit(solution)/shard_map/ppermute | solution.py:263
  21.3 15.7 %collective-permute-start.2 = (bf16[4,512,128]{2,1,0:T(8,128)(2,1)}, bf16[4,512,128]{2,1,0:T(8,128)(2,1)S(1)}, u32[]{:S(2)}, u32[]{:S(2)}) collective-permute-start(bf16[4,512,128]{2,1,0:T(8,128)(2,1)} %slice_dynamic-update-slice_fusion.refs_3_), channel_id=1, source_target_pairs={{128,0},{144,16},{160,32},{176,48},{192,64},{208,80},{224,96},{240... | collective-permute-start | bytes 1572872 | tf_op jit(solution)/shard_map/ppermute | solution.py:263
  22.6 17.2 %collective-permute-start.4 = (bf16[4,512,128]{2,1,0:T(8,128)(2,1)}, bf16[4,512,128]{2,1,0:T(8,128)(2,1)S(1)}, u32[]{:S(2)}, u32[]{:S(2)}) collective-permute-start(bf16[4,512,128]{2,1,0:T(8,128)(2,1)} %slice_dynamic-update-slice_fusion.refs_3_), channel_id=1, source_target_pairs={{0,64},{16,80},{32,96},{48,112},{64,0},{80,16},{96,32},{112,48},{1... | collective-permute-start | bytes 1572872 | tf_op jit(solution)/shard_map/ppermute | solution.py:263
  24.5 25.5 %collective-permute-start.6 = (bf16[4,512,128]{2,1,0:T(8,128)(2,1)}, bf16[4,512,128]{2,1,0:T(8,128)(2,1)S(1)}, u32[]{:S(2)}, u32[]{:S(2)}) collective-permute-start(bf16[4,512,128]{2,1,0:T(8,128)(2,1)} %slice_dynamic-update-slice_fusion.refs_3_), channel_id=1, source_target_pairs={{0,32},{16,48},{32,0},{48,16},{64,96},{80,112},{96,64},{112,80},{1... | collective-permute-start | bytes 1572872 | tf_op jit(solution)/shard_map/ppermute | solution.py:263
  26.5 23.6 %collective-permute-start.7 = (bf16[4,512,128]{2,1,0:T(8,128)(2,1)}, bf16[4,512,128]{2,1,0:T(8,128)(2,1)}, u32[]{:S(2)}, u32[]{:S(2)}) collective-permute-start(bf16[4,512,128]{2,1,0:T(8,128)(2,1)} %slice_dynamic-update-slice_fusion.refs_3_), channel_id=1, source_target_pairs={{0,256},{16,272},{32,288},{48,304},{64,320},{80,336},{96,352},{112... | collective-permute-start | bytes 1572872 | tf_op jit(solution)/shard_map/ppermute | solution.py:263
  37.9 19.0 %collective-permute-start.3 = (bf16[4,512,128]{2,1,0:T(8,128)(2,1)}, bf16[4,512,128]{2,1,0:T(8,128)(2,1)S(1)}, u32[]{:S(2)}, u32[]{:S(2)}) collective-permute-start(bf16[4,512,128]{2,1,0:T(8,128)(2,1)} %select_select_fusion), channel_id=1, source_target_pairs={{0,96},{16,112},{32,64},{48,80},{64,32},{80,48},{96,0},{112,16},{1... | collective-permute-start | bytes 1572872 | tf_op jit(solution)/shard_map/ppermute | solution.py:263
  39.8 17.1 %collective-permute-start.5 = (bf16[4,512,128]{2,1,0:T(8,128)(2,1)S(1)}, bf16[4,512,128]{2,1,0:T(8,128)(2,1)S(1)}, u32[]{:S(2)}, u32[]{:S(2)}) collective-permute-start(bf16[4,512,128]{2,1,0:T(8,128)(2,1)S(1)} %collective-permute-done.4.refs_4_), channel_id=1, source_target_pairs={{0,128},{16,144},{32,160},{48,176},{128,256},{144,272},{160,288},{... | collective-permute-start | bytes 1572872 | tf_op jit(solution)/shard_map/ppermute | solution.py:263
  45.1 1.0 copy-start.2
  46.1 1.0 copy-start.3
  50.1 1.0 copy-start.4
  90.8 7.7 %collective-permute-start.9 = (bf16[16,64,128]{2,1,0:T(8,128)(2,1)S(1)}, bf16[16,64,128]{2,1,0:T(8,128)(2,1)S(1)}, u32[]{:S(2)}, u32[]{:S(2)}) collective-permute-start(bf16[16,64,128]{2,1,0:T(8,128)(2,1)S(1)} %all_to_all.5.rows_ref), channel_id=1, source_target_pairs={{0,32},{16,48},{32,0},{48,16},{64,96},{80,112},{96,64},{112,80},{1... | collective-permute-start | bytes 786440 | tf_op jit(solution)/shard_map/ppermute | solution.py:263
  100.9 2.5 %copy-start = (bf16[2048,1280]{1,0:T(8,128)(2,1)S(1)}, bf16[2048,1280]{1,0:T(8,128)(2,1)}, u32[]{:S(2)}) copy-start(bf16[2048,1280]{1,0:T(8,128)(2,1)} %all-gather.2.cloned.1.call-done.w_ref) | copy-start | bytes 15728644
  103.4 13.1 %copy-start.1 = (bf16[2048,1280]{1,0:T(8,128)(2,1)S(1)}, bf16[2048,1280]{1,0:T(8,128)(2,1)}, u32[]{:S(2)}) copy-start(bf16[2048,1280]{1,0:T(8,128)(2,1)} %all-gather.2.cloned.1.call-done.w_ref) | copy-start | bytes 15728644
  104.4 15.0 %collective-permute-start.10 = (bf16[32,1280]{1,0:T(8,128)(2,1)S(1)}, bf16[32,1280]{1,0:T(8,128)(2,1)S(1)}, u32[]{:S(2)}, u32[]{:S(2)}) collective-permute-start(bf16[32,1280]{1,0:T(8,128)(2,1)S(1)} %get-tuple-element.33), channel_id=1, source_target_pairs={{0,32},{16,48},{32,0},{48,16},{64,96},{80,112},{96,64},{112,80},{1... | collective-permute-start | bytes 245768 | tf_op jit(solution)/shard_map/ppermute | solution.py:263
  107.5 11.9 %collective-permute-start.11 = (bf16[32,1280]{1,0:T(8,128)(2,1)S(1)}, bf16[32,1280]{1,0:T(8,128)(2,1)S(1)}, u32[]{:S(2)}, u32[]{:S(2)}) collective-permute-start(bf16[32,1280]{1,0:T(8,128)(2,1)S(1)} %get-tuple-element.34), channel_id=1, source_target_pairs={{0,48},{16,32},{32,16},{48,0},{64,112},{80,96},{96,80},{112,64},{1... | collective-permute-start | bytes 245768 | tf_op jit(solution)/shard_map/ppermute | solution.py:263
  117.5 3.2 %collective-permute-start.8 = (bf16[32,1280]{1,0:T(8,128)(2,1)S(1)}, bf16[32,1280]{1,0:T(8,128)(2,1)S(1)}, u32[]{:S(2)}, u32[]{:S(2)}) collective-permute-start(bf16[32,1280]{1,0:T(8,128)(2,1)S(1)} %get-tuple-element.32), channel_id=1, source_target_pairs={{0,16},{16,0},{32,48},{48,32},{64,80},{80,64},{96,112},{112,96},{1... | collective-permute-start | bytes 245768 | tf_op jit(solution)/shard_map/ppermute | solution.py:263
Sparse Core Ops, SparseCore 0:
  9.4 91.4 all-gather.1

commit v6 on v5

--- a/solution.py
+++ b/solution.py
@@ -18,7 +18,6 @@
 HIDDEN = -1e30
 SCALE = math.log2(math.e) / math.sqrt(HD)
 VMEM = 40 * 1024 * 1024
-WIDE = 56 * 1024 * 1024
 NARROW = 24 * 1024 * 1024
 
 
@@ -47,7 +46,7 @@
             for a in range(blocks):
                 row = []
                 for b in range(NB):
-                    shown = mask_ref[(level * NB + tile * blocks + a) * NB + b] > 0
+                    shown = mask_ref[tile * blocks + a, b, level] > 0
                     bias = jnp.where(here & shown, jnp.float32(0.0), jnp.float32(HIDDEN))
                     block = scores[a * BLK : (a + 1) * BLK, b * BLK : (b + 1) * BLK]
                     row.append(block + bias)
@@ -139,86 +138,32 @@
     return out[0] if last else out
 
 
-def give_kernel(core_ref, side_ref, k_ref, v_ref, q_ref, w_ref, give_out, w_out):
-    give_out[0] = k_ref[...]
-    give_out[1] = v_ref[...]
-    give_out[2] = q_ref[...]
-    w_out[...] = w_ref[...]
-
-
-def keep_kernel(core_ref, k_ref, v_ref, q_ref, kv_out, q_out):
-    kv_out[0] = k_ref[...]
-    kv_out[1] = v_ref[...]
-    q_out[0] = q_ref[...]
-
-
-def give(core, side, queries, keys, values, out_weight):
-    kind = queries.dtype
-    half = DOUT // 2
-    yours = pl.BlockSpec((FT, HD), lambda n, core, side: (0, 1 - core[0]))
-    return pl.pallas_call(
-        give_kernel,
-        out_shape=(
-            jax.ShapeDtypeStruct((3, FT, HD), kind),
-            jax.ShapeDtypeStruct((HD, half), kind),
-        ),
-        grid_spec=pltpu.PrefetchScalarGridSpec(
-            num_scalar_prefetch=2,
-            grid=(1,),
-            in_specs=[yours] * 3
-            + [pl.BlockSpec((HD, half), lambda n, core, side: (core[0], side[0]))],
-            out_specs=(
-                pl.BlockSpec((3, FT, HD), lambda n, core, side: (0, 0, 0)),
-                pl.BlockSpec((HD, half), lambda n, core, side: (0, 0)),
-            ),
-        ),
-        compiler_params=pltpu.CompilerParams(vmem_limit_bytes=WIDE),
-    )(core, side, keys, values, queries, out_weight)
-
-
-def keep(core, queries, keys, values):
-    kind = queries.dtype
-    mine = pl.BlockSpec((FT, HD), lambda n, core: (0, core[0]))
-    return pl.pallas_call(
-        keep_kernel,
-        out_shape=(
-            jax.ShapeDtypeStruct((4, FT, HD), kind),
-            jax.ShapeDtypeStruct((2, FT, HD), kind),
-        ),
-        grid_spec=pltpu.PrefetchScalarGridSpec(
-            num_scalar_prefetch=1,
-            grid=(1,),
-            in_specs=[mine] * 3,
-            out_specs=(
-                pl.BlockSpec((2, FT, HD), lambda n, core: (0, 0, 0)),
-                pl.BlockSpec((1, FT, HD), lambda n, core: (0, 0, 0)),
-            ),
-        ),
-        compiler_params=pltpu.CompilerParams(vmem_limit_bytes=WIDE),
-    )(core, keys, values, queries)
-
-
-def product_kernel(rows_ref, w_ref, mine_ref, yours_ref):
-    rows = jnp.concatenate([rows_ref[z] for z in range(rows_ref.shape[0])], axis=1)
-    part = jnp.dot(rows, w_ref[...], preferred_element_type=jnp.float32).astype(jnp.bfloat16)
-    mine_ref[...] = part[:ROWS]
-    yours_ref[...] = part[ROWS:]
-
-
-def product(rows, weight):
+def product_kernel(own_ref, far_ref, w_ref, *out_refs):
+    rows = [
+        jnp.concatenate([ref[z] for z in range(ref.shape[0])], axis=1)
+        for ref in (own_ref, far_ref)
+    ]
+    total = jnp.dot(
+        jnp.concatenate(rows, axis=0), w_ref[...], preferred_element_type=jnp.float32
+    ).astype(jnp.bfloat16)
+    for k, out in enumerate(out_refs):
+        out[...] = total[k * ROWS : (k + 1) * ROWS]
+
+
+def product(own, far, weight):
     depth, width = weight.shape
     vmem = pl.BlockSpec(memory_space=pltpu.VMEM)
-    part = jax.ShapeDtypeStruct((ROWS, width), rows.dtype)
+    part = jax.ShapeDtypeStruct((ROWS, width), own.dtype)
     return pl.pallas_call(
         product_kernel,
-        out_shape=(part, part),
-        in_specs=[vmem, vmem],
-        out_specs=(vmem, vmem),
+        out_shape=(part,) * 4,
+        in_specs=[vmem] * 3,
+        out_specs=(vmem,) * 4,
         compiler_params=pltpu.CompilerParams(vmem_limit_bytes=NARROW),
         cost_estimate=pl.CostEstimate(
-            flops=4 * ROWS * depth * width, bytes_accessed=depth * width * 2, transcendentals=0
+            flops=8 * ROWS * depth * width, bytes_accessed=depth * width * 2, transcendentals=0
         ),
-    )(rows, weight)
+    )(own, far, weight)
 
 
 def add_kernel(side_ref, own_ref, got_ref, far_ref, far_other_ref, out_ref):
@@ -262,18 +207,25 @@
     def send(array, pairs):
         return lax.ppermute(array, "tm", pairs)
 
-    at_core, at_side = core.reshape(1), (y & 1).reshape(1)
-    given, weight = give(at_core, at_side, queries, keys, values, out_weight)
+    half = DOUT // 2
+    weight = lax.dynamic_slice(out_weight, (core * HD, (y & 1) * half), (HD, half))
+    first_core = core == 0
+    weight, first_core = lax.optimization_barrier((weight, first_core))
     weight = lax.all_gather(weight, "head", axis=0, tiled=True)
+
+    def head(array, low):
+        return jnp.where(low, array[:, :HD], array[:, HD:])
+
     swap = [(i, i ^ 1) for i in range(32)]
+    given = jnp.stack([head(array, ~first_core) for array in (keys, values, queries)])
     got = send(given, swap)
-    at_core, _ = lax.optimization_barrier((at_core, given))
-    kv_own, q_own = keep(at_core, queries, keys, values)
-    local = lax.dynamic_update_slice(kv_own, got[:2], (2, 0, 0))
-    q = lax.dynamic_update_slice(q_own, got[2:], (1, 0, 0))
-
+    first_core, _ = lax.optimization_barrier((first_core, given))
+    k_own, v_own, q_own = (head(array, first_core) for array in (keys, values, queries))
+    local = jnp.concatenate([jnp.stack([k_own, v_own]), got[:2]], axis=0)
+    q = jnp.concatenate([q_own[None], got[2:]], axis=0)
+
+    across = send(local, chips(lambda x, y: (x, y ^ 2)))
     above = send(local, chips(lambda x, y: (x + 1, y) if x < 3 else None))
-    across = send(local, chips(lambda x, y: (x, y ^ 2)))
     below = send(local, chips(lambda x, y: (x - 1, y) if x > 0 else None))
     beside = send(local, chips(lambda x, y: (x, y ^ 1)))
     far = send(local, chips(lambda x, y: (x ^ 2, y)))
@@ -301,7 +253,7 @@
             has_below.astype(jnp.int32),
         ]
     ).astype(jnp.int32)
-    mask = block_mask.reshape(-1)
+    mask = jnp.transpose(block_mask, (1, 2, 0))
 
     state = attend(info, mask, q, [local], [(0, False, 0, 2), (0, True, 1, 2)], None, None, False)
     state = attend(
@@ -336,13 +288,11 @@
         attended.reshape(FT // ROWS, 2 * ROWS, HD), "head", 0, 0, tiled=True
     )
     pair = [(i, i ^ 2) for i in range(32)]
-    partner = send(rows, pair)
-    own, yours = product(rows, weight)
-    got = send(yours, swap)
-    far, far_yours = product(partner, weight)
+    own, yours, far, far_yours = product(rows, send(rows, pair), weight)
     far = send(far, pair)
     far_other = send(far_yours, [(i, i ^ 3) for i in range(32)])
-    return add_cores(at_side, own, got, far, far_other)
+    got = send(yours, swap)
+    return add_cores((y & 1).reshape(1), own, got, far, far_other)
 
 
 def solution(mesh):

time: 129 us -> 128 us (level)
  Pallas kernels: 18.7 us -> 13.8 us
  other arithmetic: 0.87 us -> 4.35 us
  local copies, waits for them, and re-layouts: 7.79 us -> 4.37 us
  waiting for transfers between devices: 13.1 us -> 15.1 us
  blocking collectives: 30.7 us -> 32.4 us
    pallas_call x4 -> x1, Pallas kernels: 5.94 us -> 0.85 us  [product(): pl.pallas_call(product_kernel, out_shape=(part,) * 4, in_specs=[vmem] * 3...]
    another operation x0 -> x5, other arithmetic: none -> 4.14 us  [the longest x3 2.16 us: shards(): jnp.stack([head(array, ~first_core) for array in (keys, values, queries)])]
    unnamed x11 -> x6, local copies, waits for them, and re-layouts: 6.23 us -> 2.49 us
    ppermute x12, waiting for transfers between devices: 10.7 us -> 12.7 us  [send(): return lax.ppermute(array, 'tm', pairs)]
    dynamic_slice x0 -> x1, local copies, waits for them, and re-layouts: none -> 1.76 us  [shards(): lax.dynamic_slice(out_weight, (core * HD, (y & 1) * half), (HD, half))]
    all_to_all x1, blocking collectives: 30.7 us -> 32.4 us  [shards(): lax.all_to_all(attended.reshape(FT // ROWS, 2 * ROWS, HD), 'head', 0, 0,...]
    dynamic_update_slice x2 -> x0, local copies, waits for them, and re-layouts: 1.37 us -> none  [the longest x1 0.72 us: shards(): local = lax.dynamic_update_slice(kv_own, got[:2], (2, 0, 0))]
  transfers between devices with their start and end apart: 13 -> 13, of which waited for: 5 -> 9; matrix products, arithmetic and copies ran while one was open for 3% -> 4% of each run, Pallas kernels for 12% -> 10%
where the time goes in v6:
time: 128 us; the launch traced here: 127 us
  starting transfers between devices  43.3 us (34%)
  blocking collectives  32.4 us (25%)
  waiting for transfers between devices  15.1 us (12%)
  Pallas kernels  13.8 us (11%)
  between operations  13.7 us (11%)
  local copies, waits for them, and re-layouts  4.37 us (3%)
  other arithmetic  4.35 us (3%)
    ppermute x12, starting transfers between devices, send(): return lax.ppermute(array, 'tm', pairs)  43.3 us
    all_to_all x1, blocking collectives, shards(): lax.all_to_all(attended.reshape(FT // ROWS, 2 * ROWS, HD), 'head', 0, 0,...  32.4 us
    ppermute x12, waiting for transfers between devices, send(): return lax.ppermute(array, 'tm', pairs)  12.7 us
    pallas_call x3, Pallas kernels, attend(): pl.pallas_call(functools.partial(attend_kernel, sources, split, len(kvs),...  12.2 us
  transfers between devices with their start and end apart: 13, of which 9 were waited for; matrix products, arithmetic and copies ran while one was open for 4% of the time, Pallas kernels for 10%

profile of v6, /device:TPU:1, one launch (start us, length us, event | category | flops | bytes accessed | tf_op | source)
XLA Modules:
  0.0 126.9 jit_solution(3872353718196453244)
XLA Ops:
  6.5 0.0 copy-start.2
  6.5 0.0 copy-start.1
  6.5 0.0 all-gather.2.cloned.1.call-start
  6.5 1.8 %dynamic_slice.3 = bf16[128,1280]{1,0:T(8,128)(2,1)} dynamic-slice(bf16[256,2560]{1,0:T(8,128)(2,1)} %param.9, s32[]{:T(128)S(6)} %select_n.64, s32[]{:T(128)S(6)} %select_n.65), dynamic_slice_sizes={128,1280} | dynamic-slice | bytes 655364 | tf_op jit(solution)/shard_map/dynamic_slice | solution.py:211
  8.3 0.0 all-gather.2.cloned.1.call-update
  8.3 1.0 select_bitcast_fusion.5
  9.3 1.1 select_bitcast_fusion.3
  10.5 8.8 %collective-permute-start = (bf16[3,512,128]{2,1,0:T(8,128)(2,1)S(1)}, bf16[3,512,128]{2,1,0:T(8,128)(2,1)S(1)}, u32[]{:S(2)}, u32[]{:S(2)}) collective-permute-start(bf16[3,512,128]{2,1,0:T(8,128)(2,1)S(1)} %pad_maximum_fusion.1), channel_id=1, source_target_pairs={{0,16},{16,0},{32,48},{48,32},{64,80},{80,64},{96,112},{112,96},{1... | collective-permute-start | bytes 1179656 | tf_op jit(solution)/shard_map/ppermute | solution.py:208
  19.3 1.0 select_bitcast_fusion
  20.3 1.0 select_bitcast_fusion.1
  21.3 0.0 collective-permute-done
  21.3 0.1 pad_maximum_fusion.refs_3_
  21.4 1.3 %collective-permute-start.1 = (bf16[4,512,128]{2,1,0:T(8,128)(2,1)S(1)}, bf16[4,512,128]{2,1,0:T(8,128)(2,1)S(1)}, u32[]{:S(2)}, u32[]{:S(2)}) collective-permute-start(bf16[4,512,128]{2,1,0:T(8,128)(2,1)S(1)} %pad_maximum_fusion.refs_3_), channel_id=1, source_target_pairs={{0,128},{16,144},{32,160},{48,176},{64,192},{80,208},{96,224},{112... | collective-permute-start | bytes 1572872 | tf_op jit(solution)/shard_map/ppermute | solution.py:208
  22.7 1.3 %collective-permute-start.2 = (bf16[4,512,128]{2,1,0:T(8,128)(2,1)S(1)}, bf16[4,512,128]{2,1,0:T(8,128)(2,1)S(1)}, u32[]{:S(2)}, u32[]{:S(2)}) collective-permute-start(bf16[4,512,128]{2,1,0:T(8,128)(2,1)S(1)} %pad_maximum_fusion.refs_3_), channel_id=1, source_target_pairs={{128,0},{144,16},{160,32},{176,48},{192,64},{208,80},{224,96},{240... | collective-permute-start | bytes 1572872 | tf_op jit(solution)/shard_map/ppermute | solution.py:208
  24.0 1.9 %collective-permute-start.4 = (bf16[4,512,128]{2,1,0:T(8,128)(2,1)S(1)}, bf16[4,512,128]{2,1,0:T(8,128)(2,1)S(1)}, u32[]{:S(2)}, u32[]{:S(2)}) collective-permute-start(bf16[4,512,128]{2,1,0:T(8,128)(2,1)S(1)} %pad_maximum_fusion.refs_3_), channel_id=1, source_target_pairs={{0,64},{16,80},{32,96},{48,112},{64,0},{80,16},{96,32},{112,48},{1... | collective-permute-start | bytes 1572872 | tf_op jit(solution)/shard_map/ppermute | solution.py:208
  26.0 0.1 stack.61.refs_0_
  26.1 1.9 %collective-permute-start.6 = (bf16[4,512,128]{2,1,0:T(8,128)(2,1)S(1)}, bf16[4,512,128]{2,1,0:T(8,128)(2,1)S(1)}, u32[]{:S(2)}, u32[]{:S(2)}) collective-permute-start(bf16[4,512,128]{2,1,0:T(8,128)(2,1)S(1)} %pad_maximum_fusion.refs_3_), channel_id=1, source_target_pairs={{0,32},{16,48},{32,0},{48,16},{64,96},{80,112},{96,64},{112,80},{1... | collective-permute-start | bytes 1572872 | tf_op jit(solution)/shard_map/ppermute | solution.py:208
  28.0 5.2 %collective-permute-start.7 = (bf16[4,512,128]{2,1,0:T(8,128)(2,1)S(1)}, bf16[4,512,128]{2,1,0:T(8,128)(2,1)S(1)}, u32[]{:S(2)}, u32[]{:S(2)}) collective-permute-start(bf16[4,512,128]{2,1,0:T(8,128)(2,1)S(1)} %pad_maximum_fusion.refs_3_), channel_id=1, source_target_pairs={{0,256},{16,272},{32,288},{48,304},{64,320},{80,336},{96,352},{112... | collective-permute-start | bytes 1572872 | tf_op jit(solution)/shard_map/ppermute | solution.py:208
  33.2 1.0 collective-permute-done.1.refs_5_
  34.2 4.0 %collective-permute-done.2.refs_6_ = bf16[4,512,128]{2,1,0:T(8,128)(2,1)S(1)} collective-permute-done((bf16[4,512,128]{2,1,0:T(8,128)(2,1)S(1)}, bf16[4,512,128]{2,1,0:T(8,128)(2,1)S(1)}, u32[]{:S(2)}, u32[]{:S(2)}) %collective-permute-start.2) | collective-permute-done | bytes 524320 | tf_op jit(solution)/shard_map/ppermute | solution.py:208
  38.3 0.1 select_select_fusion
  38.4 1.9 %collective-permute-start.3 = (bf16[4,512,128]{2,1,0:T(8,128)(2,1)S(1)}, bf16[4,512,128]{2,1,0:T(8,128)(2,1)S(1)}, u32[]{:S(2)}, u32[]{:S(2)}) collective-permute-start(bf16[4,512,128]{2,1,0:T(8,128)(2,1)S(1)} %select_select_fusion), channel_id=1, source_target_pairs={{0,96},{16,112},{32,64},{48,80},{64,32},{80,48},{96,0},{112,16},{1... | collective-permute-start | bytes 1572872 | tf_op jit(solution)/shard_map/ppermute | solution.py:208
  40.3 0.7 collective-permute-done.4.refs_4_
  41.0 3.7 %collective-permute-start.5 = (bf16[4,512,128]{2,1,0:T(8,128)(2,1)S(1)}, bf16[4,512,128]{2,1,0:T(8,128)(2,1)S(1)}, u32[]{:S(2)}, u32[]{:S(2)}) collective-permute-start(bf16[4,512,128]{2,1,0:T(8,128)(2,1)S(1)} %collective-permute-done.4.refs_4_), channel_id=1, source_target_pairs={{0,128},{16,144},{32,160},{48,176},{128,256},{144,272},{160,288},{... | collective-permute-start | bytes 1572872 | tf_op jit(solution)/shard_map/ppermute | solution.py:208
  44.7 0.0 copy-done.2
  44.7 0.0 copy-done.1
  44.8 3.2 %shard_map.55 = (f32[2,512,128]{2,1,0:T(8,128)S(1)}, f32[2,512,128]{2,1,0:T(8,128)S(1)}, f32[2,512,128]{2,1,0:T(8,128)S(1)}) custom-call(s32[7]{0:T(128)S(1)} %stack.61.refs_0_, s32[4,4,6]{2,1,0:T(4,128)S(1)} %bitcast.22, bf16[2,512,128]{2,1,0:T(8,128)(2,1)S(1)} %pad_maximum_fusion.2.refs_2_, bf16[4,512,128]{2,1,0:T(8,128)(2,1)S(1)} %pad_maximum_fusion.refs_3_), custom_call_target="tpu_custom_call" | custom-call | flops 536870912 | bytes 524288 | tf_op jit(solution)/shard_map/pallas_call | solution.py:126
  47.9 0.8 collective-permute-done.6.refs_3_
  48.8 0.0 collective-permute-done.7.refs_7_
  48.8 5.6 %shard_map.56 = (f32[2,512,128]{2,1,0:T(8,128)S(1)}, f32[2,512,128]{2,1,0:T(8,128)S(1)}, f32[2,512,128]{2,1,0:T(8,128)S(1)}) custom-call(s32[7]{0:T(128)S(1)} %stack.61.refs_0_, s32[4,4,6]{2,1,0:T(4,128)S(1)} %bitcast.23, bf16[2,512,128]{2,1,0:T(8,128)(2,1)S(1)} %pad_maximum_fusion.2.refs_2_, bf16[4,512,128]{2,1,0:T(8,128)(2,1)S(1)} %collective-permute-done.6.refs_3_, ...), custom_call_target="tpu_custom_call" | custom-call | flops 1476395008 | bytes 2621440 | tf_op jit(solution)/shard_map/pallas_call | solution.py:126
  54.4 0.0 collective-permute-done.3.refs_3_
  54.4 0.6 collective-permute-done.5.refs_4_
  55.0 3.4 %shard_map.57 = bf16[16,2,32,128]{3,2,1,0:T(8,128)(2,1)S(1)} custom-call(s32[7]{0:T(128)S(1)} %stack.61.refs_0_, s32[4,4,6]{2,1,0:T(4,128)S(1)} %bitcast.24, bf16[2,512,128]{2,1,0:T(8,128)(2,1)S(1)} %pad_maximum_fusion.2.refs_2_, bf16[4,512,128]{2,1,0:T(8,128)(2,1)S(1)} %collective-permute-done.3.refs_3_, ...), custom_call_target="tpu_custom_call" | custom-call | flops 671088640 | bytes 1048576 | tf_op jit(solution)/shard_map/pallas_call | solution.py:126
  58.5 32.4 %all_to_all.5.own_ref = bf16[16,64,128]{2,1,0:T(8,128)(2,1)S(1)} all-to-all(bf16[16,64,128]{2,1,0:T(8,128)(2,1)S(1)} %bitcast.21), channel_id=1, replica_groups=mesh['tm'=32,'head'=16] {'head'}, dimensions={0} | all-to-all | bytes 524288 | tf_op jit(solution)/shard_map/all_to_all | solution.py:287
  90.8 3.2 %collective-permute-start.8 = (bf16[16,64,128]{2,1,0:T(8,128)(2,1)S(1)}, bf16[16,64,128]{2,1,0:T(8,128)(2,1)S(1)}, u32[]{:S(2)}, u32[]{:S(2)}) collective-permute-start(bf16[16,64,128]{2,1,0:T(8,128)(2,1)S(1)} %all_to_all.5.own_ref), channel_id=1, source_target_pairs={{0,32},{16,48},{32,0},{48,16},{64,96},{80,112},{96,64},{112,80},{1... | collective-permute-start | bytes 786440 | tf_op jit(solution)/shard_map/ppermute | solution.py:208
  94.0 4.3 %collective-permute-done.8.far_ref = bf16[16,64,128]{2,1,0:T(8,128)(2,1)S(1)} collective-permute-done((bf16[16,64,128]{2,1,0:T(8,128)(2,1)S(1)}, bf16[16,64,128]{2,1,0:T(8,128)(2,1)S(1)}, u32[]{:S(2)}, u32[]{:S(2)}) %collective-permute-start.8) | collective-permute-done | bytes 262176 | tf_op jit(solution)/shard_map/ppermute | solution.py:208
  98.4 2.4 %all-gather.2.cloned.1.call-done.w_ref = bf16[2048,1280]{1,0:T(8,128)(2,1)} async-done(((bf16[128,1280]{1,0:T(8,128)(2,1)}), bf16[2048,1280]{1,0:T(8,128)(2,1)}) %all-gather.2.cloned.1.call-update) | async-done | bytes 5242896 | tf_op jit(solution)/shard_map/all_gather | solution.py:214
  100.8 0.0 copy-start
  100.8 2.5 %copy-done = bf16[2048,1280]{1,0:T(8,128)(2,1)S(1)} copy-done((bf16[2048,1280]{1,0:T(8,128)(2,1)S(1)}, bf16[2048,1280]{1,0:T(8,128)(2,1)}, u32[]{:S(2)}) %copy-start) | copy-done | bytes 5242904
  103.2 0.8 shard_map.58
  104.1 3.0 %collective-permute-start.10 = (bf16[32,1280]{1,0:T(8,128)(2,1)S(1)}, bf16[32,1280]{1,0:T(8,128)(2,1)S(1)}, u32[]{:S(2)}, u32[]{:S(2)}) collective-permute-start(bf16[32,1280]{1,0:T(8,128)(2,1)S(1)} %get-tuple-element.29), channel_id=1, source_target_pairs={{0,32},{16,48},{32,0},{48,16},{64,96},{80,112},{96,64},{112,80},{1... | collective-permute-start | bytes 245768 | tf_op jit(solution)/shard_map/ppermute | solution.py:208
  107.1 9.1 %collective-permute-start.11 = (bf16[32,1280]{1,0:T(8,128)(2,1)S(1)}, bf16[32,1280]{1,0:T(8,128)(2,1)S(1)}, u32[]{:S(2)}, u32[]{:S(2)}) collective-permute-start(bf16[32,1280]{1,0:T(8,128)(2,1)S(1)} %get-tuple-element.30), channel_id=1, source_target_pairs={{0,48},{16,32},{32,16},{48,0},{64,112},{80,96},{96,80},{112,64},{1... | collective-permute-start | bytes 245768 | tf_op jit(solution)/shard_map/ppermute | solution.py:208
  116.2 1.9 %collective-permute-start.9 = (bf16[32,1280]{1,0:T(8,128)(2,1)S(1)}, bf16[32,1280]{1,0:T(8,128)(2,1)S(1)}, u32[]{:S(2)}, u32[]{:S(2)}) collective-permute-start(bf16[32,1280]{1,0:T(8,128)(2,1)S(1)} %get-tuple-element.28), channel_id=1, source_target_pairs={{0,16},{16,0},{32,48},{48,32},{64,80},{80,64},{96,112},{112,96},{1... | collective-permute-start | bytes 245768 | tf_op jit(solution)/shard_map/ppermute | solution.py:208
  118.2 0.0 collective-permute-done.10.far_ref
  118.2 0.8 collective-permute-done.11.far_other_ref
  118.9 0.5 collective-permute-done.9.got_ref
  119.4 0.7 shard_map.59
  (5 shorter events, 0.1 us)
Async XLA Ops:
  6.5 38.1 %copy-start.2 = (bf16[512,256]{1,0:T(8,128)(2,1)S(1)}, bf16[512,256]{1,0:T(8,128)(2,1)}, u32[]{:S(2)}) copy-start(bf16[512,256]{1,0:T(8,128)(2,1)} %param.5) | copy-start | bytes 786436
  6.5 38.2 %copy-start.1 = (s32[6,4,4]{0,2,1:T(4,128)S(1)}, s32[6,4,4]{0,2,1:T(4,128)}, u32[]{:S(2)}) copy-start(s32[6,4,4]{0,2,1:T(4,128)} %param.8) | copy-start | bytes 1156
  6.5 94.2 %all-gather.2.cloned.1.call-start = ((), (), s32[]{:S(2)}) async-start(), calls=%async_computation.1 | async-start | bytes 5570560 | tf_op jit(solution)/shard_map/all_gather | solution.py:214
  10.5 10.8 %collective-permute-start = (bf16[3,512,128]{2,1,0:T(8,128)(2,1)S(1)}, bf16[3,512,128]{2,1,0:T(8,128)(2,1)S(1)}, u32[]{:S(2)}, u32[]{:S(2)}) collective-permute-start(bf16[3,512,128]{2,1,0:T(8,128)(2,1)S(1)} %pad_maximum_fusion.1), channel_id=1, source_target_pairs={{0,16},{16,0},{32,48},{48,32},{64,80},{80,64},{96,112},{112,96},{1... | collective-permute-start | bytes 1179656 | tf_op jit(solution)/shard_map/ppermute | solution.py:208
  21.4 12.8 %collective-permute-start.1 = (bf16[4,512,128]{2,1,0:T(8,128)(2,1)S(1)}, bf16[4,512,128]{2,1,0:T(8,128)(2,1)S(1)}, u32[]{:S(2)}, u32[]{:S(2)}) collective-permute-start(bf16[4,512,128]{2,1,0:T(8,128)(2,1)S(1)} %pad_maximum_fusion.refs_3_), channel_id=1, source_target_pairs={{0,128},{16,144},{32,160},{48,176},{64,192},{80,208},{96,224},{112... | collective-permute-start | bytes 1572872 | tf_op jit(solution)/shard_map/ppermute | solution.py:208
  22.7 15.5 %collective-permute-start.2 = (bf16[4,512,128]{2,1,0:T(8,128)(2,1)S(1)}, bf16[4,512,128]{2,1,0:T(8,128)(2,1)S(1)}, u32[]{:S(2)}, u32[]{:S(2)}) collective-permute-start(bf16[4,512,128]{2,1,0:T(8,128)(2,1)S(1)} %pad_maximum_fusion.refs_3_), channel_id=1, source_target_pairs={{128,0},{144,16},{160,32},{176,48},{192,64},{208,80},{224,96},{240... | collective-permute-start | bytes 1572872 | tf_op jit(solution)/shard_map/ppermute | solution.py:208
  24.0 16.9 %collective-permute-start.4 = (bf16[4,512,128]{2,1,0:T(8,128)(2,1)S(1)}, bf16[4,512,128]{2,1,0:T(8,128)(2,1)S(1)}, u32[]{:S(2)}, u32[]{:S(2)}) collective-permute-start(bf16[4,512,128]{2,1,0:T(8,128)(2,1)S(1)} %pad_maximum_fusion.refs_3_), channel_id=1, source_target_pairs={{0,64},{16,80},{32,96},{48,112},{64,0},{80,16},{96,32},{112,48},{1... | collective-permute-start | bytes 1572872 | tf_op jit(solution)/shard_map/ppermute | solution.py:208
  26.1 22.7 %collective-permute-start.6 = (bf16[4,512,128]{2,1,0:T(8,128)(2,1)S(1)}, bf16[4,512,128]{2,1,0:T(8,128)(2,1)S(1)}, u32[]{:S(2)}, u32[]{:S(2)}) collective-permute-start(bf16[4,512,128]{2,1,0:T(8,128)(2,1)S(1)} %pad_maximum_fusion.refs_3_), channel_id=1, source_target_pairs={{0,32},{16,48},{32,0},{48,16},{64,96},{80,112},{96,64},{112,80},{1... | collective-permute-start | bytes 1572872 | tf_op jit(solution)/shard_map/ppermute | solution.py:208
  28.0 20.8 %collective-permute-start.7 = (bf16[4,512,128]{2,1,0:T(8,128)(2,1)S(1)}, bf16[4,512,128]{2,1,0:T(8,128)(2,1)S(1)}, u32[]{:S(2)}, u32[]{:S(2)}) collective-permute-start(bf16[4,512,128]{2,1,0:T(8,128)(2,1)S(1)} %pad_maximum_fusion.refs_3_), channel_id=1, source_target_pairs={{0,256},{16,272},{32,288},{48,304},{64,320},{80,336},{96,352},{112... | collective-permute-start | bytes 1572872 | tf_op jit(solution)/shard_map/ppermute | solution.py:208
  38.4 16.1 %collective-permute-start.3 = (bf16[4,512,128]{2,1,0:T(8,128)(2,1)S(1)}, bf16[4,512,128]{2,1,0:T(8,128)(2,1)S(1)}, u32[]{:S(2)}, u32[]{:S(2)}) collective-permute-start(bf16[4,512,128]{2,1,0:T(8,128)(2,1)S(1)} %select_select_fusion), channel_id=1, source_target_pairs={{0,96},{16,112},{32,64},{48,80},{64,32},{80,48},{96,0},{112,16},{1... | collective-permute-start | bytes 1572872 | tf_op jit(solution)/shard_map/ppermute | solution.py:208
  41.0 14.1 %collective-permute-start.5 = (bf16[4,512,128]{2,1,0:T(8,128)(2,1)S(1)}, bf16[4,512,128]{2,1,0:T(8,128)(2,1)S(1)}, u32[]{:S(2)}, u32[]{:S(2)}) collective-permute-start(bf16[4,512,128]{2,1,0:T(8,128)(2,1)S(1)} %collective-permute-done.4.refs_4_), channel_id=1, source_target_pairs={{0,128},{16,144},{32,160},{48,176},{128,256},{144,272},{160,288},{... | collective-permute-start | bytes 1572872 | tf_op jit(solution)/shard_map/ppermute | solution.py:208
  90.8 7.5 %collective-permute-start.8 = (bf16[16,64,128]{2,1,0:T(8,128)(2,1)S(1)}, bf16[16,64,128]{2,1,0:T(8,128)(2,1)S(1)}, u32[]{:S(2)}, u32[]{:S(2)}) collective-permute-start(bf16[16,64,128]{2,1,0:T(8,128)(2,1)S(1)} %all_to_all.5.own_ref), channel_id=1, source_target_pairs={{0,32},{16,48},{32,0},{48,16},{64,96},{80,112},{96,64},{112,80},{1... | collective-permute-start | bytes 786440 | tf_op jit(solution)/shard_map/ppermute | solution.py:208
  100.8 2.5 %copy-start = (bf16[2048,1280]{1,0:T(8,128)(2,1)S(1)}, bf16[2048,1280]{1,0:T(8,128)(2,1)}, u32[]{:S(2)}) copy-start(bf16[2048,1280]{1,0:T(8,128)(2,1)} %all-gather.2.cloned.1.call-done.w_ref) | copy-start | bytes 15728644
  104.1 14.1 %collective-permute-start.10 = (bf16[32,1280]{1,0:T(8,128)(2,1)S(1)}, bf16[32,1280]{1,0:T(8,128)(2,1)S(1)}, u32[]{:S(2)}, u32[]{:S(2)}) collective-permute-start(bf16[32,1280]{1,0:T(8,128)(2,1)S(1)} %get-tuple-element.29), channel_id=1, source_target_pairs={{0,32},{16,48},{32,0},{48,16},{64,96},{80,112},{96,64},{112,80},{1... | collective-permute-start | bytes 245768 | tf_op jit(solution)/shard_map/ppermute | solution.py:208
  107.1 11.8 %collective-permute-start.11 = (bf16[32,1280]{1,0:T(8,128)(2,1)S(1)}, bf16[32,1280]{1,0:T(8,128)(2,1)S(1)}, u32[]{:S(2)}, u32[]{:S(2)}) collective-permute-start(bf16[32,1280]{1,0:T(8,128)(2,1)S(1)} %get-tuple-element.30), channel_id=1, source_target_pairs={{0,48},{16,32},{32,16},{48,0},{64,112},{80,96},{96,80},{112,64},{1... | collective-permute-start | bytes 245768 | tf_op jit(solution)/shard_map/ppermute | solution.py:208
  116.2 3.2 %collective-permute-start.9 = (bf16[32,1280]{1,0:T(8,128)(2,1)S(1)}, bf16[32,1280]{1,0:T(8,128)(2,1)S(1)}, u32[]{:S(2)}, u32[]{:S(2)}) collective-permute-start(bf16[32,1280]{1,0:T(8,128)(2,1)S(1)} %get-tuple-element.28), channel_id=1, source_target_pairs={{0,16},{16,0},{32,48},{48,32},{64,80},{80,64},{96,112},{112,96},{1... | collective-permute-start | bytes 245768 | tf_op jit(solution)/shard_map/ppermute | solution.py:208
Sparse Core Ops, SparseCore 0:
  9.4 91.2 all-gather.1

commit v7 on v6

--- a/solution.py
+++ b/solution.py
@@ -13,7 +13,10 @@
 FT = 512
 NB = 4
 ROWS = 32
+FRAMES = ("x", "y", "core")
+HEADS = ("high", "low")
 TILE = 256
+CORE = 7
 DOUT = 2560
 HIDDEN = -1e30
 SCALE = math.log2(math.e) / math.sqrt(HD)
@@ -91,7 +94,9 @@
                 attended = (part / denom).astype(jnp.bfloat16)
                 chunk = (tile * blocks + a) * (BLK // ROWS)
                 for i in range(BLK // ROWS):
-                    outs[0][chunk + i, frame] = attended[i * ROWS : (i + 1) * ROWS]
+                    outs[0][frame ^ info_ref[CORE], chunk + i] = attended[
+                        i * ROWS : (i + 1) * ROWS
+                    ]
             else:
                 outs[0][frame, places[a], :] = peaks[a]
                 outs[1][frame, places[a], :] = totals[a]
@@ -116,7 +121,7 @@
     first = state is None
     held = jax.ShapeDtypeStruct((2, FT, HD), jnp.float32)
     if last:
-        out_shape = (jax.ShapeDtypeStruct((FT // ROWS, 2, ROWS, HD), jnp.bfloat16),)
+        out_shape = (jax.ShapeDtypeStruct((2, FT // ROWS, ROWS, HD), jnp.bfloat16),)
     else:
         out_shape = (held,) * 3
     vmem = pl.BlockSpec(memory_space=pltpu.VMEM)
@@ -138,32 +143,31 @@
     return out[0] if last else out
 
 
-def product_kernel(own_ref, far_ref, w_ref, *out_refs):
-    rows = [
-        jnp.concatenate([ref[z] for z in range(ref.shape[0])], axis=1)
-        for ref in (own_ref, far_ref)
-    ]
-    total = jnp.dot(
-        jnp.concatenate(rows, axis=0), w_ref[...], preferred_element_type=jnp.float32
-    ).astype(jnp.bfloat16)
-    for k, out in enumerate(out_refs):
-        out[...] = total[k * ROWS : (k + 1) * ROWS]
-
-
-def product(own, far, weight):
+def product_kernel(low_ref, rows_ref, w_ref, same_ref, other_ref, part_ref):
+    rows = jnp.concatenate([rows_ref[n] for n in range(rows_ref.shape[0])], axis=1)
+    part_ref[...] = jnp.dot(rows, w_ref[...], preferred_element_type=jnp.float32).astype(
+        jnp.bfloat16
+    )
+    for k, out in enumerate((same_ref, other_ref)):
+        start = pl.multiple_of((low_ref[0] ^ k) * ROWS, ROWS)
+        out[...] = part_ref[pl.ds(start, ROWS), :]
+
+
+def product(low, rows, weight):
+    vmem = pl.BlockSpec(memory_space=pltpu.VMEM)
     depth, width = weight.shape
-    vmem = pl.BlockSpec(memory_space=pltpu.VMEM)
-    part = jax.ShapeDtypeStruct((ROWS, width), own.dtype)
+    part = jax.ShapeDtypeStruct((ROWS, width), weight.dtype)
     return pl.pallas_call(
         product_kernel,
-        out_shape=(part,) * 4,
-        in_specs=[vmem] * 3,
-        out_specs=(vmem,) * 4,
+        out_shape=(part,) * 2,
+        in_specs=[pl.BlockSpec(memory_space=pltpu.SMEM)] + [vmem] * 2,
+        out_specs=(vmem,) * 2,
+        scratch_shapes=[pltpu.VMEM((2 * ROWS, width), weight.dtype)],
         compiler_params=pltpu.CompilerParams(vmem_limit_bytes=NARROW),
         cost_estimate=pl.CostEstimate(
-            flops=8 * ROWS * depth * width, bytes_accessed=depth * width * 2, transcendentals=0
+            flops=4 * ROWS * depth * width, bytes_accessed=depth * width * 2, transcendentals=0
         ),
-    )(own, far, weight)
+    )(low, rows, weight)
 
 
 def add_kernel(side_ref, own_ref, got_ref, far_ref, far_other_ref, out_ref):
@@ -179,7 +183,7 @@
     add(1 - side, far_ref, far_other_ref)
 
 
-def add_cores(side, own, got, far, far_other):
+def add_halves(side, own, got, far, far_other):
     vmem = pl.BlockSpec(memory_space=pltpu.VMEM)
     return pl.pallas_call(
         add_kernel,
@@ -191,7 +195,7 @@
 
 
 def shards(queries, keys, values, block_mask, out_weight):
-    me = lax.axis_index("tm")
+    me = lax.axis_index(FRAMES)
     core = me & 1
     y = (me >> 1) & 3
     x = me >> 3
@@ -205,13 +209,21 @@
         return pairs
 
     def send(array, pairs):
-        return lax.ppermute(array, "tm", pairs)
+        return lax.ppermute(array, FRAMES, pairs)
+
+    first_core, first_side = core == 0, (y & 1) == 0
+
+    def corner(row, column):
+        return out_weight[row * HD : (row + 1) * HD, column * half : (column + 1) * half]
 
     half = DOUT // 2
-    weight = lax.dynamic_slice(out_weight, (core * HD, (y & 1) * half), (HD, half))
-    first_core = core == 0
+    weight = jnp.where(
+        first_core,
+        jnp.where(first_side, corner(0, 0), corner(0, 1)),
+        jnp.where(first_side, corner(1, 0), corner(1, 1)),
+    )
     weight, first_core = lax.optimization_barrier((weight, first_core))
-    weight = lax.all_gather(weight, "head", axis=0, tiled=True)
+    weight = lax.all_gather(weight, ("core", "high"), axis=0, tiled=True)
 
     def head(array, low):
         return jnp.where(low, array[:, :HD], array[:, HD:])
@@ -251,6 +263,7 @@
             row_cross.astype(jnp.int32),
             has_above.astype(jnp.int32),
             has_below.astype(jnp.int32),
+            core,
         ]
     ).astype(jnp.int32)
     mask = jnp.transpose(block_mask, (1, 2, 0))
@@ -285,21 +298,30 @@
     )
 
     rows = lax.all_to_all(
-        attended.reshape(FT // ROWS, 2 * ROWS, HD), "head", 0, 0, tiled=True
+        attended.reshape(FT // ROWS, 2 * ROWS, HD), ("core", "high"), 0, 0, tiled=True
     )
     pair = [(i, i ^ 2) for i in range(32)]
-    own, yours, far, far_yours = product(rows, send(rows, pair), weight)
-    far = send(far, pair)
-    far_other = send(far_yours, [(i, i ^ 3) for i in range(32)])
-    got = send(yours, swap)
-    return add_cores((y & 1).reshape(1), own, got, far, far_other)
+    low = lax.axis_index("low").reshape(1)
+    far_rows = send(rows, pair)
+    own, beside_z = product(low, rows, weight)
+    got = lax.ppermute(beside_z, "low", [(0, 1), (1, 0)])
+    far_rows, own = lax.optimization_barrier((far_rows, own))
+    far, far_beside = product(low, far_rows, weight)
+    far, got = lax.optimization_barrier((far, got))
+    got_far = send(far, pair)
+    both = [(2 * i + k, 2 * (i ^ 2) + (k ^ 1)) for i in range(32) for k in range(2)]
+    got_far_other = lax.ppermute(far_beside, FRAMES + ("low",), both)
+    return add_halves((y & 1).reshape(1), own, got, got_far, got_far_other)
 
 
 def solution(mesh):
+    devices = mesh.devices.reshape(4, 4, 2, 8, 2)
+    mesh = jax.sharding.Mesh(devices, FRAMES + HEADS)
+    split = P(FRAMES, HEADS)
     return jax.shard_map(
         shards,
         mesh=mesh,
-        in_specs=(P("tm", "head"), P("tm", "head"), P("tm", "head"), P(), P("head", None)),
-        out_specs=P(("tm", "head"), None),
+        in_specs=(split, split, split, P(), P(HEADS, None)),
+        out_specs=P(FRAMES + HEADS, None),
         check_vma=False,
     )

time: 128 us -> 126 us (0.984)
  blocking collectives: 32.4 us -> 41.3 us
  starting transfers between devices: 43.3 us -> 37.8 us
  waiting for transfers between devices: 15.1 us -> 11.8 us
  other arithmetic: 4.35 us -> 2.47 us
  local copies, waits for them, and re-layouts: 4.37 us -> 2.62 us
  Pallas kernels: 13.8 us -> 15.1 us
    all_to_all x1, blocking collectives: 32.4 us -> 41.3 us  [shards(): lax.all_to_all(attended.reshape(FT // ROWS, 2 * ROWS, HD), ('core', 'high...]
    ppermute x12, starting transfers between devices: 43.3 us -> 37.8 us  [the longest x10 31.3 us: send(): return lax.ppermute(array, FRAMES, pairs)]
    select_n x0 -> x1, other arithmetic: none -> 2.14 us  [shards(): jnp.where(first_core, jnp.where(first_side, corner(0, 0), corner(0, 1)),...]
    all_gather x1, waiting for transfers between devices: 2.4 us -> 0.27 us  [shards(): weight = lax.all_gather(weight, ('core', 'high'), axis=0, tiled=True)]
    another operation x3, other arithmetic: 2.16 us -> 0.11 us  [shards(): jnp.stack([head(array, ~first_core) for array in (keys, values, queries)])]
    another operation x2, other arithmetic: 1.97 us -> 0.04 us  [shards(): local = jnp.concatenate([jnp.stack([k_own, v_own]), got[:2]], axis=0)]
    dynamic_slice x1 -> x0, local copies, waits for them, and re-layouts: 1.76 us -> none  [shards(): lax.dynamic_slice(out_weight, (core * HD, (y & 1) * half), (HD, half))]
    pallas_call x2 -> x3, Pallas kernels: 1.56 us -> 2.82 us  [the longest x2 2.11 us: product(): pl.pallas_call(product_kernel, out_shape=(part,) * 2, in_specs=[pl.BlockS...]
  transfers between devices with their start and end apart: 13 -> 13, of which waited for: 9 -> 9; matrix products, arithmetic and copies ran while one was open for 4% -> 0% of each run, Pallas kernels for 10% -> 11%
where the time goes in v7:
time: 126 us; the launch traced here: 125 us
  blocking collectives  41.3 us (33%)
  starting transfers between devices  37.8 us (30%)
  Pallas kernels  15.1 us (12%)
  between operations  13.7 us (11%)
  waiting for transfers between devices  11.8 us (9%)
  local copies, waits for them, and re-layouts  2.62 us (2%)
  other arithmetic  2.47 us (2%)
    all_to_all x1, blocking collectives, shards(): lax.all_to_all(attended.reshape(FT // ROWS, 2 * ROWS, HD), ('core', 'high...  41.3 us
    ppermute x10, starting transfers between devices, send(): return lax.ppermute(array, FRAMES, pairs)  31.3 us
    pallas_call x3, Pallas kernels, attend(): pl.pallas_call(functools.partial(attend_kernel, sources, split, len(kvs),...  12.2 us
    ppermute x10, waiting for transfers between devices, send(): return lax.ppermute(array, FRAMES, pairs)  10.6 us
    ppermute x1, starting transfers between devices, shards(): got = lax.ppermute(beside_z, 'low', [(0, 1), (1, 0)])  3.4 us
    ppermute x1, starting transfers between devices, shards(): got_far_other = lax.ppermute(far_beside, FRAMES + ('low',), both)  3.07 us
  transfers between devices with their start and end apart: 13, of which 9 were waited for; matrix products, arithmetic and copies ran while one was open for 0% of the time, Pallas kernels for 11%

profile of v7, /device:TPU:1, one launch (start us, length us, event | category | flops | bytes accessed | tf_op | source)
XLA Modules:
  0.0 124.8 jit_solution(1594884060907862147)
XLA Ops:
  6.5 0.0 copy-start.3
  6.5 0.0 copy-start.5
  6.5 0.0 copy-start.4
  6.5 0.0 all-gather.2.cloned.1.call-start
  6.5 2.1 %select_select_fusion.1 = bf16[128,1280]{1,0:T(8,128)(2,1)} fusion(bf16[256,2560]{1,0:T(8,128)(2,1)} %param.9, pred[]{:T(512)S(6)} %eq.22, pred[]{:T(512)S(6)} %eq.21), kind=kLoop, calls=%fused_computation.3 | loop fusion | flops 491520 | bytes 1638402 | tf_op jit(solution)/shard_map/jit(_where)/select_n | solution.py:220
  8.7 0.0 all-gather.2.cloned.1.call-update
  8.7 0.0 copy-done.3
  8.8 0.0 copy-done.5
  8.8 0.0 copy-done.4
  8.9 8.8 %collective-permute-start = (bf16[3,512,128]{2,1,0:T(8,128)(2,1)S(1)}, bf16[3,512,128]{2,1,0:T(8,128)(2,1)S(1)}, u32[]{:S(2)}, u32[]{:S(2)}) collective-permute-start(bf16[3,512,128]{2,1,0:T(8,128)(2,1)S(1)} %pad_maximum_fusion.1), channel_id=1, source_target_pairs={{0,16},{16,0},{32,48},{48,32},{64,80},{80,64},{96,112},{112,96},{1... | collective-permute-start | bytes 1179656 | tf_op jit(solution)/shard_map/ppermute | solution.py:212
  17.7 1.3 %collective-permute-done = bf16[3,512,128]{2,1,0:T(8,128)(2,1)S(1)} collective-permute-done((bf16[3,512,128]{2,1,0:T(8,128)(2,1)S(1)}, bf16[3,512,128]{2,1,0:T(8,128)(2,1)S(1)}, u32[]{:S(2)}, u32[]{:S(2)}) %collective-permute-start) | collective-permute-done | bytes 393248 | tf_op jit(solution)/shard_map/ppermute | solution.py:212
  19.0 0.1 pad_maximum_fusion.refs_3_
  19.1 1.3 %collective-permute-start.1 = (bf16[4,512,128]{2,1,0:T(8,128)(2,1)S(1)}, bf16[4,512,128]{2,1,0:T(8,128)(2,1)S(1)}, u32[]{:S(2)}, u32[]{:S(2)}) collective-permute-start(bf16[4,512,128]{2,1,0:T(8,128)(2,1)S(1)} %pad_maximum_fusion.refs_3_), channel_id=1, source_target_pairs={{0,128},{16,144},{32,160},{48,176},{64,192},{80,208},{96,224},{112... | collective-permute-start | bytes 1572872 | tf_op jit(solution)/shard_map/ppermute | solution.py:212
  20.4 1.3 %collective-permute-start.2 = (bf16[4,512,128]{2,1,0:T(8,128)(2,1)S(1)}, bf16[4,512,128]{2,1,0:T(8,128)(2,1)S(1)}, u32[]{:S(2)}, u32[]{:S(2)}) collective-permute-start(bf16[4,512,128]{2,1,0:T(8,128)(2,1)S(1)} %pad_maximum_fusion.refs_3_), channel_id=1, source_target_pairs={{128,0},{144,16},{160,32},{176,48},{192,64},{208,80},{224,96},{240... | collective-permute-start | bytes 1572872 | tf_op jit(solution)/shard_map/ppermute | solution.py:212
  21.7 1.9 %collective-permute-start.4 = (bf16[4,512,128]{2,1,0:T(8,128)(2,1)S(1)}, bf16[4,512,128]{2,1,0:T(8,128)(2,1)S(1)}, u32[]{:S(2)}, u32[]{:S(2)}) collective-permute-start(bf16[4,512,128]{2,1,0:T(8,128)(2,1)S(1)} %pad_maximum_fusion.refs_3_), channel_id=1, source_target_pairs={{0,64},{16,80},{32,96},{48,112},{64,0},{80,16},{96,32},{112,48},{1... | collective-permute-start | bytes 1572872 | tf_op jit(solution)/shard_map/ppermute | solution.py:212
  23.7 0.1 stack.65.refs_0_
  23.8 0.0 copy-start.2
  23.8 2.0 %collective-permute-start.6 = (bf16[4,512,128]{2,1,0:T(8,128)(2,1)S(1)}, bf16[4,512,128]{2,1,0:T(8,128)(2,1)S(1)}, u32[]{:S(2)}, u32[]{:S(2)}) collective-permute-start(bf16[4,512,128]{2,1,0:T(8,128)(2,1)S(1)} %pad_maximum_fusion.refs_3_), channel_id=1, source_target_pairs={{0,32},{16,48},{32,0},{48,16},{64,96},{80,112},{96,64},{112,80},{1... | collective-permute-start | bytes 1572872 | tf_op jit(solution)/shard_map/ppermute | solution.py:212
  25.8 5.2 %collective-permute-start.7 = (bf16[4,512,128]{2,1,0:T(8,128)(2,1)S(1)}, bf16[4,512,128]{2,1,0:T(8,128)(2,1)S(1)}, u32[]{:S(2)}, u32[]{:S(2)}) collective-permute-start(bf16[4,512,128]{2,1,0:T(8,128)(2,1)S(1)} %pad_maximum_fusion.refs_3_), channel_id=1, source_target_pairs={{0,256},{16,272},{32,288},{48,304},{64,320},{80,336},{96,352},{112... | collective-permute-start | bytes 1572872 | tf_op jit(solution)/shard_map/ppermute | solution.py:212
  31.1 0.6 collective-permute-done.1.refs_5_
  31.6 3.9 %collective-permute-done.2.refs_6_ = bf16[4,512,128]{2,1,0:T(8,128)(2,1)S(1)} collective-permute-done((bf16[4,512,128]{2,1,0:T(8,128)(2,1)S(1)}, bf16[4,512,128]{2,1,0:T(8,128)(2,1)S(1)}, u32[]{:S(2)}, u32[]{:S(2)}) %collective-permute-start.2) | collective-permute-done | bytes 524320 | tf_op jit(solution)/shard_map/ppermute | solution.py:212
  35.5 0.1 select_select_fusion
  35.6 1.9 %collective-permute-start.3 = (bf16[4,512,128]{2,1,0:T(8,128)(2,1)S(1)}, bf16[4,512,128]{2,1,0:T(8,128)(2,1)S(1)}, u32[]{:S(2)}, u32[]{:S(2)}) collective-permute-start(bf16[4,512,128]{2,1,0:T(8,128)(2,1)S(1)} %select_select_fusion), channel_id=1, source_target_pairs={{0,96},{16,112},{32,64},{48,80},{64,32},{80,48},{96,0},{112,16},{1... | collective-permute-start | bytes 1572872 | tf_op jit(solution)/shard_map/ppermute | solution.py:212
  37.6 0.8 collective-permute-done.4.refs_4_
  38.4 3.7 %collective-permute-start.5 = (bf16[4,512,128]{2,1,0:T(8,128)(2,1)S(1)}, bf16[4,512,128]{2,1,0:T(8,128)(2,1)S(1)}, u32[]{:S(2)}, u32[]{:S(2)}) collective-permute-start(bf16[4,512,128]{2,1,0:T(8,128)(2,1)S(1)} %collective-permute-done.4.refs_4_), channel_id=1, source_target_pairs={{0,128},{16,144},{32,160},{48,176},{128,256},{144,272},{160,288},{... | collective-permute-start | bytes 1572872 | tf_op jit(solution)/shard_map/ppermute | solution.py:212
  42.1 0.0 copy-done.2
  42.1 3.2 %shard_map.55 = (f32[2,512,128]{2,1,0:T(8,128)S(1)}, f32[2,512,128]{2,1,0:T(8,128)S(1)}, f32[2,512,128]{2,1,0:T(8,128)S(1)}) custom-call(s32[8]{0:T(128)S(1)} %stack.65.refs_0_, s32[4,4,6]{2,1,0:T(4,128)S(1)} %bitcast.24, bf16[2,512,128]{2,1,0:T(8,128)(2,1)S(1)} %pad_maximum_fusion.2.refs_2_, bf16[4,512,128]{2,1,0:T(8,128)(2,1)S(1)} %pad_maximum_fusion.refs_3_), custom_call_target="tpu_custom_call" | custom-call | flops 536870912 | bytes 524288 | tf_op jit(solution)/shard_map/pallas_call | solution.py:131
  45.3 0.8 collective-permute-done.6.refs_3_
  46.1 0.0 collective-permute-done.7.refs_7_
  46.1 5.7 %shard_map.56 = (f32[2,512,128]{2,1,0:T(8,128)S(1)}, f32[2,512,128]{2,1,0:T(8,128)S(1)}, f32[2,512,128]{2,1,0:T(8,128)S(1)}) custom-call(s32[8]{0:T(128)S(1)} %stack.65.refs_0_, s32[4,4,6]{2,1,0:T(4,128)S(1)} %bitcast.25, bf16[2,512,128]{2,1,0:T(8,128)(2,1)S(1)} %pad_maximum_fusion.2.refs_2_, bf16[4,512,128]{2,1,0:T(8,128)(2,1)S(1)} %collective-permute-done.6.refs_3_, ...), custom_call_target="tpu_custom_call" | custom-call | flops 1476395008 | bytes 2621440 | tf_op jit(solution)/shard_map/pallas_call | solution.py:131
  51.8 0.0 collective-permute-done.3.refs_3_
  51.8 0.5 collective-permute-done.5.refs_4_
  52.3 3.4 %shard_map.57 = bf16[2,16,32,128]{3,2,1,0:T(8,128)(2,1)S(1)} custom-call(s32[8]{0:T(128)S(1)} %stack.65.refs_0_, s32[4,4,6]{2,1,0:T(4,128)S(1)} %bitcast.26, bf16[2,512,128]{2,1,0:T(8,128)(2,1)S(1)} %pad_maximum_fusion.2.refs_2_, bf16[4,512,128]{2,1,0:T(8,128)(2,1)S(1)} %collective-permute-done.3.refs_3_, ...), custom_call_target="tpu_custom_call" | custom-call | flops 671088640 | bytes 1048576 | tf_op jit(solution)/shard_map/pallas_call | solution.py:131
  55.8 41.3 %all_to_all.5.rows_ref = bf16[16,64,128]{2,1,0:T(8,128)(2,1)S(1)} all-to-all(bf16[16,64,128]{2,1,0:T(8,128)(2,1)S(1)} %bitcast.23), channel_id=1, replica_groups=mesh['x'=4,'y'=4,'core'=2,'high'=8,'low'=2] {'core','high'}, dimensions={0} | all-to-all | bytes 524288 | tf_op jit(solution)/shard_map/all_to_all | solution.py:300
  97.1 3.0 %collective-permute-start.8 = (bf16[16,64,128]{2,1,0:T(8,128)(2,1)S(1)}, bf16[16,64,128]{2,1,0:T(8,128)(2,1)S(1)}, u32[]{:S(2)}, u32[]{:S(2)}) collective-permute-start(bf16[16,64,128]{2,1,0:T(8,128)(2,1)S(1)} %all_to_all.5.rows_ref), channel_id=1, source_target_pairs={{0,32},{16,48},{32,0},{48,16},{64,96},{80,112},{96,64},{112,80},{1... | collective-permute-start | bytes 786440 | tf_op jit(solution)/shard_map/ppermute | solution.py:212
  100.1 0.3 all-gather.2.cloned.1.call-done.w_ref
  100.4 0.0 copy-start
  100.4 2.5 %copy-done = bf16[2048,1280]{1,0:T(8,128)(2,1)S(1)} copy-done((bf16[2048,1280]{1,0:T(8,128)(2,1)S(1)}, bf16[2048,1280]{1,0:T(8,128)(2,1)}, u32[]{:S(2)}) %copy-start) | copy-done | bytes 5242904
  102.9 0.0 copy-start.1
  102.9 1.1 shard_map.58
  103.9 3.4 %collective-permute-start.9 = (bf16[32,1280]{1,0:T(8,128)(2,1)S(1)}, bf16[32,1280]{1,0:T(8,128)(2,1)S(1)}, u32[]{:S(2)}, u32[]{:S(2)}) collective-permute-start(bf16[32,1280]{1,0:T(8,128)(2,1)S(1)} %get-tuple-element.35), channel_id=1, source_target_pairs={{0,1},{1,0},{2,3},{3,2},{4,5},{5,4},{6,7},{7,6},{8,9},{9,8},{10,11... | collective-permute-start | bytes 245768 | tf_op jit(solution)/shard_map/ppermute | solution.py:307
  107.3 0.0 collective-permute-done.8.rows_ref
  107.4 0.0 copy-done.1
  107.4 1.1 shard_map.59
  108.4 3.1 %collective-permute-start.11 = (bf16[32,1280]{1,0:T(8,128)(2,1)S(1)}, bf16[32,1280]{1,0:T(8,128)(2,1)S(1)}, u32[]{:S(2)}, u32[]{:S(2)}) collective-permute-start(bf16[32,1280]{1,0:T(8,128)(2,1)S(1)} %get-tuple-element.38), channel_id=1, source_target_pairs={{0,33},{1,32},{16,49},{17,48},{32,1},{33,0},{48,17},{49,16},{64,97... | collective-permute-start | bytes 245768 | tf_op jit(solution)/shard_map/ppermute | solution.py:313
  111.5 0.0 collective-permute-done.9.got_ref
  111.5 2.1 %collective-permute-start.10 = (bf16[32,1280]{1,0:T(8,128)(2,1)S(1)}, bf16[32,1280]{1,0:T(8,128)(2,1)S(1)}, u32[]{:S(2)}, u32[]{:S(2)}) collective-permute-start(bf16[32,1280]{1,0:T(8,128)(2,1)S(1)} %get-tuple-element.37), channel_id=1, source_target_pairs={{0,32},{16,48},{32,0},{48,16},{64,96},{80,112},{96,64},{112,80},{1... | collective-permute-start | bytes 245768 | tf_op jit(solution)/shard_map/ppermute | solution.py:212
  113.6 0.9 collective-permute-done.11.far_other_ref
  114.5 2.7 %collective-permute-done.10.far_ref = bf16[32,1280]{1,0:T(8,128)(2,1)S(1)} collective-permute-done((bf16[32,1280]{1,0:T(8,128)(2,1)S(1)}, bf16[32,1280]{1,0:T(8,128)(2,1)S(1)}, u32[]{:S(2)}, u32[]{:S(2)}) %collective-permute-start.10) | collective-permute-done | bytes 81952 | tf_op jit(solution)/shard_map/ppermute | solution.py:212
  117.2 0.7 shard_map.60
  (9 shorter events, 0.2 us)
Async XLA Ops:
  6.5 2.2 %copy-start.3 = (bf16[512,256]{1,0:T(8,128)(2,1)S(1)}, bf16[512,256]{1,0:T(8,128)(2,1)}, u32[]{:S(2)}) copy-start(bf16[512,256]{1,0:T(8,128)(2,1)} %param.6) | copy-start | bytes 786436
  6.5 2.2 %copy-start.5 = (bf16[512,256]{1,0:T(8,128)(2,1)S(1)}, bf16[512,256]{1,0:T(8,128)(2,1)}, u32[]{:S(2)}) copy-start(bf16[512,256]{1,0:T(8,128)(2,1)} %param.5) | copy-start | bytes 786436
  6.5 2.2 %copy-start.4 = (bf16[512,256]{1,0:T(8,128)(2,1)S(1)}, bf16[512,256]{1,0:T(8,128)(2,1)}, u32[]{:S(2)}) copy-start(bf16[512,256]{1,0:T(8,128)(2,1)} %param.7) | copy-start | bytes 786436
  6.5 93.8 %all-gather.2.cloned.1.call-start = ((), (), s32[]{:S(2)}) async-start(), calls=%async_computation.1 | async-start | bytes 5570560 | tf_op jit(solution)/shard_map/all_gather | solution.py:226
  8.9 10.1 %collective-permute-start = (bf16[3,512,128]{2,1,0:T(8,128)(2,1)S(1)}, bf16[3,512,128]{2,1,0:T(8,128)(2,1)S(1)}, u32[]{:S(2)}, u32[]{:S(2)}) collective-permute-start(bf16[3,512,128]{2,1,0:T(8,128)(2,1)S(1)} %pad_maximum_fusion.1), channel_id=1, source_target_pairs={{0,16},{16,0},{32,48},{48,32},{64,80},{80,64},{96,112},{112,96},{1... | collective-permute-start | bytes 1179656 | tf_op jit(solution)/shard_map/ppermute | solution.py:212
  19.1 12.5 %collective-permute-start.1 = (bf16[4,512,128]{2,1,0:T(8,128)(2,1)S(1)}, bf16[4,512,128]{2,1,0:T(8,128)(2,1)S(1)}, u32[]{:S(2)}, u32[]{:S(2)}) collective-permute-start(bf16[4,512,128]{2,1,0:T(8,128)(2,1)S(1)} %pad_maximum_fusion.refs_3_), channel_id=1, source_target_pairs={{0,128},{16,144},{32,160},{48,176},{64,192},{80,208},{96,224},{112... | collective-permute-start | bytes 1572872 | tf_op jit(solution)/shard_map/ppermute | solution.py:212
  20.4 15.1 %collective-permute-start.2 = (bf16[4,512,128]{2,1,0:T(8,128)(2,1)S(1)}, bf16[4,512,128]{2,1,0:T(8,128)(2,1)S(1)}, u32[]{:S(2)}, u32[]{:S(2)}) collective-permute-start(bf16[4,512,128]{2,1,0:T(8,128)(2,1)S(1)} %pad_maximum_fusion.refs_3_), channel_id=1, source_target_pairs={{128,0},{144,16},{160,32},{176,48},{192,64},{208,80},{224,96},{240... | collective-permute-start | bytes 1572872 | tf_op jit(solution)/shard_map/ppermute | solution.py:212
  21.7 16.6 %collective-permute-start.4 = (bf16[4,512,128]{2,1,0:T(8,128)(2,1)S(1)}, bf16[4,512,128]{2,1,0:T(8,128)(2,1)S(1)}, u32[]{:S(2)}, u32[]{:S(2)}) collective-permute-start(bf16[4,512,128]{2,1,0:T(8,128)(2,1)S(1)} %pad_maximum_fusion.refs_3_), channel_id=1, source_target_pairs={{0,64},{16,80},{32,96},{48,112},{64,0},{80,16},{96,32},{112,48},{1... | collective-permute-start | bytes 1572872 | tf_op jit(solution)/shard_map/ppermute | solution.py:212
  23.8 18.4 %copy-start.2 = (s32[6,4,4]{0,2,1:T(4,128)S(1)}, s32[6,4,4]{0,2,1:T(4,128)}, u32[]{:S(2)}) copy-start(s32[6,4,4]{0,2,1:T(4,128)} %param.8) | copy-start | bytes 1156
  23.8 22.3 %collective-permute-start.6 = (bf16[4,512,128]{2,1,0:T(8,128)(2,1)S(1)}, bf16[4,512,128]{2,1,0:T(8,128)(2,1)S(1)}, u32[]{:S(2)}, u32[]{:S(2)}) collective-permute-start(bf16[4,512,128]{2,1,0:T(8,128)(2,1)S(1)} %pad_maximum_fusion.refs_3_), channel_id=1, source_target_pairs={{0,32},{16,48},{32,0},{48,16},{64,96},{80,112},{96,64},{112,80},{1... | collective-permute-start | bytes 1572872 | tf_op jit(solution)/shard_map/ppermute | solution.py:212
  25.8 20.3 %collective-permute-start.7 = (bf16[4,512,128]{2,1,0:T(8,128)(2,1)S(1)}, bf16[4,512,128]{2,1,0:T(8,128)(2,1)S(1)}, u32[]{:S(2)}, u32[]{:S(2)}) collective-permute-start(bf16[4,512,128]{2,1,0:T(8,128)(2,1)S(1)} %pad_maximum_fusion.refs_3_), channel_id=1, source_target_pairs={{0,256},{16,272},{32,288},{48,304},{64,320},{80,336},{96,352},{112... | collective-permute-start | bytes 1572872 | tf_op jit(solution)/shard_map/ppermute | solution.py:212
  35.6 16.1 %collective-permute-start.3 = (bf16[4,512,128]{2,1,0:T(8,128)(2,1)S(1)}, bf16[4,512,128]{2,1,0:T(8,128)(2,1)S(1)}, u32[]{:S(2)}, u32[]{:S(2)}) collective-permute-start(bf16[4,512,128]{2,1,0:T(8,128)(2,1)S(1)} %select_select_fusion), channel_id=1, source_target_pairs={{0,96},{16,112},{32,64},{48,80},{64,32},{80,48},{96,0},{112,16},{1... | collective-permute-start | bytes 1572872 | tf_op jit(solution)/shard_map/ppermute | solution.py:212
  38.4 14.0 %collective-permute-start.5 = (bf16[4,512,128]{2,1,0:T(8,128)(2,1)S(1)}, bf16[4,512,128]{2,1,0:T(8,128)(2,1)S(1)}, u32[]{:S(2)}, u32[]{:S(2)}) collective-permute-start(bf16[4,512,128]{2,1,0:T(8,128)(2,1)S(1)} %collective-permute-done.4.refs_4_), channel_id=1, source_target_pairs={{0,128},{16,144},{32,160},{48,176},{128,256},{144,272},{160,288},{... | collective-permute-start | bytes 1572872 | tf_op jit(solution)/shard_map/ppermute | solution.py:212
  97.1 10.2 %collective-permute-start.8 = (bf16[16,64,128]{2,1,0:T(8,128)(2,1)S(1)}, bf16[16,64,128]{2,1,0:T(8,128)(2,1)S(1)}, u32[]{:S(2)}, u32[]{:S(2)}) collective-permute-start(bf16[16,64,128]{2,1,0:T(8,128)(2,1)S(1)} %all_to_all.5.rows_ref), channel_id=1, source_target_pairs={{0,32},{16,48},{32,0},{48,16},{64,96},{80,112},{96,64},{112,80},{1... | collective-permute-start | bytes 786440 | tf_op jit(solution)/shard_map/ppermute | solution.py:212
  100.4 2.5 %copy-start = (bf16[2048,1280]{1,0:T(8,128)(2,1)S(1)}, bf16[2048,1280]{1,0:T(8,128)(2,1)}, u32[]{:S(2)}) copy-start(bf16[2048,1280]{1,0:T(8,128)(2,1)} %all-gather.2.cloned.1.call-done.w_ref) | copy-start | bytes 15728644
  102.9 4.5 %copy-start.1 = (bf16[2048,1280]{1,0:T(8,128)(2,1)S(1)}, bf16[2048,1280]{1,0:T(8,128)(2,1)}, u32[]{:S(2)}) copy-start(bf16[2048,1280]{1,0:T(8,128)(2,1)} %all-gather.2.cloned.1.call-done.w_ref) | copy-start | bytes 15728644
  103.9 7.6 %collective-permute-start.9 = (bf16[32,1280]{1,0:T(8,128)(2,1)S(1)}, bf16[32,1280]{1,0:T(8,128)(2,1)S(1)}, u32[]{:S(2)}, u32[]{:S(2)}) collective-permute-start(bf16[32,1280]{1,0:T(8,128)(2,1)S(1)} %get-tuple-element.35), channel_id=1, source_target_pairs={{0,1},{1,0},{2,3},{3,2},{4,5},{5,4},{6,7},{7,6},{8,9},{9,8},{10,11... | collective-permute-start | bytes 245768 | tf_op jit(solution)/shard_map/ppermute | solution.py:307
  108.4 6.1 %collective-permute-start.11 = (bf16[32,1280]{1,0:T(8,128)(2,1)S(1)}, bf16[32,1280]{1,0:T(8,128)(2,1)S(1)}, u32[]{:S(2)}, u32[]{:S(2)}) collective-permute-start(bf16[32,1280]{1,0:T(8,128)(2,1)S(1)} %get-tuple-element.38), channel_id=1, source_target_pairs={{0,33},{1,32},{16,49},{17,48},{32,1},{33,0},{48,17},{49,16},{64,97... | collective-permute-start | bytes 245768 | tf_op jit(solution)/shard_map/ppermute | solution.py:313
  111.5 5.7 %collective-permute-start.10 = (bf16[32,1280]{1,0:T(8,128)(2,1)S(1)}, bf16[32,1280]{1,0:T(8,128)(2,1)S(1)}, u32[]{:S(2)}, u32[]{:S(2)}) collective-permute-start(bf16[32,1280]{1,0:T(8,128)(2,1)S(1)} %get-tuple-element.37), channel_id=1, source_target_pairs={{0,32},{16,48},{32,0},{48,16},{64,96},{80,112},{96,64},{112,80},{1... | collective-permute-start | bytes 245768 | tf_op jit(solution)/shard_map/ppermute | solution.py:212
Sparse Core Ops, SparseCore 0:
  9.5 90.8 all-gather.1

commit v8 on v7

--- a/solution.py
+++ b/solution.py
@@ -286,16 +286,8 @@
         state,
         False,
     )
-    attended = attend(
-        info,
-        mask,
-        q,
-        [other, across_row],
-        [(0, False, 2, 3), (0, True, 1, 3), (1, False, 3, 4)],
-        1,
-        state,
-        True,
-    )
+    state = attend(info, mask, q, [other], [(0, False, 2, 3), (0, True, 1, 3)], 1, state, False)
+    attended = attend(info, mask, q, [across_row], [(0, False, 3, 4)], None, state, True)
 
     rows = lax.all_to_all(
         attended.reshape(FT // ROWS, 2 * ROWS, HD), ("core", "high"), 0, 0, tiled=True

time: 126 us -> 126 us (level)
  Pallas kernels: 15.1 us -> 16.8 us
  blocking collectives: 41.3 us -> 40 us
    pallas_call x3 -> x4, Pallas kernels: 12.2 us -> 14 us  [attend(): pl.pallas_call(functools.partial(attend_kernel, sources, split, len(kvs),...]
    all_to_all x1, blocking collectives: 41.3 us -> 40 us  [shards(): lax.all_to_all(attended.reshape(FT // ROWS, 2 * ROWS, HD), ('core', 'high...]
  transfers between devices with their start and end apart: 13 -> 13, of which waited for: 9 -> 8; matrix products, arithmetic and copies ran while one was open for 0% -> 0% of each run, Pallas kernels for 11% -> 13%
where the time goes in v8:
time: 126 us; the launch traced here: 125 us
  blocking collectives  40 us (32%)
  starting transfers between devices  38.5 us (31%)
  Pallas kernels  16.8 us (13%)
  between operations  13.7 us (11%)
  waiting for transfers between devices  10.9 us (9%)
  local copies, waits for them, and re-layouts  2.62 us (2%)
  other arithmetic  2.47 us (2%)
    all_to_all x1, blocking collectives, shards(): lax.all_to_all(attended.reshape(FT // ROWS, 2 * ROWS, HD), ('core', 'high...  40 us
    ppermute x10, starting transfers between devices, send(): return lax.ppermute(array, FRAMES, pairs)  31.1 us
    pallas_call x4, Pallas kernels, attend(): pl.pallas_call(functools.partial(attend_kernel, sources, split, len(kvs),...  14 us
    ppermute x10, waiting for transfers between devices, send(): return lax.ppermute(array, FRAMES, pairs)  9.95 us
    ppermute x1, starting transfers between devices, shards(): got = lax.ppermute(beside_z, 'low', [(0, 1), (1, 0)])  3.94 us
    ppermute x1, starting transfers between devices, shards(): got_far_other = lax.ppermute(far_beside, FRAMES + ('low',), both)  3.44 us
  transfers between devices with their start and end apart: 13, of which 8 were waited for; matrix products, arithmetic and copies ran while one was open for 0% of the time, Pallas kernels for 13%

profile of v8, /device:TPU:1, one launch (start us, length us, event | category | flops | bytes accessed | tf_op | source)
XLA Modules:
  0.0 125.0 jit_solution(14318639525399131967)
XLA Ops:
  6.5 0.0 copy-start.3
  6.5 0.0 copy-start.5
  6.5 0.0 copy-start.4
  6.5 0.0 all-gather.2.cloned.1.call-start
  6.5 2.1 %select_select_fusion.1 = bf16[128,1280]{1,0:T(8,128)(2,1)} fusion(bf16[256,2560]{1,0:T(8,128)(2,1)} %param.9, pred[]{:T(512)S(6)} %eq.22, pred[]{:T(512)S(6)} %eq.21), kind=kLoop, calls=%fused_computation.3 | loop fusion | flops 491520 | bytes 1638402 | tf_op jit(solution)/shard_map/jit(_where)/select_n | solution.py:220
  8.7 0.0 all-gather.2.cloned.1.call-update
  8.7 0.0 copy-done.3
  8.8 0.0 copy-done.5
  8.8 0.0 copy-done.4
  8.9 8.8 %collective-permute-start = (bf16[3,512,128]{2,1,0:T(8,128)(2,1)S(1)}, bf16[3,512,128]{2,1,0:T(8,128)(2,1)S(1)}, u32[]{:S(2)}, u32[]{:S(2)}) collective-permute-start(bf16[3,512,128]{2,1,0:T(8,128)(2,1)S(1)} %pad_maximum_fusion.1), channel_id=1, source_target_pairs={{0,16},{16,0},{32,48},{48,32},{64,80},{80,64},{96,112},{112,96},{1... | collective-permute-start | bytes 1179656 | tf_op jit(solution)/shard_map/ppermute | solution.py:212
  17.7 1.3 %collective-permute-done = bf16[3,512,128]{2,1,0:T(8,128)(2,1)S(1)} collective-permute-done((bf16[3,512,128]{2,1,0:T(8,128)(2,1)S(1)}, bf16[3,512,128]{2,1,0:T(8,128)(2,1)S(1)}, u32[]{:S(2)}, u32[]{:S(2)}) %collective-permute-start) | collective-permute-done | bytes 393248 | tf_op jit(solution)/shard_map/ppermute | solution.py:212
  19.0 0.1 pad_maximum_fusion.refs_3_
  19.1 1.3 %collective-permute-start.3 = (bf16[4,512,128]{2,1,0:T(8,128)(2,1)S(1)}, bf16[4,512,128]{2,1,0:T(8,128)(2,1)S(1)}, u32[]{:S(2)}, u32[]{:S(2)}) collective-permute-start(bf16[4,512,128]{2,1,0:T(8,128)(2,1)S(1)} %pad_maximum_fusion.refs_3_), channel_id=1, source_target_pairs={{0,128},{16,144},{32,160},{48,176},{64,192},{80,208},{96,224},{112... | collective-permute-start | bytes 1572872 | tf_op jit(solution)/shard_map/ppermute | solution.py:212
  20.4 1.3 %collective-permute-start.4 = (bf16[4,512,128]{2,1,0:T(8,128)(2,1)S(1)}, bf16[4,512,128]{2,1,0:T(8,128)(2,1)S(1)}, u32[]{:S(2)}, u32[]{:S(2)}) collective-permute-start(bf16[4,512,128]{2,1,0:T(8,128)(2,1)S(1)} %pad_maximum_fusion.refs_3_), channel_id=1, source_target_pairs={{128,0},{144,16},{160,32},{176,48},{192,64},{208,80},{224,96},{240... | collective-permute-start | bytes 1572872 | tf_op jit(solution)/shard_map/ppermute | solution.py:212
  21.7 1.9 %collective-permute-start.1 = (bf16[4,512,128]{2,1,0:T(8,128)(2,1)S(1)}, bf16[4,512,128]{2,1,0:T(8,128)(2,1)S(1)}, u32[]{:S(2)}, u32[]{:S(2)}) collective-permute-start(bf16[4,512,128]{2,1,0:T(8,128)(2,1)S(1)} %pad_maximum_fusion.refs_3_), channel_id=1, source_target_pairs={{0,64},{16,80},{32,96},{48,112},{64,0},{80,16},{96,32},{112,48},{1... | collective-permute-start | bytes 1572872 | tf_op jit(solution)/shard_map/ppermute | solution.py:212
  23.7 0.1 stack.65.refs_0_
  23.8 0.0 copy-start.2
  23.8 2.0 %collective-permute-start.6 = (bf16[4,512,128]{2,1,0:T(8,128)(2,1)S(1)}, bf16[4,512,128]{2,1,0:T(8,128)(2,1)S(1)}, u32[]{:S(2)}, u32[]{:S(2)}) collective-permute-start(bf16[4,512,128]{2,1,0:T(8,128)(2,1)S(1)} %pad_maximum_fusion.refs_3_), channel_id=1, source_target_pairs={{0,32},{16,48},{32,0},{48,16},{64,96},{80,112},{96,64},{112,80},{1... | collective-permute-start | bytes 1572872 | tf_op jit(solution)/shard_map/ppermute | solution.py:212
  25.8 5.2 %collective-permute-start.7 = (bf16[4,512,128]{2,1,0:T(8,128)(2,1)S(1)}, bf16[4,512,128]{2,1,0:T(8,128)(2,1)S(1)}, u32[]{:S(2)}, u32[]{:S(2)}) collective-permute-start(bf16[4,512,128]{2,1,0:T(8,128)(2,1)S(1)} %pad_maximum_fusion.refs_3_), channel_id=1, source_target_pairs={{0,256},{16,272},{32,288},{48,304},{64,320},{80,336},{96,352},{112... | collective-permute-start | bytes 1572872 | tf_op jit(solution)/shard_map/ppermute | solution.py:212
  31.1 0.6 collective-permute-done.3.refs_5_
  31.6 3.9 %collective-permute-done.4.refs_6_ = bf16[4,512,128]{2,1,0:T(8,128)(2,1)S(1)} collective-permute-done((bf16[4,512,128]{2,1,0:T(8,128)(2,1)S(1)}, bf16[4,512,128]{2,1,0:T(8,128)(2,1)S(1)}, u32[]{:S(2)}, u32[]{:S(2)}) %collective-permute-start.4) | collective-permute-done | bytes 524320 | tf_op jit(solution)/shard_map/ppermute | solution.py:212
  35.5 0.1 select_select_fusion
  35.6 1.9 %collective-permute-start.5 = (bf16[4,512,128]{2,1,0:T(8,128)(2,1)S(1)}, bf16[4,512,128]{2,1,0:T(8,128)(2,1)S(1)}, u32[]{:S(2)}, u32[]{:S(2)}) collective-permute-start(bf16[4,512,128]{2,1,0:T(8,128)(2,1)S(1)} %select_select_fusion), channel_id=1, source_target_pairs={{0,96},{16,112},{32,64},{48,80},{64,32},{80,48},{96,0},{112,16},{1... | collective-permute-start | bytes 1572872 | tf_op jit(solution)/shard_map/ppermute | solution.py:212
  37.6 0.8 collective-permute-done.1.refs_4_
  38.4 3.7 %collective-permute-start.2 = (bf16[4,512,128]{2,1,0:T(8,128)(2,1)S(1)}, bf16[4,512,128]{2,1,0:T(8,128)(2,1)S(1)}, u32[]{:S(2)}, u32[]{:S(2)}) collective-permute-start(bf16[4,512,128]{2,1,0:T(8,128)(2,1)S(1)} %collective-permute-done.1.refs_4_), channel_id=1, source_target_pairs={{0,128},{16,144},{32,160},{48,176},{128,256},{144,272},{160,288},{... | collective-permute-start | bytes 1572872 | tf_op jit(solution)/shard_map/ppermute | solution.py:212
  42.1 0.0 copy-done.2
  42.1 3.1 %shard_map.55 = (f32[2,512,128]{2,1,0:T(8,128)S(1)}, f32[2,512,128]{2,1,0:T(8,128)S(1)}, f32[2,512,128]{2,1,0:T(8,128)S(1)}) custom-call(s32[8]{0:T(128)S(1)} %stack.65.refs_0_, s32[4,4,6]{2,1,0:T(4,128)S(1)} %bitcast.24, bf16[2,512,128]{2,1,0:T(8,128)(2,1)S(1)} %pad_maximum_fusion.2.refs_2_, bf16[4,512,128]{2,1,0:T(8,128)(2,1)S(1)} %pad_maximum_fusion.refs_3_), custom_call_target="tpu_custom_call" | custom-call | flops 536870912 | bytes 524288 | tf_op jit(solution)/shard_map/pallas_call | solution.py:131
  45.3 0.8 collective-permute-done.6.refs_3_
  46.1 0.0 collective-permute-done.7.refs_7_
  46.1 5.7 %shard_map.56 = (f32[2,512,128]{2,1,0:T(8,128)S(1)}, f32[2,512,128]{2,1,0:T(8,128)S(1)}, f32[2,512,128]{2,1,0:T(8,128)S(1)}) custom-call(s32[8]{0:T(128)S(1)} %stack.65.refs_0_, s32[4,4,6]{2,1,0:T(4,128)S(1)} %bitcast.25, bf16[2,512,128]{2,1,0:T(8,128)(2,1)S(1)} %pad_maximum_fusion.2.refs_2_, bf16[4,512,128]{2,1,0:T(8,128)(2,1)S(1)} %collective-permute-done.6.refs_3_, ...), custom_call_target="tpu_custom_call" | custom-call | flops 1476395008 | bytes 2621440 | tf_op jit(solution)/shard_map/pallas_call | solution.py:131
  51.8 0.0 collective-permute-done.5.refs_3_
  51.8 2.6 %shard_map.57 = (f32[2,512,128]{2,1,0:T(8,128)S(1)}, f32[2,512,128]{2,1,0:T(8,128)S(1)}, f32[2,512,128]{2,1,0:T(8,128)S(1)}) custom-call(s32[8]{0:T(128)S(1)} %stack.65.refs_0_, s32[4,4,6]{2,1,0:T(4,128)S(1)} %bitcast.26, bf16[2,512,128]{2,1,0:T(8,128)(2,1)S(1)} %pad_maximum_fusion.2.refs_2_, bf16[4,512,128]{2,1,0:T(8,128)(2,1)S(1)} %collective-permute-done.5.refs_3_, ...), custom_call_target="tpu_custom_call" | custom-call | flops 402653184 | bytes 524288 | tf_op jit(solution)/shard_map/pallas_call | solution.py:131
  54.4 0.0 collective-permute-done.2.refs_3_
  54.4 2.6 %shard_map.58 = bf16[2,16,32,128]{3,2,1,0:T(8,128)(2,1)S(1)} custom-call(s32[8]{0:T(128)S(1)} %stack.65.refs_0_, s32[4,4,6]{2,1,0:T(4,128)S(1)} %bitcast.27, bf16[2,512,128]{2,1,0:T(8,128)(2,1)S(1)} %pad_maximum_fusion.2.refs_2_, bf16[4,512,128]{2,1,0:T(8,128)(2,1)S(1)} %collective-permute-done.2.refs_3_, f32[2,512,128]{2,1,0:T(8,128)S(1)} %get-tuple-element.33.refs_4_, ...), custom_call_target="tpu_custom_call" | custom-call | flops 268435456 | bytes 524288 | tf_op jit(solution)/shard_map/pallas_call | solution.py:131
  57.0 40.0 %all_to_all.5.rows_ref = bf16[16,64,128]{2,1,0:T(8,128)(2,1)S(1)} all-to-all(bf16[16,64,128]{2,1,0:T(8,128)(2,1)S(1)} %bitcast.23), channel_id=1, replica_groups=mesh['x'=4,'y'=4,'core'=2,'high'=8,'low'=2] {'core','high'}, dimensions={0} | all-to-all | bytes 524288 | tf_op jit(solution)/shard_map/all_to_all | solution.py:292
  97.0 2.7 %collective-permute-start.8 = (bf16[16,64,128]{2,1,0:T(8,128)(2,1)S(1)}, bf16[16,64,128]{2,1,0:T(8,128)(2,1)S(1)}, u32[]{:S(2)}, u32[]{:S(2)}) collective-permute-start(bf16[16,64,128]{2,1,0:T(8,128)(2,1)S(1)} %all_to_all.5.rows_ref), channel_id=1, source_target_pairs={{0,32},{16,48},{32,0},{48,16},{64,96},{80,112},{96,64},{112,80},{1... | collective-permute-start | bytes 786440 | tf_op jit(solution)/shard_map/ppermute | solution.py:212
  99.7 0.6 all-gather.2.cloned.1.call-done.w_ref
  100.3 0.0 copy-start
  100.3 2.5 %copy-done = bf16[2048,1280]{1,0:T(8,128)(2,1)S(1)} copy-done((bf16[2048,1280]{1,0:T(8,128)(2,1)S(1)}, bf16[2048,1280]{1,0:T(8,128)(2,1)}, u32[]{:S(2)}) %copy-start) | copy-done | bytes 5242904
  102.7 0.0 copy-start.1
  102.7 1.1 shard_map.59
  103.8 3.9 %collective-permute-start.9 = (bf16[32,1280]{1,0:T(8,128)(2,1)S(1)}, bf16[32,1280]{1,0:T(8,128)(2,1)S(1)}, u32[]{:S(2)}, u32[]{:S(2)}) collective-permute-start(bf16[32,1280]{1,0:T(8,128)(2,1)S(1)} %get-tuple-element.41), channel_id=1, source_target_pairs={{0,1},{1,0},{2,3},{3,2},{4,5},{5,4},{6,7},{7,6},{8,9},{9,8},{10,11... | collective-permute-start | bytes 245768 | tf_op jit(solution)/shard_map/ppermute | solution.py:299
  107.8 0.0 collective-permute-done.8.rows_ref
  107.8 0.0 copy-done.1
  107.8 1.1 shard_map.60
  108.8 3.4 %collective-permute-start.11 = (bf16[32,1280]{1,0:T(8,128)(2,1)S(1)}, bf16[32,1280]{1,0:T(8,128)(2,1)S(1)}, u32[]{:S(2)}, u32[]{:S(2)}) collective-permute-start(bf16[32,1280]{1,0:T(8,128)(2,1)S(1)} %get-tuple-element.44), channel_id=1, source_target_pairs={{0,33},{1,32},{16,49},{17,48},{32,1},{33,0},{48,17},{49,16},{64,97... | collective-permute-start | bytes 245768 | tf_op jit(solution)/shard_map/ppermute | solution.py:305
  112.3 0.0 collective-permute-done.9.got_ref
  112.3 2.2 %collective-permute-start.10 = (bf16[32,1280]{1,0:T(8,128)(2,1)S(1)}, bf16[32,1280]{1,0:T(8,128)(2,1)S(1)}, u32[]{:S(2)}, u32[]{:S(2)}) collective-permute-start(bf16[32,1280]{1,0:T(8,128)(2,1)S(1)} %get-tuple-element.43), channel_id=1, source_target_pairs={{0,32},{16,48},{32,0},{48,16},{64,96},{80,112},{96,64},{112,80},{1... | collective-permute-start | bytes 245768 | tf_op jit(solution)/shard_map/ppermute | solution.py:212
  114.5 0.4 collective-permute-done.11.far_other_ref
  114.9 2.6 %collective-permute-done.10.far_ref = bf16[32,1280]{1,0:T(8,128)(2,1)S(1)} collective-permute-done((bf16[32,1280]{1,0:T(8,128)(2,1)S(1)}, bf16[32,1280]{1,0:T(8,128)(2,1)S(1)}, u32[]{:S(2)}, u32[]{:S(2)}) %collective-permute-start.10) | collective-permute-done | bytes 81952 | tf_op jit(solution)/shard_map/ppermute | solution.py:212
  117.5 0.7 shard_map.61
  (9 shorter events, 0.2 us)
Async XLA Ops:
  6.5 2.2 %copy-start.3 = (bf16[512,256]{1,0:T(8,128)(2,1)S(1)}, bf16[512,256]{1,0:T(8,128)(2,1)}, u32[]{:S(2)}) copy-start(bf16[512,256]{1,0:T(8,128)(2,1)} %param.6) | copy-start | bytes 786436
  6.5 2.2 %copy-start.5 = (bf16[512,256]{1,0:T(8,128)(2,1)S(1)}, bf16[512,256]{1,0:T(8,128)(2,1)}, u32[]{:S(2)}) copy-start(bf16[512,256]{1,0:T(8,128)(2,1)} %param.5) | copy-start | bytes 786436
  6.5 2.2 %copy-start.4 = (bf16[512,256]{1,0:T(8,128)(2,1)S(1)}, bf16[512,256]{1,0:T(8,128)(2,1)}, u32[]{:S(2)}) copy-start(bf16[512,256]{1,0:T(8,128)(2,1)} %param.7) | copy-start | bytes 786436
  6.5 93.7 %all-gather.2.cloned.1.call-start = ((), (), s32[]{:S(2)}) async-start(), calls=%async_computation.1 | async-start | bytes 5570560 | tf_op jit(solution)/shard_map/all_gather | solution.py:226
  8.9 10.1 %collective-permute-start = (bf16[3,512,128]{2,1,0:T(8,128)(2,1)S(1)}, bf16[3,512,128]{2,1,0:T(8,128)(2,1)S(1)}, u32[]{:S(2)}, u32[]{:S(2)}) collective-permute-start(bf16[3,512,128]{2,1,0:T(8,128)(2,1)S(1)} %pad_maximum_fusion.1), channel_id=1, source_target_pairs={{0,16},{16,0},{32,48},{48,32},{64,80},{80,64},{96,112},{112,96},{1... | collective-permute-start | bytes 1179656 | tf_op jit(solution)/shard_map/ppermute | solution.py:212
  19.1 12.5 %collective-permute-start.3 = (bf16[4,512,128]{2,1,0:T(8,128)(2,1)S(1)}, bf16[4,512,128]{2,1,0:T(8,128)(2,1)S(1)}, u32[]{:S(2)}, u32[]{:S(2)}) collective-permute-start(bf16[4,512,128]{2,1,0:T(8,128)(2,1)S(1)} %pad_maximum_fusion.refs_3_), channel_id=1, source_target_pairs={{0,128},{16,144},{32,160},{48,176},{64,192},{80,208},{96,224},{112... | collective-permute-start | bytes 1572872 | tf_op jit(solution)/shard_map/ppermute | solution.py:212
  20.4 15.1 %collective-permute-start.4 = (bf16[4,512,128]{2,1,0:T(8,128)(2,1)S(1)}, bf16[4,512,128]{2,1,0:T(8,128)(2,1)S(1)}, u32[]{:S(2)}, u32[]{:S(2)}) collective-permute-start(bf16[4,512,128]{2,1,0:T(8,128)(2,1)S(1)} %pad_maximum_fusion.refs_3_), channel_id=1, source_target_pairs={{128,0},{144,16},{160,32},{176,48},{192,64},{208,80},{224,96},{240... | collective-permute-start | bytes 1572872 | tf_op jit(solution)/shard_map/ppermute | solution.py:212
  21.7 16.6 %collective-permute-start.1 = (bf16[4,512,128]{2,1,0:T(8,128)(2,1)S(1)}, bf16[4,512,128]{2,1,0:T(8,128)(2,1)S(1)}, u32[]{:S(2)}, u32[]{:S(2)}) collective-permute-start(bf16[4,512,128]{2,1,0:T(8,128)(2,1)S(1)} %pad_maximum_fusion.refs_3_), channel_id=1, source_target_pairs={{0,64},{16,80},{32,96},{48,112},{64,0},{80,16},{96,32},{112,48},{1... | collective-permute-start | bytes 1572872 | tf_op jit(solution)/shard_map/ppermute | solution.py:212
  23.8 18.4 %copy-start.2 = (s32[6,4,4]{0,2,1:T(4,128)S(1)}, s32[6,4,4]{0,2,1:T(4,128)}, u32[]{:S(2)}) copy-start(s32[6,4,4]{0,2,1:T(4,128)} %param.8) | copy-start | bytes 1156
  23.8 22.3 %collective-permute-start.6 = (bf16[4,512,128]{2,1,0:T(8,128)(2,1)S(1)}, bf16[4,512,128]{2,1,0:T(8,128)(2,1)S(1)}, u32[]{:S(2)}, u32[]{:S(2)}) collective-permute-start(bf16[4,512,128]{2,1,0:T(8,128)(2,1)S(1)} %pad_maximum_fusion.refs_3_), channel_id=1, source_target_pairs={{0,32},{16,48},{32,0},{48,16},{64,96},{80,112},{96,64},{112,80},{1... | collective-permute-start | bytes 1572872 | tf_op jit(solution)/shard_map/ppermute | solution.py:212
  25.8 20.3 %collective-permute-start.7 = (bf16[4,512,128]{2,1,0:T(8,128)(2,1)S(1)}, bf16[4,512,128]{2,1,0:T(8,128)(2,1)S(1)}, u32[]{:S(2)}, u32[]{:S(2)}) collective-permute-start(bf16[4,512,128]{2,1,0:T(8,128)(2,1)S(1)} %pad_maximum_fusion.refs_3_), channel_id=1, source_target_pairs={{0,256},{16,272},{32,288},{48,304},{64,320},{80,336},{96,352},{112... | collective-permute-start | bytes 1572872 | tf_op jit(solution)/shard_map/ppermute | solution.py:212
  35.6 16.1 %collective-permute-start.5 = (bf16[4,512,128]{2,1,0:T(8,128)(2,1)S(1)}, bf16[4,512,128]{2,1,0:T(8,128)(2,1)S(1)}, u32[]{:S(2)}, u32[]{:S(2)}) collective-permute-start(bf16[4,512,128]{2,1,0:T(8,128)(2,1)S(1)} %select_select_fusion), channel_id=1, source_target_pairs={{0,96},{16,112},{32,64},{48,80},{64,32},{80,48},{96,0},{112,16},{1... | collective-permute-start | bytes 1572872 | tf_op jit(solution)/shard_map/ppermute | solution.py:212
  38.4 16.0 %collective-permute-start.2 = (bf16[4,512,128]{2,1,0:T(8,128)(2,1)S(1)}, bf16[4,512,128]{2,1,0:T(8,128)(2,1)S(1)}, u32[]{:S(2)}, u32[]{:S(2)}) collective-permute-start(bf16[4,512,128]{2,1,0:T(8,128)(2,1)S(1)} %collective-permute-done.1.refs_4_), channel_id=1, source_target_pairs={{0,128},{16,144},{32,160},{48,176},{128,256},{144,272},{160,288},{... | collective-permute-start | bytes 1572872 | tf_op jit(solution)/shard_map/ppermute | solution.py:212
  97.0 10.8 %collective-permute-start.8 = (bf16[16,64,128]{2,1,0:T(8,128)(2,1)S(1)}, bf16[16,64,128]{2,1,0:T(8,128)(2,1)S(1)}, u32[]{:S(2)}, u32[]{:S(2)}) collective-permute-start(bf16[16,64,128]{2,1,0:T(8,128)(2,1)S(1)} %all_to_all.5.rows_ref), channel_id=1, source_target_pairs={{0,32},{16,48},{32,0},{48,16},{64,96},{80,112},{96,64},{112,80},{1... | collective-permute-start | bytes 786440 | tf_op jit(solution)/shard_map/ppermute | solution.py:212
  100.3 2.5 %copy-start = (bf16[2048,1280]{1,0:T(8,128)(2,1)S(1)}, bf16[2048,1280]{1,0:T(8,128)(2,1)}, u32[]{:S(2)}) copy-start(bf16[2048,1280]{1,0:T(8,128)(2,1)} %all-gather.2.cloned.1.call-done.w_ref) | copy-start | bytes 15728644
  102.7 5.0 %copy-start.1 = (bf16[2048,1280]{1,0:T(8,128)(2,1)S(1)}, bf16[2048,1280]{1,0:T(8,128)(2,1)}, u32[]{:S(2)}) copy-start(bf16[2048,1280]{1,0:T(8,128)(2,1)} %all-gather.2.cloned.1.call-done.w_ref) | copy-start | bytes 15728644
  103.8 8.5 %collective-permute-start.9 = (bf16[32,1280]{1,0:T(8,128)(2,1)S(1)}, bf16[32,1280]{1,0:T(8,128)(2,1)S(1)}, u32[]{:S(2)}, u32[]{:S(2)}) collective-permute-start(bf16[32,1280]{1,0:T(8,128)(2,1)S(1)} %get-tuple-element.41), channel_id=1, source_target_pairs={{0,1},{1,0},{2,3},{3,2},{4,5},{5,4},{6,7},{7,6},{8,9},{9,8},{10,11... | collective-permute-start | bytes 245768 | tf_op jit(solution)/shard_map/ppermute | solution.py:299
  108.8 6.1 %collective-permute-start.11 = (bf16[32,1280]{1,0:T(8,128)(2,1)S(1)}, bf16[32,1280]{1,0:T(8,128)(2,1)S(1)}, u32[]{:S(2)}, u32[]{:S(2)}) collective-permute-start(bf16[32,1280]{1,0:T(8,128)(2,1)S(1)} %get-tuple-element.44), channel_id=1, source_target_pairs={{0,33},{1,32},{16,49},{17,48},{32,1},{33,0},{48,17},{49,16},{64,97... | collective-permute-start | bytes 245768 | tf_op jit(solution)/shard_map/ppermute | solution.py:305
  112.3 5.2 %collective-permute-start.10 = (bf16[32,1280]{1,0:T(8,128)(2,1)S(1)}, bf16[32,1280]{1,0:T(8,128)(2,1)S(1)}, u32[]{:S(2)}, u32[]{:S(2)}) collective-permute-start(bf16[32,1280]{1,0:T(8,128)(2,1)S(1)} %get-tuple-element.43), channel_id=1, source_target_pairs={{0,32},{16,48},{32,0},{48,16},{64,96},{80,112},{96,64},{112,80},{1... | collective-permute-start | bytes 245768 | tf_op jit(solution)/shard_map/ppermute | solution.py:212
Sparse Core Ops, SparseCore 0:
  9.5 90.7 all-gather.1

commit v9 on v8

--- a/solution.py
+++ b/solution.py
@@ -102,19 +102,17 @@
                 outs[1][frame, places[a], :] = totals[a]
                 outs[2][frame, places[a], :] = part
 
-    if split is None:
-
-        @pl.loop(0, 2 * tiles)
-        def _(step):
-            fold(step // tiles, step % tiles, sources)
-
-    else:
-        favoured = info_ref[split]
-
-        @pl.loop(0, tiles)
-        def _(tile):
+    alone = [source for source in sources if not source[1]]
+    favoured = None if split is None else info_ref[split]
+
+    @pl.loop(0, tiles)
+    def _(tile):
+        if split is None:
+            fold(0, tile, sources)
+            fold(1, tile, sources)
+        else:
             fold(favoured, tile, sources)
-            fold(1 - favoured, tile, [s for s in sources if not s[1]])
+            fold(1 - favoured, tile, alone)
 
 
 def attend(info, mask, q, kvs, sources, split, state, last):
@@ -273,15 +271,18 @@
         info,
         mask,
         q,
-        [beside, across, above, below, far],
-        [
-            (0, False, 2, 2),
-            (0, True, 1, 2),
-            (1, False, 3, 2),
-            (2, False, 4, 5),
-            (3, False, 4, 6),
-            (4, False, 5, 2),
-        ],
+        [across, above, below],
+        [(0, False, 3, 2), (1, False, 4, 5), (2, False, 4, 6)],
+        None,
+        state,
+        False,
+    )
+    state = attend(
+        info,
+        mask,
+        q,
+        [beside, far],
+        [(0, False, 2, 2), (0, True, 1, 2), (1, False, 5, 2)],
         0,
         state,
         False,

time: 126 us -> 126 us (level)
    ppermute x1, starting transfers between devices: 3.94 us -> 2.05 us  [shards(): got = lax.ppermute(beside_z, 'low', [(0, 1), (1, 0)])]
    pallas_call x4 -> x5, Pallas kernels: 14 us -> 14.7 us  [attend(): pl.pallas_call(functools.partial(attend_kernel, sources, split, len(kvs),...]
where the time goes in v9:
time: 126 us; the launch traced here: 125 us
  blocking collectives  40.4 us (32%)
  starting transfers between devices  37.4 us (30%)
  Pallas kernels  17.5 us (14%)
  between operations  13.7 us (11%)
  waiting for transfers between devices  10.4 us (8%)
  local copies, waits for them, and re-layouts  2.62 us (2%)
  other arithmetic  2.46 us (2%)
    all_to_all x1, blocking collectives, shards(): lax.all_to_all(attended.reshape(FT // ROWS, 2 * ROWS, HD), ('core', 'high...  40.4 us
    ppermute x10, starting transfers between devices, send(): return lax.ppermute(array, FRAMES, pairs)  31.3 us
    pallas_call x5, Pallas kernels, attend(): pl.pallas_call(functools.partial(attend_kernel, sources, split, len(kvs),...  14.7 us
    ppermute x10, waiting for transfers between devices, send(): return lax.ppermute(array, FRAMES, pairs)  10.3 us
    ppermute x1, starting transfers between devices, shards(): got_far_other = lax.ppermute(far_beside, FRAMES + ('low',), both)  4.08 us
  transfers between devices with their start and end apart: 13, of which 8 were waited for; matrix products, arithmetic and copies ran while one was open for 0% of the time, Pallas kernels for 13%

profile of v9, /device:TPU:1, one launch (start us, length us, event | category | flops | bytes accessed | tf_op | source)
XLA Modules:
  0.0 124.5 jit_solution(5201745933635006445)
XLA Ops:
  6.5 0.0 copy-start.3
  6.5 0.0 copy-start.5
  6.5 0.0 copy-start.4
  6.5 0.0 all-gather.2.cloned.1.call-start
  6.5 2.1 %select_select_fusion.1 = bf16[128,1280]{1,0:T(8,128)(2,1)} fusion(bf16[256,2560]{1,0:T(8,128)(2,1)} %param.9, pred[]{:T(512)S(6)} %eq.22, pred[]{:T(512)S(6)} %eq.21), kind=kLoop, calls=%fused_computation.3 | loop fusion | flops 491520 | bytes 1638402 | tf_op jit(solution)/shard_map/jit(_where)/select_n | solution.py:218
  8.7 0.0 all-gather.2.cloned.1.call-update
  8.7 0.0 copy-done.3
  8.7 0.0 copy-done.5
  8.8 0.0 copy-done.4
  8.9 8.8 %collective-permute-start = (bf16[3,512,128]{2,1,0:T(8,128)(2,1)S(1)}, bf16[3,512,128]{2,1,0:T(8,128)(2,1)S(1)}, u32[]{:S(2)}, u32[]{:S(2)}) collective-permute-start(bf16[3,512,128]{2,1,0:T(8,128)(2,1)S(1)} %pad_maximum_fusion.1), channel_id=1, source_target_pairs={{0,16},{16,0},{32,48},{48,32},{64,80},{80,64},{96,112},{112,96},{1... | collective-permute-start | bytes 1179656 | tf_op jit(solution)/shard_map/ppermute | solution.py:210
  17.7 1.3 %collective-permute-done = bf16[3,512,128]{2,1,0:T(8,128)(2,1)S(1)} collective-permute-done((bf16[3,512,128]{2,1,0:T(8,128)(2,1)S(1)}, bf16[3,512,128]{2,1,0:T(8,128)(2,1)S(1)}, u32[]{:S(2)}, u32[]{:S(2)}) %collective-permute-start) | collective-permute-done | bytes 393248 | tf_op jit(solution)/shard_map/ppermute | solution.py:210
  19.0 0.1 pad_maximum_fusion.refs_3_
  19.1 1.3 %collective-permute-start.3 = (bf16[4,512,128]{2,1,0:T(8,128)(2,1)S(1)}, bf16[4,512,128]{2,1,0:T(8,128)(2,1)S(1)}, u32[]{:S(2)}, u32[]{:S(2)}) collective-permute-start(bf16[4,512,128]{2,1,0:T(8,128)(2,1)S(1)} %pad_maximum_fusion.refs_3_), channel_id=1, source_target_pairs={{0,128},{16,144},{32,160},{48,176},{64,192},{80,208},{96,224},{112... | collective-permute-start | bytes 1572872 | tf_op jit(solution)/shard_map/ppermute | solution.py:210
  20.4 1.3 %collective-permute-start.4 = (bf16[4,512,128]{2,1,0:T(8,128)(2,1)S(1)}, bf16[4,512,128]{2,1,0:T(8,128)(2,1)S(1)}, u32[]{:S(2)}, u32[]{:S(2)}) collective-permute-start(bf16[4,512,128]{2,1,0:T(8,128)(2,1)S(1)} %pad_maximum_fusion.refs_3_), channel_id=1, source_target_pairs={{128,0},{144,16},{160,32},{176,48},{192,64},{208,80},{224,96},{240... | collective-permute-start | bytes 1572872 | tf_op jit(solution)/shard_map/ppermute | solution.py:210
  21.7 1.9 %collective-permute-start.1 = (bf16[4,512,128]{2,1,0:T(8,128)(2,1)S(1)}, bf16[4,512,128]{2,1,0:T(8,128)(2,1)S(1)}, u32[]{:S(2)}, u32[]{:S(2)}) collective-permute-start(bf16[4,512,128]{2,1,0:T(8,128)(2,1)S(1)} %pad_maximum_fusion.refs_3_), channel_id=1, source_target_pairs={{0,64},{16,80},{32,96},{48,112},{64,0},{80,16},{96,32},{112,48},{1... | collective-permute-start | bytes 1572872 | tf_op jit(solution)/shard_map/ppermute | solution.py:210
  23.7 0.1 stack.65.refs_0_
  23.8 0.0 copy-start.2
  23.8 2.0 %collective-permute-start.6 = (bf16[4,512,128]{2,1,0:T(8,128)(2,1)S(1)}, bf16[4,512,128]{2,1,0:T(8,128)(2,1)S(1)}, u32[]{:S(2)}, u32[]{:S(2)}) collective-permute-start(bf16[4,512,128]{2,1,0:T(8,128)(2,1)S(1)} %pad_maximum_fusion.refs_3_), channel_id=1, source_target_pairs={{0,32},{16,48},{32,0},{48,16},{64,96},{80,112},{96,64},{112,80},{1... | collective-permute-start | bytes 1572872 | tf_op jit(solution)/shard_map/ppermute | solution.py:210
  25.8 5.2 %collective-permute-start.7 = (bf16[4,512,128]{2,1,0:T(8,128)(2,1)S(1)}, bf16[4,512,128]{2,1,0:T(8,128)(2,1)S(1)}, u32[]{:S(2)}, u32[]{:S(2)}) collective-permute-start(bf16[4,512,128]{2,1,0:T(8,128)(2,1)S(1)} %pad_maximum_fusion.refs_3_), channel_id=1, source_target_pairs={{0,256},{16,272},{32,288},{48,304},{64,320},{80,336},{96,352},{112... | collective-permute-start | bytes 1572872 | tf_op jit(solution)/shard_map/ppermute | solution.py:210
  31.0 0.6 collective-permute-done.3.refs_4_
  31.6 3.9 %collective-permute-done.4.refs_5_ = bf16[4,512,128]{2,1,0:T(8,128)(2,1)S(1)} collective-permute-done((bf16[4,512,128]{2,1,0:T(8,128)(2,1)S(1)}, bf16[4,512,128]{2,1,0:T(8,128)(2,1)S(1)}, u32[]{:S(2)}, u32[]{:S(2)}) %collective-permute-start.4) | collective-permute-done | bytes 524320 | tf_op jit(solution)/shard_map/ppermute | solution.py:210
  35.5 0.1 select_select_fusion
  35.6 1.9 %collective-permute-start.5 = (bf16[4,512,128]{2,1,0:T(8,128)(2,1)S(1)}, bf16[4,512,128]{2,1,0:T(8,128)(2,1)S(1)}, u32[]{:S(2)}, u32[]{:S(2)}) collective-permute-start(bf16[4,512,128]{2,1,0:T(8,128)(2,1)S(1)} %select_select_fusion), channel_id=1, source_target_pairs={{0,96},{16,112},{32,64},{48,80},{64,32},{80,48},{96,0},{112,16},{1... | collective-permute-start | bytes 1572872 | tf_op jit(solution)/shard_map/ppermute | solution.py:210
  37.6 0.8 collective-permute-done.1.refs_3_
  38.3 3.7 %collective-permute-start.2 = (bf16[4,512,128]{2,1,0:T(8,128)(2,1)S(1)}, bf16[4,512,128]{2,1,0:T(8,128)(2,1)S(1)}, u32[]{:S(2)}, u32[]{:S(2)}) collective-permute-start(bf16[4,512,128]{2,1,0:T(8,128)(2,1)S(1)} %collective-permute-done.1.refs_3_), channel_id=1, source_target_pairs={{0,128},{16,144},{32,160},{48,176},{128,256},{144,272},{160,288},{... | collective-permute-start | bytes 1572872 | tf_op jit(solution)/shard_map/ppermute | solution.py:210
  42.1 0.0 copy-done.2
  42.1 2.9 %shard_map.55 = (f32[2,512,128]{2,1,0:T(8,128)S(1)}, f32[2,512,128]{2,1,0:T(8,128)S(1)}, f32[2,512,128]{2,1,0:T(8,128)S(1)}) custom-call(s32[8]{0:T(128)S(1)} %stack.65.refs_0_, s32[4,4,6]{2,1,0:T(4,128)S(1)} %bitcast.24, bf16[2,512,128]{2,1,0:T(8,128)(2,1)S(1)} %pad_maximum_fusion.2.refs_2_, bf16[4,512,128]{2,1,0:T(8,128)(2,1)S(1)} %pad_maximum_fusion.refs_3_), custom_call_target="tpu_custom_call" | custom-call | flops 536870912 | bytes 524288 | tf_op jit(solution)/shard_map/pallas_call | solution.py:129
  45.0 3.6 %shard_map.56 = (f32[2,512,128]{2,1,0:T(8,128)S(1)}, f32[2,512,128]{2,1,0:T(8,128)S(1)}, f32[2,512,128]{2,1,0:T(8,128)S(1)}) custom-call(s32[8]{0:T(128)S(1)} %stack.65.refs_0_, s32[4,4,6]{2,1,0:T(4,128)S(1)} %bitcast.25, bf16[2,512,128]{2,1,0:T(8,128)(2,1)S(1)} %pad_maximum_fusion.2.refs_2_, bf16[4,512,128]{2,1,0:T(8,128)(2,1)S(1)} %collective-permute-done.1.refs_3_, ...), custom_call_target="tpu_custom_call" | custom-call | flops 805306368 | bytes 1572864 | tf_op jit(solution)/shard_map/pallas_call | solution.py:129
  48.6 0.0 collective-permute-done.6.refs_3_
  48.6 0.0 collective-permute-done.7.refs_4_
  48.7 3.3 %shard_map.57 = (f32[2,512,128]{2,1,0:T(8,128)S(1)}, f32[2,512,128]{2,1,0:T(8,128)S(1)}, f32[2,512,128]{2,1,0:T(8,128)S(1)}) custom-call(s32[8]{0:T(128)S(1)} %stack.65.refs_0_, s32[4,4,6]{2,1,0:T(4,128)S(1)} %bitcast.26, bf16[2,512,128]{2,1,0:T(8,128)(2,1)S(1)} %pad_maximum_fusion.2.refs_2_, bf16[4,512,128]{2,1,0:T(8,128)(2,1)S(1)} %collective-permute-done.6.refs_3_, ...), custom_call_target="tpu_custom_call" | custom-call | flops 671088640 | bytes 1048576 | tf_op jit(solution)/shard_map/pallas_call | solution.py:129
  52.0 0.0 collective-permute-done.5.refs_3_
  52.0 2.6 %shard_map.58 = (f32[2,512,128]{2,1,0:T(8,128)S(1)}, f32[2,512,128]{2,1,0:T(8,128)S(1)}, f32[2,512,128]{2,1,0:T(8,128)S(1)}) custom-call(s32[8]{0:T(128)S(1)} %stack.65.refs_0_, s32[4,4,6]{2,1,0:T(4,128)S(1)} %bitcast.27, bf16[2,512,128]{2,1,0:T(8,128)(2,1)S(1)} %pad_maximum_fusion.2.refs_2_, bf16[4,512,128]{2,1,0:T(8,128)(2,1)S(1)} %collective-permute-done.5.refs_3_, ...), custom_call_target="tpu_custom_call" | custom-call | flops 402653184 | bytes 524288 | tf_op jit(solution)/shard_map/pallas_call | solution.py:129
  54.6 0.0 collective-permute-done.2.refs_3_
  54.6 2.3 %shard_map.59 = bf16[2,16,32,128]{3,2,1,0:T(8,128)(2,1)S(1)} custom-call(s32[8]{0:T(128)S(1)} %stack.65.refs_0_, s32[4,4,6]{2,1,0:T(4,128)S(1)} %bitcast.28, bf16[2,512,128]{2,1,0:T(8,128)(2,1)S(1)} %pad_maximum_fusion.2.refs_2_, bf16[4,512,128]{2,1,0:T(8,128)(2,1)S(1)} %collective-permute-done.2.refs_3_, f32[2,512,128]{2,1,0:T(8,128)S(1)} %get-tuple-element.39.refs_4_, ...), custom_call_target="tpu_custom_call" | custom-call | flops 268435456 | bytes 524288 | tf_op jit(solution)/shard_map/pallas_call | solution.py:129
  56.9 40.4 %all_to_all.5.rows_ref = bf16[16,64,128]{2,1,0:T(8,128)(2,1)S(1)} all-to-all(bf16[16,64,128]{2,1,0:T(8,128)(2,1)S(1)} %bitcast.23), channel_id=1, replica_groups=mesh['x'=4,'y'=4,'core'=2,'high'=8,'low'=2] {'core','high'}, dimensions={0} | all-to-all | bytes 524288 | tf_op jit(solution)/shard_map/all_to_all | solution.py:293
  97.2 3.2 %collective-permute-start.8 = (bf16[16,64,128]{2,1,0:T(8,128)(2,1)S(1)}, bf16[16,64,128]{2,1,0:T(8,128)(2,1)S(1)}, u32[]{:S(2)}, u32[]{:S(2)}) collective-permute-start(bf16[16,64,128]{2,1,0:T(8,128)(2,1)S(1)} %all_to_all.5.rows_ref), channel_id=1, source_target_pairs={{0,32},{16,48},{32,0},{48,16},{64,96},{80,112},{96,64},{112,80},{1... | collective-permute-start | bytes 786440 | tf_op jit(solution)/shard_map/ppermute | solution.py:210
  100.4 0.1 all-gather.2.cloned.1.call-done.w_ref
  100.5 0.0 copy-start
  100.5 2.5 %copy-done = bf16[2048,1280]{1,0:T(8,128)(2,1)S(1)} copy-done((bf16[2048,1280]{1,0:T(8,128)(2,1)S(1)}, bf16[2048,1280]{1,0:T(8,128)(2,1)}, u32[]{:S(2)}) %copy-start) | copy-done | bytes 5242904
  103.0 0.0 copy-start.1
  103.0 1.1 shard_map.60
  104.0 2.1 %collective-permute-start.9 = (bf16[32,1280]{1,0:T(8,128)(2,1)S(1)}, bf16[32,1280]{1,0:T(8,128)(2,1)S(1)}, u32[]{:S(2)}, u32[]{:S(2)}) collective-permute-start(bf16[32,1280]{1,0:T(8,128)(2,1)S(1)} %get-tuple-element.47), channel_id=1, source_target_pairs={{0,1},{1,0},{2,3},{3,2},{4,5},{5,4},{6,7},{7,6},{8,9},{9,8},{10,11... | collective-permute-start | bytes 245768 | tf_op jit(solution)/shard_map/ppermute | solution.py:300
  106.1 0.5 collective-permute-done.8.rows_ref
  106.6 0.0 copy-done.1
  106.6 1.1 shard_map.61
  107.7 4.1 %collective-permute-start.11 = (bf16[32,1280]{1,0:T(8,128)(2,1)S(1)}, bf16[32,1280]{1,0:T(8,128)(2,1)S(1)}, u32[]{:S(2)}, u32[]{:S(2)}) collective-permute-start(bf16[32,1280]{1,0:T(8,128)(2,1)S(1)} %get-tuple-element.50), channel_id=1, source_target_pairs={{0,33},{1,32},{16,49},{17,48},{32,1},{33,0},{48,17},{49,16},{64,97... | collective-permute-start | bytes 245768 | tf_op jit(solution)/shard_map/ppermute | solution.py:306
  111.8 0.0 collective-permute-done.9.got_ref
  111.8 1.9 %collective-permute-start.10 = (bf16[32,1280]{1,0:T(8,128)(2,1)S(1)}, bf16[32,1280]{1,0:T(8,128)(2,1)S(1)}, u32[]{:S(2)}, u32[]{:S(2)}) collective-permute-start(bf16[32,1280]{1,0:T(8,128)(2,1)S(1)} %get-tuple-element.49), channel_id=1, source_target_pairs={{0,32},{16,48},{32,0},{48,16},{64,96},{80,112},{96,64},{112,80},{1... | collective-permute-start | bytes 245768 | tf_op jit(solution)/shard_map/ppermute | solution.py:210
  113.7 0.1 collective-permute-done.11.far_other_ref
  113.7 3.2 %collective-permute-done.10.far_ref = bf16[32,1280]{1,0:T(8,128)(2,1)S(1)} collective-permute-done((bf16[32,1280]{1,0:T(8,128)(2,1)S(1)}, bf16[32,1280]{1,0:T(8,128)(2,1)S(1)}, u32[]{:S(2)}, u32[]{:S(2)}) %collective-permute-start.10) | collective-permute-done | bytes 81952 | tf_op jit(solution)/shard_map/ppermute | solution.py:210
  117.0 0.7 shard_map.62
  (9 shorter events, 0.2 us)
Async XLA Ops:
  6.5 2.2 %copy-start.3 = (bf16[512,256]{1,0:T(8,128)(2,1)S(1)}, bf16[512,256]{1,0:T(8,128)(2,1)}, u32[]{:S(2)}) copy-start(bf16[512,256]{1,0:T(8,128)(2,1)} %param.6) | copy-start | bytes 786436
  6.5 2.2 %copy-start.5 = (bf16[512,256]{1,0:T(8,128)(2,1)S(1)}, bf16[512,256]{1,0:T(8,128)(2,1)}, u32[]{:S(2)}) copy-start(bf16[512,256]{1,0:T(8,128)(2,1)} %param.5) | copy-start | bytes 786436
  6.5 2.2 %copy-start.4 = (bf16[512,256]{1,0:T(8,128)(2,1)S(1)}, bf16[512,256]{1,0:T(8,128)(2,1)}, u32[]{:S(2)}) copy-start(bf16[512,256]{1,0:T(8,128)(2,1)} %param.7) | copy-start | bytes 786436
  6.5 94.0 %all-gather.2.cloned.1.call-start = ((), (), s32[]{:S(2)}) async-start(), calls=%async_computation.1 | async-start | bytes 5570560 | tf_op jit(solution)/shard_map/all_gather | solution.py:224
  8.9 10.1 %collective-permute-start = (bf16[3,512,128]{2,1,0:T(8,128)(2,1)S(1)}, bf16[3,512,128]{2,1,0:T(8,128)(2,1)S(1)}, u32[]{:S(2)}, u32[]{:S(2)}) collective-permute-start(bf16[3,512,128]{2,1,0:T(8,128)(2,1)S(1)} %pad_maximum_fusion.1), channel_id=1, source_target_pairs={{0,16},{16,0},{32,48},{48,32},{64,80},{80,64},{96,112},{112,96},{1... | collective-permute-start | bytes 1179656 | tf_op jit(solution)/shard_map/ppermute | solution.py:210
  19.1 12.5 %collective-permute-start.3 = (bf16[4,512,128]{2,1,0:T(8,128)(2,1)S(1)}, bf16[4,512,128]{2,1,0:T(8,128)(2,1)S(1)}, u32[]{:S(2)}, u32[]{:S(2)}) collective-permute-start(bf16[4,512,128]{2,1,0:T(8,128)(2,1)S(1)} %pad_maximum_fusion.refs_3_), channel_id=1, source_target_pairs={{0,128},{16,144},{32,160},{48,176},{64,192},{80,208},{96,224},{112... | collective-permute-start | bytes 1572872 | tf_op jit(solution)/shard_map/ppermute | solution.py:210
  20.4 15.1 %collective-permute-start.4 = (bf16[4,512,128]{2,1,0:T(8,128)(2,1)S(1)}, bf16[4,512,128]{2,1,0:T(8,128)(2,1)S(1)}, u32[]{:S(2)}, u32[]{:S(2)}) collective-permute-start(bf16[4,512,128]{2,1,0:T(8,128)(2,1)S(1)} %pad_maximum_fusion.refs_3_), channel_id=1, source_target_pairs={{128,0},{144,16},{160,32},{176,48},{192,64},{208,80},{224,96},{240... | collective-permute-start | bytes 1572872 | tf_op jit(solution)/shard_map/ppermute | solution.py:210
  21.7 16.6 %collective-permute-start.1 = (bf16[4,512,128]{2,1,0:T(8,128)(2,1)S(1)}, bf16[4,512,128]{2,1,0:T(8,128)(2,1)S(1)}, u32[]{:S(2)}, u32[]{:S(2)}) collective-permute-start(bf16[4,512,128]{2,1,0:T(8,128)(2,1)S(1)} %pad_maximum_fusion.refs_3_), channel_id=1, source_target_pairs={{0,64},{16,80},{32,96},{48,112},{64,0},{80,16},{96,32},{112,48},{1... | collective-permute-start | bytes 1572872 | tf_op jit(solution)/shard_map/ppermute | solution.py:210
  23.8 18.4 %copy-start.2 = (s32[6,4,4]{0,2,1:T(4,128)S(1)}, s32[6,4,4]{0,2,1:T(4,128)}, u32[]{:S(2)}) copy-start(s32[6,4,4]{0,2,1:T(4,128)} %param.8) | copy-start | bytes 1156
  23.8 24.9 %collective-permute-start.6 = (bf16[4,512,128]{2,1,0:T(8,128)(2,1)S(1)}, bf16[4,512,128]{2,1,0:T(8,128)(2,1)S(1)}, u32[]{:S(2)}, u32[]{:S(2)}) collective-permute-start(bf16[4,512,128]{2,1,0:T(8,128)(2,1)S(1)} %pad_maximum_fusion.refs_3_), channel_id=1, source_target_pairs={{0,32},{16,48},{32,0},{48,16},{64,96},{80,112},{96,64},{112,80},{1... | collective-permute-start | bytes 1572872 | tf_op jit(solution)/shard_map/ppermute | solution.py:210
  25.8 22.8 %collective-permute-start.7 = (bf16[4,512,128]{2,1,0:T(8,128)(2,1)S(1)}, bf16[4,512,128]{2,1,0:T(8,128)(2,1)S(1)}, u32[]{:S(2)}, u32[]{:S(2)}) collective-permute-start(bf16[4,512,128]{2,1,0:T(8,128)(2,1)S(1)} %pad_maximum_fusion.refs_3_), channel_id=1, source_target_pairs={{0,256},{16,272},{32,288},{48,304},{64,320},{80,336},{96,352},{112... | collective-permute-start | bytes 1572872 | tf_op jit(solution)/shard_map/ppermute | solution.py:210
  35.6 16.4 %collective-permute-start.5 = (bf16[4,512,128]{2,1,0:T(8,128)(2,1)S(1)}, bf16[4,512,128]{2,1,0:T(8,128)(2,1)S(1)}, u32[]{:S(2)}, u32[]{:S(2)}) collective-permute-start(bf16[4,512,128]{2,1,0:T(8,128)(2,1)S(1)} %select_select_fusion), channel_id=1, source_target_pairs={{0,96},{16,112},{32,64},{48,80},{64,32},{80,48},{96,0},{112,16},{1... | collective-permute-start | bytes 1572872 | tf_op jit(solution)/shard_map/ppermute | solution.py:210
  38.3 16.2 %collective-permute-start.2 = (bf16[4,512,128]{2,1,0:T(8,128)(2,1)S(1)}, bf16[4,512,128]{2,1,0:T(8,128)(2,1)S(1)}, u32[]{:S(2)}, u32[]{:S(2)}) collective-permute-start(bf16[4,512,128]{2,1,0:T(8,128)(2,1)S(1)} %collective-permute-done.1.refs_3_), channel_id=1, source_target_pairs={{0,128},{16,144},{32,160},{48,176},{128,256},{144,272},{160,288},{... | collective-permute-start | bytes 1572872 | tf_op jit(solution)/shard_map/ppermute | solution.py:210
  97.2 9.4 %collective-permute-start.8 = (bf16[16,64,128]{2,1,0:T(8,128)(2,1)S(1)}, bf16[16,64,128]{2,1,0:T(8,128)(2,1)S(1)}, u32[]{:S(2)}, u32[]{:S(2)}) collective-permute-start(bf16[16,64,128]{2,1,0:T(8,128)(2,1)S(1)} %all_to_all.5.rows_ref), channel_id=1, source_target_pairs={{0,32},{16,48},{32,0},{48,16},{64,96},{80,112},{96,64},{112,80},{1... | collective-permute-start | bytes 786440 | tf_op jit(solution)/shard_map/ppermute | solution.py:210
  100.5 2.5 %copy-start = (bf16[2048,1280]{1,0:T(8,128)(2,1)S(1)}, bf16[2048,1280]{1,0:T(8,128)(2,1)}, u32[]{:S(2)}) copy-start(bf16[2048,1280]{1,0:T(8,128)(2,1)} %all-gather.2.cloned.1.call-done.w_ref) | copy-start | bytes 15728644
  103.0 3.6 %copy-start.1 = (bf16[2048,1280]{1,0:T(8,128)(2,1)S(1)}, bf16[2048,1280]{1,0:T(8,128)(2,1)}, u32[]{:S(2)}) copy-start(bf16[2048,1280]{1,0:T(8,128)(2,1)} %all-gather.2.cloned.1.call-done.w_ref) | copy-start | bytes 15728644
  104.0 7.7 %collective-permute-start.9 = (bf16[32,1280]{1,0:T(8,128)(2,1)S(1)}, bf16[32,1280]{1,0:T(8,128)(2,1)S(1)}, u32[]{:S(2)}, u32[]{:S(2)}) collective-permute-start(bf16[32,1280]{1,0:T(8,128)(2,1)S(1)} %get-tuple-element.47), channel_id=1, source_target_pairs={{0,1},{1,0},{2,3},{3,2},{4,5},{5,4},{6,7},{7,6},{8,9},{9,8},{10,11... | collective-permute-start | bytes 245768 | tf_op jit(solution)/shard_map/ppermute | solution.py:300
  107.7 6.1 %collective-permute-start.11 = (bf16[32,1280]{1,0:T(8,128)(2,1)S(1)}, bf16[32,1280]{1,0:T(8,128)(2,1)S(1)}, u32[]{:S(2)}, u32[]{:S(2)}) collective-permute-start(bf16[32,1280]{1,0:T(8,128)(2,1)S(1)} %get-tuple-element.50), channel_id=1, source_target_pairs={{0,33},{1,32},{16,49},{17,48},{32,1},{33,0},{48,17},{49,16},{64,97... | collective-permute-start | bytes 245768 | tf_op jit(solution)/shard_map/ppermute | solution.py:306
  111.8 5.2 %collective-permute-start.10 = (bf16[32,1280]{1,0:T(8,128)(2,1)S(1)}, bf16[32,1280]{1,0:T(8,128)(2,1)S(1)}, u32[]{:S(2)}, u32[]{:S(2)}) collective-permute-start(bf16[32,1280]{1,0:T(8,128)(2,1)S(1)} %get-tuple-element.49), channel_id=1, source_target_pairs={{0,32},{16,48},{32,0},{48,16},{64,96},{80,112},{96,64},{112,80},{1... | collective-permute-start | bytes 245768 | tf_op jit(solution)/shard_map/ppermute | solution.py:210
Sparse Core Ops, SparseCore 0:
  9.5 90.9 all-gather.1

commit v10 on v9

--- a/solution.py
+++ b/solution.py
@@ -209,17 +209,9 @@
     def send(array, pairs):
         return lax.ppermute(array, FRAMES, pairs)
 
-    first_core, first_side = core == 0, (y & 1) == 0
-
-    def corner(row, column):
-        return out_weight[row * HD : (row + 1) * HD, column * half : (column + 1) * half]
-
-    half = DOUT // 2
-    weight = jnp.where(
-        first_core,
-        jnp.where(first_side, corner(0, 0), corner(0, 1)),
-        jnp.where(first_side, corner(1, 0), corner(1, 1)),
-    )
+    first_core, half = core == 0, DOUT // 2
+    weight = lax.dynamic_slice_in_dim(out_weight, core * HD, HD, 0)
+    weight = jnp.where((y & 1) == 0, weight[:, :half], weight[:, half:])
     weight, first_core = lax.optimization_barrier((weight, first_core))
     weight = lax.all_gather(weight, ("core", "high"), axis=0, tiled=True)
 

time: 126 us -> 126 us (level)
  transfers between devices with their start and end apart: 13 -> 13, of which waited for: 8 -> 6; matrix products, arithmetic and copies ran while one was open for 0% -> 0% of each run, Pallas kernels for 13% -> 13%
where the time goes in v10:
time: 126 us; the launch traced here: 125 us
  blocking collectives  40.2 us (32%)
  starting transfers between devices  38.1 us (30%)
  Pallas kernels  17.5 us (14%)
  between operations  13.8 us (11%)
  waiting for transfers between devices  10.1 us (8%)
  local copies, waits for them, and re-layouts  2.62 us (2%)
  other arithmetic  2.28 us (2%)
    all_to_all x1, blocking collectives, shards(): lax.all_to_all(attended.reshape(FT // ROWS, 2 * ROWS, HD), ('core', 'high...  40.2 us
    ppermute x10, starting transfers between devices, send(): return lax.ppermute(array, FRAMES, pairs)  31.3 us
    pallas_call x5, Pallas kernels, attend(): pl.pallas_call(functools.partial(attend_kernel, sources, split, len(kvs),...  14.7 us
    ppermute x10, waiting for transfers between devices, send(): return lax.ppermute(array, FRAMES, pairs)  9.81 us
    ppermute x1, starting transfers between devices, shards(): got_far_other = lax.ppermute(far_beside, FRAMES + ('low',), both)  4.67 us
  transfers between devices with their start and end apart: 13, of which 6 were waited for; matrix products, arithmetic and copies ran while one was open for 0% of the time, Pallas kernels for 13%

profile of v10, /device:TPU:1, one launch (start us, length us, event | category | flops | bytes accessed | tf_op | source)
XLA Modules:
  0.0 124.5 jit_solution(7360799196746153173)
XLA Ops:
  6.5 0.0 copy-start.3
  6.5 0.0 copy-start.5
  6.5 0.0 copy-start.4
  6.5 0.0 all-gather.2.cloned.1.call-start
  6.5 1.9 %dynamic-slice_select_fusion = bf16[128,1280]{1,0:T(8,128)(2,1)} fusion(bf16[256,2560]{1,0:T(8,128)(2,1)} %param.9, s32[]{:T(128)S(6)} %select_n.70, s32[]{:T(128)S(6)} %add.12, pred[]{:T(512)S(6)} %eq.21), kind=kLoop, calls=%fused_computation.3 | loop fusion | flops 163840 | bytes 983049 | tf_op jit(solution)/shard_map/jit(_where)/select_n | solution.py:214
  8.5 0.0 all-gather.2.cloned.1.call-update
  8.5 0.0 copy-done.3
  8.6 0.0 copy-done.5
  8.6 0.0 copy-done.4
  8.7 8.8 %collective-permute-start = (bf16[3,512,128]{2,1,0:T(8,128)(2,1)S(1)}, bf16[3,512,128]{2,1,0:T(8,128)(2,1)S(1)}, u32[]{:S(2)}, u32[]{:S(2)}) collective-permute-start(bf16[3,512,128]{2,1,0:T(8,128)(2,1)S(1)} %pad_maximum_fusion.1), channel_id=1, source_target_pairs={{0,16},{16,0},{32,48},{48,32},{64,80},{80,64},{96,112},{112,96},{1... | collective-permute-start | bytes 1179656 | tf_op jit(solution)/shard_map/ppermute | solution.py:210
  17.5 1.3 %collective-permute-done = bf16[3,512,128]{2,1,0:T(8,128)(2,1)S(1)} collective-permute-done((bf16[3,512,128]{2,1,0:T(8,128)(2,1)S(1)}, bf16[3,512,128]{2,1,0:T(8,128)(2,1)S(1)}, u32[]{:S(2)}, u32[]{:S(2)}) %collective-permute-start) | collective-permute-done | bytes 393248 | tf_op jit(solution)/shard_map/ppermute | solution.py:210
  18.8 0.1 pad_maximum_fusion.refs_3_
  18.9 1.3 %collective-permute-start.3 = (bf16[4,512,128]{2,1,0:T(8,128)(2,1)S(1)}, bf16[4,512,128]{2,1,0:T(8,128)(2,1)S(1)}, u32[]{:S(2)}, u32[]{:S(2)}) collective-permute-start(bf16[4,512,128]{2,1,0:T(8,128)(2,1)S(1)} %pad_maximum_fusion.refs_3_), channel_id=1, source_target_pairs={{0,128},{16,144},{32,160},{48,176},{64,192},{80,208},{96,224},{112... | collective-permute-start | bytes 1572872 | tf_op jit(solution)/shard_map/ppermute | solution.py:210
  20.2 1.3 %collective-permute-start.4 = (bf16[4,512,128]{2,1,0:T(8,128)(2,1)S(1)}, bf16[4,512,128]{2,1,0:T(8,128)(2,1)S(1)}, u32[]{:S(2)}, u32[]{:S(2)}) collective-permute-start(bf16[4,512,128]{2,1,0:T(8,128)(2,1)S(1)} %pad_maximum_fusion.refs_3_), channel_id=1, source_target_pairs={{128,0},{144,16},{160,32},{176,48},{192,64},{208,80},{224,96},{240... | collective-permute-start | bytes 1572872 | tf_op jit(solution)/shard_map/ppermute | solution.py:210
  21.5 1.9 %collective-permute-start.1 = (bf16[4,512,128]{2,1,0:T(8,128)(2,1)S(1)}, bf16[4,512,128]{2,1,0:T(8,128)(2,1)S(1)}, u32[]{:S(2)}, u32[]{:S(2)}) collective-permute-start(bf16[4,512,128]{2,1,0:T(8,128)(2,1)S(1)} %pad_maximum_fusion.refs_3_), channel_id=1, source_target_pairs={{0,64},{16,80},{32,96},{48,112},{64,0},{80,16},{96,32},{112,48},{1... | collective-permute-start | bytes 1572872 | tf_op jit(solution)/shard_map/ppermute | solution.py:210
  23.5 0.1 stack.65.refs_0_
  23.6 0.0 copy-start.2
  23.6 2.0 %collective-permute-start.6 = (bf16[4,512,128]{2,1,0:T(8,128)(2,1)S(1)}, bf16[4,512,128]{2,1,0:T(8,128)(2,1)S(1)}, u32[]{:S(2)}, u32[]{:S(2)}) collective-permute-start(bf16[4,512,128]{2,1,0:T(8,128)(2,1)S(1)} %pad_maximum_fusion.refs_3_), channel_id=1, source_target_pairs={{0,32},{16,48},{32,0},{48,16},{64,96},{80,112},{96,64},{112,80},{1... | collective-permute-start | bytes 1572872 | tf_op jit(solution)/shard_map/ppermute | solution.py:210
  25.6 5.2 %collective-permute-start.7 = (bf16[4,512,128]{2,1,0:T(8,128)(2,1)S(1)}, bf16[4,512,128]{2,1,0:T(8,128)(2,1)S(1)}, u32[]{:S(2)}, u32[]{:S(2)}) collective-permute-start(bf16[4,512,128]{2,1,0:T(8,128)(2,1)S(1)} %pad_maximum_fusion.refs_3_), channel_id=1, source_target_pairs={{0,256},{16,272},{32,288},{48,304},{64,320},{80,336},{96,352},{112... | collective-permute-start | bytes 1572872 | tf_op jit(solution)/shard_map/ppermute | solution.py:210
  30.9 0.6 collective-permute-done.3.refs_4_
  31.4 3.9 %collective-permute-done.4.refs_5_ = bf16[4,512,128]{2,1,0:T(8,128)(2,1)S(1)} collective-permute-done((bf16[4,512,128]{2,1,0:T(8,128)(2,1)S(1)}, bf16[4,512,128]{2,1,0:T(8,128)(2,1)S(1)}, u32[]{:S(2)}, u32[]{:S(2)}) %collective-permute-start.4) | collective-permute-done | bytes 524320 | tf_op jit(solution)/shard_map/ppermute | solution.py:210
  35.4 0.1 select_select_fusion
  35.4 1.9 %collective-permute-start.5 = (bf16[4,512,128]{2,1,0:T(8,128)(2,1)S(1)}, bf16[4,512,128]{2,1,0:T(8,128)(2,1)S(1)}, u32[]{:S(2)}, u32[]{:S(2)}) collective-permute-start(bf16[4,512,128]{2,1,0:T(8,128)(2,1)S(1)} %select_select_fusion), channel_id=1, source_target_pairs={{0,96},{16,112},{32,64},{48,80},{64,32},{80,48},{96,0},{112,16},{1... | collective-permute-start | bytes 1572872 | tf_op jit(solution)/shard_map/ppermute | solution.py:210
  37.4 0.8 collective-permute-done.1.refs_3_
  38.2 3.7 %collective-permute-start.2 = (bf16[4,512,128]{2,1,0:T(8,128)(2,1)S(1)}, bf16[4,512,128]{2,1,0:T(8,128)(2,1)S(1)}, u32[]{:S(2)}, u32[]{:S(2)}) collective-permute-start(bf16[4,512,128]{2,1,0:T(8,128)(2,1)S(1)} %collective-permute-done.1.refs_3_), channel_id=1, source_target_pairs={{0,128},{16,144},{32,160},{48,176},{128,256},{144,272},{160,288},{... | collective-permute-start | bytes 1572872 | tf_op jit(solution)/shard_map/ppermute | solution.py:210
  41.9 0.0 copy-done.2
  41.9 2.9 %shard_map.55 = (f32[2,512,128]{2,1,0:T(8,128)S(1)}, f32[2,512,128]{2,1,0:T(8,128)S(1)}, f32[2,512,128]{2,1,0:T(8,128)S(1)}) custom-call(s32[8]{0:T(128)S(1)} %stack.65.refs_0_, s32[4,4,6]{2,1,0:T(4,128)S(1)} %bitcast.24, bf16[2,512,128]{2,1,0:T(8,128)(2,1)S(1)} %pad_maximum_fusion.2.refs_2_, bf16[4,512,128]{2,1,0:T(8,128)(2,1)S(1)} %pad_maximum_fusion.refs_3_), custom_call_target="tpu_custom_call" | custom-call | flops 536870912 | bytes 524288 | tf_op jit(solution)/shard_map/pallas_call | solution.py:129
  44.8 3.6 %shard_map.56 = (f32[2,512,128]{2,1,0:T(8,128)S(1)}, f32[2,512,128]{2,1,0:T(8,128)S(1)}, f32[2,512,128]{2,1,0:T(8,128)S(1)}) custom-call(s32[8]{0:T(128)S(1)} %stack.65.refs_0_, s32[4,4,6]{2,1,0:T(4,128)S(1)} %bitcast.25, bf16[2,512,128]{2,1,0:T(8,128)(2,1)S(1)} %pad_maximum_fusion.2.refs_2_, bf16[4,512,128]{2,1,0:T(8,128)(2,1)S(1)} %collective-permute-done.1.refs_3_, ...), custom_call_target="tpu_custom_call" | custom-call | flops 805306368 | bytes 1572864 | tf_op jit(solution)/shard_map/pallas_call | solution.py:129
  48.5 0.0 collective-permute-done.6.refs_3_
  48.5 0.0 collective-permute-done.7.refs_4_
  48.5 3.3 %shard_map.57 = (f32[2,512,128]{2,1,0:T(8,128)S(1)}, f32[2,512,128]{2,1,0:T(8,128)S(1)}, f32[2,512,128]{2,1,0:T(8,128)S(1)}) custom-call(s32[8]{0:T(128)S(1)} %stack.65.refs_0_, s32[4,4,6]{2,1,0:T(4,128)S(1)} %bitcast.26, bf16[2,512,128]{2,1,0:T(8,128)(2,1)S(1)} %pad_maximum_fusion.2.refs_2_, bf16[4,512,128]{2,1,0:T(8,128)(2,1)S(1)} %collective-permute-done.6.refs_3_, ...), custom_call_target="tpu_custom_call" | custom-call | flops 671088640 | bytes 1048576 | tf_op jit(solution)/shard_map/pallas_call | solution.py:129
  51.8 0.0 collective-permute-done.5.refs_3_
  51.8 2.6 %shard_map.58 = (f32[2,512,128]{2,1,0:T(8,128)S(1)}, f32[2,512,128]{2,1,0:T(8,128)S(1)}, f32[2,512,128]{2,1,0:T(8,128)S(1)}) custom-call(s32[8]{0:T(128)S(1)} %stack.65.refs_0_, s32[4,4,6]{2,1,0:T(4,128)S(1)} %bitcast.27, bf16[2,512,128]{2,1,0:T(8,128)(2,1)S(1)} %pad_maximum_fusion.2.refs_2_, bf16[4,512,128]{2,1,0:T(8,128)(2,1)S(1)} %collective-permute-done.5.refs_3_, ...), custom_call_target="tpu_custom_call" | custom-call | flops 402653184 | bytes 524288 | tf_op jit(solution)/shard_map/pallas_call | solution.py:129
  54.4 0.0 collective-permute-done.2.refs_3_
  54.4 2.3 %shard_map.59 = bf16[2,16,32,128]{3,2,1,0:T(8,128)(2,1)S(1)} custom-call(s32[8]{0:T(128)S(1)} %stack.65.refs_0_, s32[4,4,6]{2,1,0:T(4,128)S(1)} %bitcast.28, bf16[2,512,128]{2,1,0:T(8,128)(2,1)S(1)} %pad_maximum_fusion.2.refs_2_, bf16[4,512,128]{2,1,0:T(8,128)(2,1)S(1)} %collective-permute-done.2.refs_3_, f32[2,512,128]{2,1,0:T(8,128)S(1)} %get-tuple-element.39.refs_4_, ...), custom_call_target="tpu_custom_call" | custom-call | flops 268435456 | bytes 524288 | tf_op jit(solution)/shard_map/pallas_call | solution.py:129
  56.7 40.2 %all_to_all.5.rows_ref = bf16[16,64,128]{2,1,0:T(8,128)(2,1)S(1)} all-to-all(bf16[16,64,128]{2,1,0:T(8,128)(2,1)S(1)} %bitcast.23), channel_id=1, replica_groups=mesh['x'=4,'y'=4,'core'=2,'high'=8,'low'=2] {'core','high'}, dimensions={0} | all-to-all | bytes 524288 | tf_op jit(solution)/shard_map/all_to_all | solution.py:285
  96.9 3.2 %collective-permute-start.8 = (bf16[16,64,128]{2,1,0:T(8,128)(2,1)S(1)}, bf16[16,64,128]{2,1,0:T(8,128)(2,1)S(1)}, u32[]{:S(2)}, u32[]{:S(2)}) collective-permute-start(bf16[16,64,128]{2,1,0:T(8,128)(2,1)S(1)} %all_to_all.5.rows_ref), channel_id=1, source_target_pairs={{0,32},{16,48},{32,0},{48,16},{64,96},{80,112},{96,64},{112,80},{1... | collective-permute-start | bytes 786440 | tf_op jit(solution)/shard_map/ppermute | solution.py:210
  100.2 0.2 all-gather.2.cloned.1.call-done.w_ref
  100.4 0.0 copy-start
  100.4 2.5 %copy-done = bf16[2048,1280]{1,0:T(8,128)(2,1)S(1)} copy-done((bf16[2048,1280]{1,0:T(8,128)(2,1)S(1)}, bf16[2048,1280]{1,0:T(8,128)(2,1)}, u32[]{:S(2)}) %copy-start) | copy-done | bytes 5242904
  102.9 0.0 copy-start.1
  102.9 1.0 shard_map.60
  103.9 2.1 %collective-permute-start.9 = (bf16[32,1280]{1,0:T(8,128)(2,1)S(1)}, bf16[32,1280]{1,0:T(8,128)(2,1)S(1)}, u32[]{:S(2)}, u32[]{:S(2)}) collective-permute-start(bf16[32,1280]{1,0:T(8,128)(2,1)S(1)} %get-tuple-element.47), channel_id=1, source_target_pairs={{0,1},{1,0},{2,3},{3,2},{4,5},{5,4},{6,7},{7,6},{8,9},{9,8},{10,11... | collective-permute-start | bytes 245768 | tf_op jit(solution)/shard_map/ppermute | solution.py:292
  106.0 0.0 collective-permute-done.8.rows_ref
  106.0 0.0 copy-done.1
  106.0 1.1 shard_map.61
  107.1 4.7 %collective-permute-start.11 = (bf16[32,1280]{1,0:T(8,128)(2,1)S(1)}, bf16[32,1280]{1,0:T(8,128)(2,1)S(1)}, u32[]{:S(2)}, u32[]{:S(2)}) collective-permute-start(bf16[32,1280]{1,0:T(8,128)(2,1)S(1)} %get-tuple-element.50), channel_id=1, source_target_pairs={{0,33},{1,32},{16,49},{17,48},{32,1},{33,0},{48,17},{49,16},{64,97... | collective-permute-start | bytes 245768 | tf_op jit(solution)/shard_map/ppermute | solution.py:298
  111.8 0.0 collective-permute-done.9.got_ref
  111.8 1.9 %collective-permute-start.10 = (bf16[32,1280]{1,0:T(8,128)(2,1)S(1)}, bf16[32,1280]{1,0:T(8,128)(2,1)S(1)}, u32[]{:S(2)}, u32[]{:S(2)}) collective-permute-start(bf16[32,1280]{1,0:T(8,128)(2,1)S(1)} %get-tuple-element.49), channel_id=1, source_target_pairs={{0,32},{16,48},{32,0},{48,16},{64,96},{80,112},{96,64},{112,80},{1... | collective-permute-start | bytes 245768 | tf_op jit(solution)/shard_map/ppermute | solution.py:210
  113.7 0.0 collective-permute-done.11.far_other_ref
  113.7 3.2 %collective-permute-done.10.far_ref = bf16[32,1280]{1,0:T(8,128)(2,1)S(1)} collective-permute-done((bf16[32,1280]{1,0:T(8,128)(2,1)S(1)}, bf16[32,1280]{1,0:T(8,128)(2,1)S(1)}, u32[]{:S(2)}, u32[]{:S(2)}) %collective-permute-start.10) | collective-permute-done | bytes 81952 | tf_op jit(solution)/shard_map/ppermute | solution.py:210
  117.0 0.7 shard_map.62
  (9 shorter events, 0.2 us)
Async XLA Ops:
  6.5 2.0 %copy-start.3 = (bf16[512,256]{1,0:T(8,128)(2,1)S(1)}, bf16[512,256]{1,0:T(8,128)(2,1)}, u32[]{:S(2)}) copy-start(bf16[512,256]{1,0:T(8,128)(2,1)} %param.6) | copy-start | bytes 786436
  6.5 2.0 %copy-start.5 = (bf16[512,256]{1,0:T(8,128)(2,1)S(1)}, bf16[512,256]{1,0:T(8,128)(2,1)}, u32[]{:S(2)}) copy-start(bf16[512,256]{1,0:T(8,128)(2,1)} %param.5) | copy-start | bytes 786436
  6.5 2.0 %copy-start.4 = (bf16[512,256]{1,0:T(8,128)(2,1)S(1)}, bf16[512,256]{1,0:T(8,128)(2,1)}, u32[]{:S(2)}) copy-start(bf16[512,256]{1,0:T(8,128)(2,1)} %param.7) | copy-start | bytes 786436
  6.5 93.9 %all-gather.2.cloned.1.call-start = ((), (), s32[]{:S(2)}) async-start(), calls=%async_computation.1 | async-start | bytes 5570560 | tf_op jit(solution)/shard_map/all_gather | solution.py:216
  8.7 10.1 %collective-permute-start = (bf16[3,512,128]{2,1,0:T(8,128)(2,1)S(1)}, bf16[3,512,128]{2,1,0:T(8,128)(2,1)S(1)}, u32[]{:S(2)}, u32[]{:S(2)}) collective-permute-start(bf16[3,512,128]{2,1,0:T(8,128)(2,1)S(1)} %pad_maximum_fusion.1), channel_id=1, source_target_pairs={{0,16},{16,0},{32,48},{48,32},{64,80},{80,64},{96,112},{112,96},{1... | collective-permute-start | bytes 1179656 | tf_op jit(solution)/shard_map/ppermute | solution.py:210
  18.9 12.5 %collective-permute-start.3 = (bf16[4,512,128]{2,1,0:T(8,128)(2,1)S(1)}, bf16[4,512,128]{2,1,0:T(8,128)(2,1)S(1)}, u32[]{:S(2)}, u32[]{:S(2)}) collective-permute-start(bf16[4,512,128]{2,1,0:T(8,128)(2,1)S(1)} %pad_maximum_fusion.refs_3_), channel_id=1, source_target_pairs={{0,128},{16,144},{32,160},{48,176},{64,192},{80,208},{96,224},{112... | collective-permute-start | bytes 1572872 | tf_op jit(solution)/shard_map/ppermute | solution.py:210
  20.2 15.1 %collective-permute-start.4 = (bf16[4,512,128]{2,1,0:T(8,128)(2,1)S(1)}, bf16[4,512,128]{2,1,0:T(8,128)(2,1)S(1)}, u32[]{:S(2)}, u32[]{:S(2)}) collective-permute-start(bf16[4,512,128]{2,1,0:T(8,128)(2,1)S(1)} %pad_maximum_fusion.refs_3_), channel_id=1, source_target_pairs={{128,0},{144,16},{160,32},{176,48},{192,64},{208,80},{224,96},{240... | collective-permute-start | bytes 1572872 | tf_op jit(solution)/shard_map/ppermute | solution.py:210
  21.5 16.6 %collective-permute-start.1 = (bf16[4,512,128]{2,1,0:T(8,128)(2,1)S(1)}, bf16[4,512,128]{2,1,0:T(8,128)(2,1)S(1)}, u32[]{:S(2)}, u32[]{:S(2)}) collective-permute-start(bf16[4,512,128]{2,1,0:T(8,128)(2,1)S(1)} %pad_maximum_fusion.refs_3_), channel_id=1, source_target_pairs={{0,64},{16,80},{32,96},{48,112},{64,0},{80,16},{96,32},{112,48},{1... | collective-permute-start | bytes 1572872 | tf_op jit(solution)/shard_map/ppermute | solution.py:210
  23.6 18.4 %copy-start.2 = (s32[6,4,4]{0,2,1:T(4,128)S(1)}, s32[6,4,4]{0,2,1:T(4,128)}, u32[]{:S(2)}) copy-start(s32[6,4,4]{0,2,1:T(4,128)} %param.8) | copy-start | bytes 1156
  23.6 24.9 %collective-permute-start.6 = (bf16[4,512,128]{2,1,0:T(8,128)(2,1)S(1)}, bf16[4,512,128]{2,1,0:T(8,128)(2,1)S(1)}, u32[]{:S(2)}, u32[]{:S(2)}) collective-permute-start(bf16[4,512,128]{2,1,0:T(8,128)(2,1)S(1)} %pad_maximum_fusion.refs_3_), channel_id=1, source_target_pairs={{0,32},{16,48},{32,0},{48,16},{64,96},{80,112},{96,64},{112,80},{1... | collective-permute-start | bytes 1572872 | tf_op jit(solution)/shard_map/ppermute | solution.py:210
  25.6 22.8 %collective-permute-start.7 = (bf16[4,512,128]{2,1,0:T(8,128)(2,1)S(1)}, bf16[4,512,128]{2,1,0:T(8,128)(2,1)S(1)}, u32[]{:S(2)}, u32[]{:S(2)}) collective-permute-start(bf16[4,512,128]{2,1,0:T(8,128)(2,1)S(1)} %pad_maximum_fusion.refs_3_), channel_id=1, source_target_pairs={{0,256},{16,272},{32,288},{48,304},{64,320},{80,336},{96,352},{112... | collective-permute-start | bytes 1572872 | tf_op jit(solution)/shard_map/ppermute | solution.py:210
  35.4 16.4 %collective-permute-start.5 = (bf16[4,512,128]{2,1,0:T(8,128)(2,1)S(1)}, bf16[4,512,128]{2,1,0:T(8,128)(2,1)S(1)}, u32[]{:S(2)}, u32[]{:S(2)}) collective-permute-start(bf16[4,512,128]{2,1,0:T(8,128)(2,1)S(1)} %select_select_fusion), channel_id=1, source_target_pairs={{0,96},{16,112},{32,64},{48,80},{64,32},{80,48},{96,0},{112,16},{1... | collective-permute-start | bytes 1572872 | tf_op jit(solution)/shard_map/ppermute | solution.py:210
  38.2 16.2 %collective-permute-start.2 = (bf16[4,512,128]{2,1,0:T(8,128)(2,1)S(1)}, bf16[4,512,128]{2,1,0:T(8,128)(2,1)S(1)}, u32[]{:S(2)}, u32[]{:S(2)}) collective-permute-start(bf16[4,512,128]{2,1,0:T(8,128)(2,1)S(1)} %collective-permute-done.1.refs_3_), channel_id=1, source_target_pairs={{0,128},{16,144},{32,160},{48,176},{128,256},{144,272},{160,288},{... | collective-permute-start | bytes 1572872 | tf_op jit(solution)/shard_map/ppermute | solution.py:210
  96.9 9.1 %collective-permute-start.8 = (bf16[16,64,128]{2,1,0:T(8,128)(2,1)S(1)}, bf16[16,64,128]{2,1,0:T(8,128)(2,1)S(1)}, u32[]{:S(2)}, u32[]{:S(2)}) collective-permute-start(bf16[16,64,128]{2,1,0:T(8,128)(2,1)S(1)} %all_to_all.5.rows_ref), channel_id=1, source_target_pairs={{0,32},{16,48},{32,0},{48,16},{64,96},{80,112},{96,64},{112,80},{1... | collective-permute-start | bytes 786440 | tf_op jit(solution)/shard_map/ppermute | solution.py:210
  100.4 2.5 %copy-start = (bf16[2048,1280]{1,0:T(8,128)(2,1)S(1)}, bf16[2048,1280]{1,0:T(8,128)(2,1)}, u32[]{:S(2)}) copy-start(bf16[2048,1280]{1,0:T(8,128)(2,1)} %all-gather.2.cloned.1.call-done.w_ref) | copy-start | bytes 15728644
  102.9 3.1 %copy-start.1 = (bf16[2048,1280]{1,0:T(8,128)(2,1)S(1)}, bf16[2048,1280]{1,0:T(8,128)(2,1)}, u32[]{:S(2)}) copy-start(bf16[2048,1280]{1,0:T(8,128)(2,1)} %all-gather.2.cloned.1.call-done.w_ref) | copy-start | bytes 15728644
  103.9 7.8 %collective-permute-start.9 = (bf16[32,1280]{1,0:T(8,128)(2,1)S(1)}, bf16[32,1280]{1,0:T(8,128)(2,1)S(1)}, u32[]{:S(2)}, u32[]{:S(2)}) collective-permute-start(bf16[32,1280]{1,0:T(8,128)(2,1)S(1)} %get-tuple-element.47), channel_id=1, source_target_pairs={{0,1},{1,0},{2,3},{3,2},{4,5},{5,4},{6,7},{7,6},{8,9},{9,8},{10,11... | collective-permute-start | bytes 245768 | tf_op jit(solution)/shard_map/ppermute | solution.py:292
  107.1 6.6 %collective-permute-start.11 = (bf16[32,1280]{1,0:T(8,128)(2,1)S(1)}, bf16[32,1280]{1,0:T(8,128)(2,1)S(1)}, u32[]{:S(2)}, u32[]{:S(2)}) collective-permute-start(bf16[32,1280]{1,0:T(8,128)(2,1)S(1)} %get-tuple-element.50), channel_id=1, source_target_pairs={{0,33},{1,32},{16,49},{17,48},{32,1},{33,0},{48,17},{49,16},{64,97... | collective-permute-start | bytes 245768 | tf_op jit(solution)/shard_map/ppermute | solution.py:298
  111.8 5.2 %collective-permute-start.10 = (bf16[32,1280]{1,0:T(8,128)(2,1)S(1)}, bf16[32,1280]{1,0:T(8,128)(2,1)S(1)}, u32[]{:S(2)}, u32[]{:S(2)}) collective-permute-start(bf16[32,1280]{1,0:T(8,128)(2,1)S(1)} %get-tuple-element.49), channel_id=1, source_target_pairs={{0,32},{16,48},{32,0},{48,16},{64,96},{80,112},{96,64},{112,80},{1... | collective-permute-start | bytes 245768 | tf_op jit(solution)/shard_map/ppermute | solution.py:210
Sparse Core Ops, SparseCore 0:
  9.5 90.8 all-gather.1
